TPU v7x, 256 devices: a whole 4x4x8 slice. The times are simulated.
256 devices in a mesh: section: 2 (over x_hi), dp: 128 (over y, z, x_lo, core).
Axes of the slice: x: 4 (x_hi: 2, x_lo: 2; x = x_hi * 2 + x_lo), y: 4, z: 8, core: 2. Of those that a mesh axis runs over, the one named last changes fastest.
Arguments:
- inputs: bfloat16 [2, 2, 16384, 1280], P('section', None, 'dp'), may hold values from -24 to 24
- weights: bfloat16 [2, 1280, 1280], P('section'), may hold values from -0.15625 to 0.15625
- gains: float32 [2, 1280], P('section'), may hold values from 0.1 to 1.9
- timesteps: int32 [2, 16], replicated, may hold values from 0 to 999
- text_pooled: bfloat16 [2, 16, 1280], replicated, may hold values from -6 to 6
Outputs:
- section_outputs: bfloat16 [2, 2, 16384, 1280], P('section', None, 'dp')
- weight_grad: float32 [2, 1280, 1280], P('section', 'dp')
All inputs are finite; a program needn't handle non-finite values.
Results may differ from a plain program's by a relative error of at most 0.0047.
Values may be sent and summed in bfloat16 or wider, within the bound.
No kernel may reach another device: no remote copies, remote signals or barrier semaphores. Data moves between devices by JAX's collectives and lax.ppermute only.
A program may use at most 64 MiB of HBM per device.

v0:
```python
import math

import jax
import jax.numpy as jnp
from jax import lax
from jax.sharding import PartitionSpec as P

PIX = 1024
MICRO = 2
TOK_DEV = 128


def from_behind(block, axis, distance):
    devices = range(lax.axis_size(axis))
    route = [(i - distance, i) for i in devices if i - distance in devices]
    return lax.ppermute(block, axis, route)


def latent_condition(steps_row, pooled_row):
    width = pooled_row.shape[-1]
    half_width = width // 2
    frequency = jnp.exp(-math.log(10000.0) * jnp.arange(half_width, dtype=jnp.float32) / half_width)
    angles = steps_row.astype(jnp.float32)[:, None] * frequency[None, :]
    return jnp.concatenate([jnp.cos(angles), jnp.sin(angles)], axis=1) + pooled_row.astype(
        jnp.float32
    )


def forward_layer(hidden, condition, weight, gain):
    shifted = hidden.astype(jnp.float32) + condition
    inverse = lax.rsqrt(jnp.mean(shifted * shifted, axis=-1, keepdims=True) + 1e-05)
    normed = shifted * inverse * gain
    active = jax.nn.silu(normed).astype(jnp.bfloat16)
    result = hidden.astype(jnp.float32) + jnp.dot(
        active, weight, preferred_element_type=jnp.float32
    )
    return (result, (shifted, inverse, normed, active))


def backward_layer(upstream, saved, weight, gain):
    shifted, inverse, normed, active = saved
    through = lax.dot_general(
        upstream, weight, (((1,), (1,)), ((), ())), preferred_element_type=jnp.float32
    )
    sigma = jax.nn.sigmoid(normed)
    scaled = through * sigma * (1.0 + normed * (1.0 - sigma)) * gain
    inner = jnp.mean(scaled * shifted, axis=-1, keepdims=True)
    return (
        upstream.astype(jnp.float32) + inverse * scaled - shifted * inverse**3 * inner
    ).astype(jnp.bfloat16)


def weight_term(active_rows, upstream_rows):
    return lax.dot_general(
        active_rows, upstream_rows, (((0,), (0,)), ((), ())), preferred_element_type=jnp.float32
    )


def local(inputs, weights, gains, timesteps, text_pooled):
    local_rows = inputs[0]
    weight = weights[0]
    gain = gains[0]
    width = weight.shape[0]
    down_section = lax.axis_index("section") == 0
    lane_count = lax.axis_size("dp")
    latent_count = text_pooled.shape[1]
    loss_scale = math.sqrt(MICRO * TOK_DEV * lane_count)
    pixel_ids = lax.axis_index("dp") * TOK_DEV + jnp.arange(TOK_DEV, dtype=jnp.int32)
    selector = (
        pixel_ids[:, None] // PIX == jnp.arange(latent_count, dtype=jnp.int32)[None, :]
    ).astype(jnp.float32)
    conditions = [
        jnp.dot(
            selector,
            latent_condition(timesteps[number], text_pooled[number]),
            precision=lax.Precision.HIGHEST,
            preferred_element_type=jnp.float32,
        )
        for number in range(MICRO)
    ]
    first_pass = [
        forward_layer(local_rows[number], conditions[number], weight, gain)
        for number in range(MICRO)
    ]
    sent_rows = jnp.stack([pair[0].astype(jnp.bfloat16) for pair in first_pass])
    received = from_behind(sent_rows, "section", 1)
    second_pass = [
        forward_layer(received[number], conditions[number], weight, gain) for number in range(MICRO)
    ]
    upper_rows = jnp.stack([pair[0].astype(jnp.bfloat16) for pair in second_pass])
    results = jnp.where(down_section, sent_rows, upper_rows)
    target_cots = [
        ((second_pass[number][0] - local_rows[number].astype(jnp.float32)) / loss_scale).astype(
            jnp.bfloat16
        )
        for number in range(MICRO)
    ]
    back_rows = jnp.stack(
        [
            backward_layer(target_cots[number], second_pass[number][1], weight, gain)
            for number in range(MICRO)
        ]
    )
    returned = from_behind(back_rows, "section", -1)
    active_rows = jnp.where(
        down_section,
        jnp.concatenate([pair[1][3] for pair in first_pass]),
        jnp.concatenate([pair[1][3] for pair in second_pass]),
    )
    upstream_rows = jnp.where(
        down_section, returned.reshape(-1, width), jnp.concatenate(target_cots)
    )
    gradient = lax.psum_scatter(
        weight_term(active_rows, upstream_rows), "dp", scatter_dimension=0, tiled=True
    )
    return (results[None], gradient[None])


def solution(mesh):
    return jax.shard_map(
        local,
        mesh=mesh,
        in_specs=(
            P("section", None, "dp", None),
            P("section", None, None),
            P("section", None),
            P(),
            P(),
        ),
        out_specs=(P("section", None, "dp", None), P("section", "dp", None)),
        check_vma=False,
    )
```

profile of v0, /device:TPU:6, one launch (start us, length us, event | category | flops | bytes accessed | tf_op | source)
XLA Modules:
  0.0 1159.1 jit_solution(4284364219565632758)
XLA Ops:
  7.2 0.0 copy-start
  7.2 0.0 all-reduce.3.cloned.1.call-start
  7.2 0.9 convert_bitcast_fusion.3
  8.1 0.8 reduce
  8.9 0.4 multiply_cosine_fusion.1
  9.3 1.2 fusion.66
  10.5 1.8 multiply_reduce_fusion.5
  12.3 1.6 multiply_convert_fusion.3
  13.9 0.6 fusion.42
  14.5 0.6 fusion.45
  15.2 0.1 pad_maximum_fusion
  15.3 1.3 collective-permute-start
  16.6 18.6 %collective-permute-done = bf16[2,128,1280]{2,1,0:T(8,128)(2,1)S(1)} collective-permute-done((bf16[2,128,1280]{2,1,0:T(8,128)(2,1)S(1)}, bf16[2,128,1280]{2,1,0:T(8,128)(2,1)S(1)}, u32[]{:S(2)}, u32[]{:S(2)}) %collective-permute-start) | collective-permute-done | bytes 655392 | tf_op jit(solution)/shard_map/ppermute | solution.py:16
  35.1 0.3 multiply_reduce_fusion.3
  35.4 0.5 multiply_convert_fusion.1
  35.9 0.6 fusion.21
  36.6 0.1 copy-done.7
  36.6 1.5 fusion.49
  38.1 1.2 fusion.33
  39.4 1.4 multiply_reduce_fusion.1
  40.8 0.4 fusion.61
  41.3 0.9 pad_maximum_fusion.1
  42.2 2.3 collective-permute-start.1
  44.5 12.7 %collective-permute-done.1 = bf16[2,128,1280]{2,1,0:T(8,128)(2,1)} collective-permute-done((bf16[2,128,1280]{2,1,0:T(8,128)(2,1)}, bf16[2,128,1280]{2,1,0:T(8,128)(2,1)}, u32[]{:S(2)}, u32[]{:S(2)}) %collective-permute-start.1) | collective-permute-done | bytes 655392 | tf_op jit(solution)/shard_map/ppermute | solution.py:16
  57.2 5.3 fusion.52
  62.5 0.0 all-reduce.3.cloned.1.call-update
  62.5 0.6 copy-done.10
  63.2 0.6 dynamic-slice
  64.4 2.2 maximum_select_fusion
  66.6 1084.0 %all-reduce.3.cloned.1.call-done = f32[1280,1280]{1,0:T(8,128)} async-done(((f32[1280,1280]{1,0:T(8,128)}), f32[1280,1280]{1,0:T(8,128)}) %all-reduce.3.cloned.1.call-update) | async-done | bytes 6553616
  1150.7 0.9 dynamic-slice_bitcast_fusion
  1151.6 0.7 copy.8
  (26 shorter events, 0.1 us)
Async XLA Ops:
  7.2 6.7 copy-start
  7.2 1143.5 %all-reduce.3.cloned.1.call-start = ((), (), s32[]{:S(2)}) async-start(), calls=%async_computation | async-start | bytes 13107200
  8.9 5.0 copy-start.1
  13.9 1.3 copy-start.5
  13.9 22.7 %copy-start.4 = (bf16[128,1280]{1,0:T(8,128)(2,1)}, bf16[128,1280]{1,0:T(8,128)(2,1)S(1)}, u32[]{:S(2)}) copy-start(bf16[128,1280]{1,0:T(8,128)(2,1)S(1)} %get-tuple-element.14) | copy-start | bytes 983044
  14.5 20.8 %copy-start.8 = (bf16[128,1280]{1,0:T(8,128)(2,1)}, bf16[128,1280]{1,0:T(8,128)(2,1)S(1)}, u32[]{:S(2)}) copy-start(bf16[128,1280]{1,0:T(8,128)(2,1)S(1)} %fusion.42) | copy-start | bytes 983044
  15.2 21.4 %copy-start.9 = (bf16[128,1280]{1,0:T(8,128)(2,1)}, bf16[128,1280]{1,0:T(8,128)(2,1)S(1)}, u32[]{:S(2)}) copy-start(bf16[128,1280]{1,0:T(8,128)(2,1)S(1)} %fusion.45) | copy-start | bytes 983044
  15.3 19.9 %collective-permute-start = (bf16[2,128,1280]{2,1,0:T(8,128)(2,1)S(1)}, bf16[2,128,1280]{2,1,0:T(8,128)(2,1)S(1)}, u32[]{:S(2)}, u32[]{:S(2)}) collective-permute-start(bf16[2,128,1280]{2,1,0:T(8,128)(2,1)S(1)} %pad_maximum_fusion), channel_id=1, source_target_pairs={{0,128},{1,129},{2,130},{3,131},{4,132},{5,133},{6,134},{7,135},{8... | collective-permute-start | bytes 1966088 | tf_op jit(solution)/shard_map/ppermute | solution.py:16
  35.9 0.7 copy-start.7
  35.9 2.2 copy-start.6
  38.1 3.1 copy-start.2
  38.1 3.1 copy-start.3
  42.2 15.0 %collective-permute-start.1 = (bf16[2,128,1280]{2,1,0:T(8,128)(2,1)}, bf16[2,128,1280]{2,1,0:T(8,128)(2,1)}, u32[]{:S(2)}, u32[]{:S(2)}) collective-permute-start(bf16[2,128,1280]{2,1,0:T(8,128)(2,1)} %pad_maximum_fusion.1), channel_id=1, source_target_pairs={{128,0},{129,1},{130,2},{131,3},{132,4},{133,5},{134,6},{135,7},{1... | collective-permute-start | bytes 1966088 | tf_op jit(solution)/shard_map/ppermute | solution.py:16
  62.5 0.7 copy-start.10
Sparse Core Ops, SparseCore 0:
  62.6 1087.9 all-reduce.2
where the time goes:
time: 1160 us
  waiting for transfers between devices  1120 us (97%)
  between operations  14.9 us (1%)
  matrix products  14.4 us (1%)
    unnamed x2, waiting for transfers between devices  1080 us
    ppermute x2, waiting for transfers between devices, from_behind(): return lax.ppermute(block, axis, route)  31.2 us
  transfers between devices with their start and end apart: 3, of which 3 were waited for; matrix products, arithmetic and copies ran while one was open for 0% of the time, Pallas kernels for 0%

commit v1 on v0

v1 whole, which is shorter than its diff:
```python
import math

import jax
import jax.numpy as jnp
from jax import lax
from jax.sharding import Mesh, PartitionSpec as P

PIX = 1024
MICRO = 2
TOK_DEV = 128
DP = ("y", "z", "x", "core")
GROUP = ("x", "core")
LANES = 128


def latent_condition(step, pooled_row):
    width = pooled_row.shape[-1]
    half_width = width // 2
    frequency = jnp.exp(-math.log(10000.0) * jnp.arange(half_width, dtype=jnp.float32) / half_width)
    angles = step.astype(jnp.float32) * frequency
    return jnp.concatenate([jnp.cos(angles), jnp.sin(angles)]) + pooled_row.astype(jnp.float32)


def forward_layer(hidden, condition, weight, gain):
    shifted = hidden.astype(jnp.float32) + condition
    inverse = lax.rsqrt(jnp.mean(shifted * shifted, axis=-1, keepdims=True) + 1e-05)
    normed = shifted * inverse * gain
    active = jax.nn.silu(normed).astype(jnp.bfloat16)
    result = hidden.astype(jnp.float32) + jnp.dot(
        active, weight, preferred_element_type=jnp.float32
    )
    return (result, (shifted, inverse, normed, active))


def backward_layer(upstream, saved, weight, gain):
    shifted, inverse, normed, active = saved
    through = lax.dot_general(
        upstream, weight, (((1,), (1,)), ((), ())), preferred_element_type=jnp.float32
    )
    sigma = jax.nn.sigmoid(normed)
    scaled = through * sigma * (1.0 + normed * (1.0 - sigma)) * gain
    inner = jnp.mean(scaled * shifted, axis=-1, keepdims=True)
    return (
        upstream.astype(jnp.float32) + inverse * scaled - shifted * inverse**3 * inner
    ).astype(jnp.bfloat16)


def swap(block, axis):
    return lax.ppermute(block, axis, [(0, 1), (1, 0)])


def local(inputs, weights, gains, timesteps, text_pooled):
    local_rows = inputs[0]
    weight = weights[0]
    gain = gains[0]
    width = weight.shape[0]
    quarter = width // 4
    down_section = lax.axis_index("section") == 0
    loss_scale = math.sqrt(MICRO * TOK_DEV * LANES)
    latent = lax.axis_index(DP) * TOK_DEV // PIX
    conditions = [
        latent_condition(timesteps[number, latent], text_pooled[number, latent])
        for number in range(MICRO)
    ]
    first_out, first_active, received = [], [], []
    for number in range(MICRO):
        out, saved = forward_layer(local_rows[number], conditions[number], weight, gain)
        first_out.append(out.astype(jnp.bfloat16))
        first_active.append(saved[3])
        received.append(lax.ppermute(first_out[-1], "section", [(0, 1)]))
    second_out, second_active, cots, backs = [], [], [], []
    for number in range(MICRO):
        out, saved = forward_layer(received[number], conditions[number], weight, gain)
        second_out.append(out.astype(jnp.bfloat16))
        second_active.append(saved[3])
        cot = ((out - local_rows[number].astype(jnp.float32)) / loss_scale).astype(jnp.bfloat16)
        cots.append(cot)
        backs.append(backward_layer(cot, saved, weight, gain))
    results = jnp.where(down_section, jnp.stack(first_out), jnp.stack(second_out))
    active = jnp.where(down_section, jnp.concatenate(first_active), jnp.concatenate(second_active))
    far = swap(active, "x")
    near = swap(active, "core")
    far_core = swap(far, "core")

    upstream = jnp.stack([jnp.concatenate(backs), jnp.concatenate(cots)])
    pieces = jnp.transpose(upstream.reshape(2, -1, 4, quarter), (0, 2, 1, 3))
    pieces = pieces.reshape(8, -1, quarter)
    arrived = lax.all_to_all(pieces, ("section",) + GROUP, 0, 0, tiled=True)[4:]
    x_at, core_at = lax.axis_index("x"), lax.axis_index("core")
    partial = jnp.zeros((width, quarter), jnp.float32)
    for block, x_off, core_off in ((active, 0, 0), (near, 0, 1), (far, 1, 0), (far_core, 1, 1)):
        source = ((x_at + x_off) % 2) * 2 + (core_at + core_off) % 2
        rows = lax.dynamic_index_in_dim(arrived, source, 0, keepdims=False)
        partial += lax.dot_general(
            block, rows, (((0,), (0,)), ((), ())), preferred_element_type=jnp.float32
        )
    shares = partial.astype(jnp.bfloat16).reshape(LANES, width // LANES, quarter)
    shares = lax.all_to_all(shares, DP, 0, 0, tiled=True)
    shares = shares.reshape(LANES // 4, 4, width // LANES, quarter).astype(jnp.float32)
    summed = jnp.sum(shares, axis=0)
    gradient = jnp.transpose(summed, (1, 0, 2)).reshape(width // LANES, width)
    return (results[None], gradient[None])


def solution(mesh):
    fine = Mesh(mesh.devices.reshape(2, 4, 8, 2, 2), ("section",) + DP)
    return jax.shard_map(
        local,
        mesh=fine,
        in_specs=(
            P("section", None, DP, None),
            P("section", None, None),
            P("section", None),
            P(),
            P(),
        ),
        out_specs=(P("section", None, DP, None), P("section", DP, None)),
        check_vma=False,
    )
```

time: 1160 us -> 147 us (0.13)
  waiting for transfers between devices: 1120 us -> 80.9 us
  starting transfers between devices: 3.64 us -> 22.6 us
  between operations: 14.9 us -> 2.22 us
    unnamed x2 -> x0, waiting for transfers between devices: 1080 us -> none
    all_to_all x0 -> x2, waiting for transfers between devices: none -> 37.5 us  [the longest x1 37.5 us: local(): shares = lax.all_to_all(shares, DP, 0, 0, tiled=True)]
    all_to_all x0 -> x2, starting transfers between devices: none -> 19.2 us  [the longest x1 14.4 us: local(): shares = lax.all_to_all(shares, DP, 0, 0, tiled=True)]
    ppermute x2 -> x5, waiting for transfers between devices: 31.2 us -> 43.4 us  [the longest x3 27.1 us: swap(): return lax.ppermute(block, axis, [(0, 1), (1, 0)])]
  transfers between devices with their start and end apart: 3 -> 7, of which waited for: 3 -> 4; matrix products, arithmetic and copies ran while one was open for 0% -> 8% of each run, Pallas kernels for 0% -> 0%
where the time goes in v1:
time: 147 us; the launch traced here: 146 us
  waiting for transfers between devices  80.9 us (55%)
  starting transfers between devices  22.6 us (15%)
  matrix products  14.9 us (10%)
  other arithmetic  13.7 us (9%)
  local copies, waits for them, and re-layouts  11.2 us (8%)
  between operations  2.22 us (2%)
    all_to_all x1, waiting for transfers between devices, local(): shares = lax.all_to_all(shares, DP, 0, 0, tiled=True)  37.5 us
    ppermute x3, waiting for transfers between devices, swap(): return lax.ppermute(block, axis, [(0, 1), (1, 0)])  27.1 us
    ppermute x2, waiting for transfers between devices, local(): received.append(lax.ppermute(first_out[-1], 'section', [(0, 1)]))  16.3 us
    all_to_all x1, starting transfers between devices, local(): shares = lax.all_to_all(shares, DP, 0, 0, tiled=True)  14.4 us
    dot_general x4, matrix products, local(): lax.dot_general(block, rows, (((0,), (0,)), ((), ())), preferred_element_...  6.8 us
    dot_general x4, matrix products, forward_layer(): jnp.dot(active, weight, preferred_element_type=jnp.float32)  5.44 us
    all_to_all x1, starting transfers between devices, local(): arrived = lax.all_to_all(pieces, ('section',) + GROUP, 0, 0, tiled=True)[4:]  4.78 us
    reshape x1, local copies, waits for them, and re-layouts, local(): partial.astype(jnp.bfloat16).reshape(LANES, width // LANES, quarter)  3.1 us
  transfers between devices with their start and end apart: 7, of which 4 were waited for; matrix products, arithmetic and copies ran while one was open for 8% of the time, Pallas kernels for 0%

profile of v1, /device:TPU:6, one launch (start us, length us, event | category | flops | bytes accessed | tf_op | source)
XLA Modules:
  0.0 145.7 jit_solution(2110138833818750783)
XLA Ops:
  0.7 1.4 constant_dynamic-slice_fusion.1
  3.6 0.8 convert_reduce_fusion.2
  4.4 1.3 fusion.74
  6.5 1.9 %fusion.43 = bf16[128,1280]{1,0:T(8,128)(2,1)S(1)} fusion(bf16[1,1280,1280]{2,1,0:T(8,128)(2,1)S(1)} %copy-done, f32[128]{0:T(128)S(1)} %add_rsqrt_fusion.2, f32[1280]{0:T(1024)S(1)} %get-tuple-element.34, f32[1280]{0:T(1024)S(1)} %reduce.1, bf16[1,2,128,1280]{3,2,1,0:T(8,128)(2,1)} %param.5), kind=kOutput, calls=%fused_computation.27 | convolution fusion | flops 421396480 | bytes 4270592 | tf_op jit(solution)/shard_map/dot_general | solution.py:29
  8.4 1.3 collective-permute-start.1
  10.5 1.3 collective-permute-start
  11.8 10.6 %collective-permute-done.1 = bf16[128,1280]{1,0:T(8,128)(2,1)S(1)} collective-permute-done((bf16[128,1280]{1,0:T(8,128)(2,1)S(1)}, bf16[128,1280]{1,0:T(8,128)(2,1)S(1)}, u32[]{:S(2)}, u32[]{:S(2)}) %collective-permute-start.1) | collective-permute-done | bytes 327712 | tf_op jit(solution)/shard_map/ppermute | solution.py:70
  22.6 5.7 %collective-permute-done = bf16[128,1280]{1,0:T(8,128)(2,1)S(1)} collective-permute-done((bf16[128,1280]{1,0:T(8,128)(2,1)S(1)}, bf16[128,1280]{1,0:T(8,128)(2,1)S(1)}, u32[]{:S(2)}, u32[]{:S(2)}) %collective-permute-start) | collective-permute-done | bytes 327712 | tf_op jit(solution)/shard_map/ppermute | solution.py:70
  28.4 0.7 fusion.22
  29.2 2.1 %fusion.111 = (bf16[128,1280]{1,0:T(8,128)(2,1)S(1)}, bf16[128,1280]{1,0:T(8,128)(2,1)S(1)}, bf16[1,1,128,1280]{3,2,1,0:T(8,128)(2,1)}, bf16[128,1280]{1,0:T(8,1...) fusion(bf16[1,2,128,1280]{3,2,1,0:T(8,128)(2,1)S(1)} %copy-done.1, f32[128,1280]{1,0:T(8,128)S(1)} %fusion.22, ...), kind=kOutput, calls=%fused_computation.104 | convolution fusion | flops 425492480 | bytes 7251456 | tf_op jit(solution)/shard_map/dot_general | solution.py:29
  31.3 1.4 fusion.109
  32.7 1.3 fusion.95
  34.1 1.2 fusion.108
  35.3 1.2 fusion.94
  36.8 1.4 fusion.49
  38.2 2.5 %copy.10 = bf16[8,256,320]{1,2,0:T(8,128)(2,1)} copy(bf16[8,256,320]{2,1,0:T(8,128)(2,1)} %bitcast.151) | data formatting | bytes 2621440 | tf_op jit(solution)/shard_map/reshape | solution.py:87
  40.7 4.8 %all-to-all-start = ((bf16[8,256,320]{1,2,0:T(8,128)(2,1)}), bf16[8,256,320]{1,2,0:T(8,128)(2,1)}, u32[]{:S(2)}, u32[]{:S(2)}) async-start(bf16[8,256,320]{1,2,0:T(8,128)(2,1)} %copy.10), calls=%async_computation | async-start | bytes 2621440 | tf_op jit(solution)/shard_map/all_to_all | solution.py:88
  45.5 2.3 %maximum_select_fusion.1 = bf16[256,1280]{1,0:T(8,128)(2,1)} fusion(bf16[128,1280]{1,0:T(8,128)(2,1)} %get-tuple-element.16, bf16[128,1280]{1,0:T(8,128)(2,1)} %get-tuple-element.17, bf16[128,1280]{1,0:T(8,128)(2,1)} %get-tuple-element.22, bf16[128,1280]{1,0:T(8,128)(2,1)} %get-tuple-element.20, pred[]{:T(512)S(6)} %eq.12), kind=kLoop, calls=%fused_computation.126 | loop fusion | flops 2949120 | bytes 1966081 | tf_op jit(solution)/shard_map/jit(_where)/select_n | solution.py:80
  47.8 0.9 collective-permute-start.3
  48.6 27.1 %collective-permute-done.3 = bf16[256,1280]{1,0:T(8,128)(2,1)} collective-permute-done((bf16[256,1280]{1,0:T(8,128)(2,1)}, bf16[256,1280]{1,0:T(8,128)(2,1)}, u32[]{:S(2)}, u32[]{:S(2)}) %collective-permute-start.3) | collective-permute-done | bytes 655392 | tf_op jit(solution)/shard_map/ppermute | solution.py:49
  75.8 1.1 slice.38
  76.9 1.5 %fusion.150 = f32[1280,320]{0,1:T(8,128)S(1)} fusion(bf16[256,1280]{1,0:T(8,128)(2,1)} %maximum_select_fusion.1, bf16[4,256,320]{1,2,0:T(8,128)(2,1)S(1)} %slice.38, s32[]{:T(128)S(6)} %select_n.81), kind=kOutput, calls=%fused_computation.147 | convolution fusion | flops 209715200 | bytes 2457604 | tf_op jit(solution)/shard_map/dot_general | solution.py:94
  78.4 1.5 %convolution_add_fusion.2 = f32[1280,320]{0,1:T(8,128)S(1)} fusion(f32[1280,320]{0,1:T(8,128)S(1)} %fusion.150, bf16[256,1280]{1,0:T(8,128)(2,1)} %collective-permute-done.2, bf16[4,256,320]{1,2,0:T(8,128)(2,1)S(1)} %slice.38, s32[]{:T(128)S(6)} %select_n.83), kind=kOutput, calls=%fused_computation.15 | convolution fusion | flops 210124800 | bytes 4096004 | tf_op jit(solution)/shard_map/dot_general | solution.py:94
  79.9 1.5 %convolution_add_fusion.1 = f32[1280,320]{0,1:T(8,128)S(1)} fusion(f32[1280,320]{0,1:T(8,128)S(1)} %convolution_add_fusion.2, bf16[256,1280]{1,0:T(8,128)(2,1)} %collective-permute-done.3, bf16[4,256,320]{1,2,0:T(8,128)(2,1)S(1)} %slice.38, s32[]{:T(128)S(6)} %select_n.85), kind=kOutput, calls=%fused_computation.14 | convolution fusion | flops 210124800 | bytes 4096004 | tf_op jit(solution)/shard_map/dot_general | solution.py:94
  81.4 2.4 %fusion.12 = bf16[1280,320]{0,1:T(8,128)(2,1)} fusion(f32[1280,320]{0,1:T(8,128)S(1)} %convolution_add_fusion.1, bf16[256,1280]{1,0:T(8,128)(2,1)} %collective-permute-done.4, bf16[4,256,320]{1,2,0:T(8,128)(2,1)S(1)} %slice.38, s32[]{:T(128)S(6)} %select_n.86), kind=kOutput, calls=%fused_computation.16 | convolution fusion | flops 210534400 | bytes 3276804 | tf_op jit(solution)/shard_map/dot_general | solution.py:94
  83.7 2.2 %copy.11 = bf16[1280,320]{1,0:T(8,128)(2,1)} copy(bf16[1280,320]{0,1:T(8,128)(2,1)} %fusion.12) | data formatting | bytes 1638400 | tf_op jit(solution)/shard_map/convert_element_type | solution.py:97
  85.9 3.1 %reshape.216 = bf16[128,10,320]{2,1,0:T(8,128)(2,1)} reshape(bf16[1280,320]{1,0:T(8,128)(2,1)} %copy.11) | data formatting | bytes 1638400 | tf_op jit(solution)/shard_map/reshape | solution.py:97
  89.0 14.4 %all-to-all-start.1 = ((bf16[128,10,320]{2,1,0:T(8,128)(2,1)}), bf16[128,10,320]{2,1,0:T(8,128)(2,1)}, u32[]{:S(2)}, u32[]{:S(2)}) async-start(bf16[128,10,320]{2,1,0:T(8,128)(2,1)} %reshape.216), calls=%async_computation.1 | async-start | bytes 3145728 | tf_op jit(solution)/shard_map/all_to_all | solution.py:98
  103.5 2.2 %maximum_select_fusion = bf16[1,2,128,1280]{3,2,1,0:T(8,128)(2,1)} fusion(bf16[1,1,128,1280]{3,2,1,0:T(8,128)(2,1)} %bitcast.153, bf16[1,1,128,1280]{3,2,1,0:T(8,128)(2,1)} %bitcast.154, bf16[1,1,128,1280]{3,2,1,0:T(8,128)(2,1)} %get-tuple-element.15, bf16[1,1,128,1280]{3,2,1,0:T(8,128)(2,1)} %get-tuple-element.18, pred[]{:T(512)S(6)} %eq.12), kind=kLoop, calls=%fused_computation.123 | loop fusion | flops 983040 | bytes 1966081 | tf_op jit(solution)/shard_map/jit(_where)/select_n | solution.py:79
  105.7 37.5 %all-to-all-done.1 = bf16[128,10,320]{2,1,0:T(8,128)(2,1)} async-done(((bf16[128,10,320]{2,1,0:T(8,128)(2,1)}), bf16[128,10,320]{2,1,0:T(8,128)(2,1)}, u32[]{:S(2)}, u32[]{:S(2)}) %all-to-all-start.1) | async-done | bytes 819232 | tf_op jit(solution)/shard_map/all_to_all | solution.py:98
  143.2 1.7 %convert_reduce_fusion = f32[4,10,320]{2,1,0:T(8,128)S(1)} fusion(bf16[32,4,10,320]{3,2,1,0:T(8,128)(2,1)} %bitcast.20), kind=kLoop, calls=%fused_computation.12 | loop fusion | flops 806400 | bytes 870400 | tf_op jit(solution)/shard_map/reduce_sum | solution.py:100
  144.9 0.8 broadcast_in_dim_reshape.4
  (32 shorter events, 2.4 us)
Async XLA Ops:
  0.6 5.9 %copy-start = (bf16[1,1280,1280]{2,1,0:T(8,128)(2,1)S(1)}, bf16[1,1280,1280]{2,1,0:T(8,128)(2,1)}, u32[]{:S(2)}) copy-start(bf16[1,1280,1280]{2,1,0:T(8,128)(2,1)} %param.6) | copy-start | bytes 9830404
  6.5 3.2 %copy-start.1 = (bf16[1,2,128,1280]{3,2,1,0:T(8,128)(2,1)S(1)}, bf16[1,2,128,1280]{3,2,1,0:T(8,128)(2,1)}, u32[]{:S(2)}) copy-start(bf16[1,2,128,1280]{3,2,1,0:T(8,128)(2,1)} %param.5) | copy-start | bytes 1966084
  8.4 2.1 %copy-start.2 = (bf16[128,1280]{1,0:T(8,128)(2,1)}, bf16[128,1280]{1,0:T(8,128)(2,1)S(1)}, u32[]{:S(2)}) copy-start(bf16[128,1280]{1,0:T(8,128)(2,1)S(1)} %fusion.43) | copy-start | bytes 983044
  8.4 14.0 %collective-permute-start.1 = (bf16[128,1280]{1,0:T(8,128)(2,1)S(1)}, bf16[128,1280]{1,0:T(8,128)(2,1)S(1)}, u32[]{:S(2)}, u32[]{:S(2)}) collective-permute-start(bf16[128,1280]{1,0:T(8,128)(2,1)S(1)} %fusion.43), channel_id=1, source_target_pairs={{0,128},{1,129},{2,130},{3,131},{4,132},{5,133},{6,134},{7,135},{8... | collective-permute-start | bytes 983048 | tf_op jit(solution)/shard_map/ppermute | solution.py:70
  10.5 18.7 %copy-start.3 = (bf16[128,1280]{1,0:T(8,128)(2,1)}, bf16[128,1280]{1,0:T(8,128)(2,1)S(1)}, u32[]{:S(2)}) copy-start(bf16[128,1280]{1,0:T(8,128)(2,1)S(1)} %fusion.46) | copy-start | bytes 983044
  10.5 17.8 %collective-permute-start = (bf16[128,1280]{1,0:T(8,128)(2,1)S(1)}, bf16[128,1280]{1,0:T(8,128)(2,1)S(1)}, u32[]{:S(2)}, u32[]{:S(2)}) collective-permute-start(bf16[128,1280]{1,0:T(8,128)(2,1)S(1)} %fusion.46), channel_id=1, source_target_pairs={{0,128},{1,129},{2,130},{3,131},{4,132},{5,133},{6,134},{7,135},{8... | collective-permute-start | bytes 983048 | tf_op jit(solution)/shard_map/ppermute | solution.py:70
  40.7 35.0 %all-to-all-start = ((bf16[8,256,320]{1,2,0:T(8,128)(2,1)}), bf16[8,256,320]{1,2,0:T(8,128)(2,1)}, u32[]{:S(2)}, u32[]{:S(2)}) async-start(bf16[8,256,320]{1,2,0:T(8,128)(2,1)} %copy.10), calls=%async_computation | async-start | bytes 2621440 | tf_op jit(solution)/shard_map/all_to_all | solution.py:88
  47.8 28.0 %collective-permute-start.3 = (bf16[256,1280]{1,0:T(8,128)(2,1)}, bf16[256,1280]{1,0:T(8,128)(2,1)}, u32[]{:S(2)}, u32[]{:S(2)}) collective-permute-start(bf16[256,1280]{1,0:T(8,128)(2,1)} %maximum_select_fusion.1), channel_id=1, source_target_pairs={{0,2},{2,0},{1,3},{3,1},{4,6},{6,4},{5,7},{7,5},{8,10},{10,8},{9,1... | collective-permute-start | bytes 1966088 | tf_op jit(solution)/shard_map/ppermute | solution.py:49
  48.6 29.8 %collective-permute-start.2 = (bf16[256,1280]{1,0:T(8,128)(2,1)}, bf16[256,1280]{1,0:T(8,128)(2,1)}, u32[]{:S(2)}, u32[]{:S(2)}) collective-permute-start(bf16[256,1280]{1,0:T(8,128)(2,1)} %maximum_select_fusion.1), channel_id=1, source_target_pairs={{0,1},{1,0},{2,3},{3,2},{4,5},{5,4},{6,7},{7,6},{8,9},{9,8},{10,11... | collective-permute-start | bytes 1966088 | tf_op jit(solution)/shard_map/ppermute | solution.py:49
  75.8 5.6 %collective-permute-start.4 = (bf16[256,1280]{1,0:T(8,128)(2,1)}, bf16[256,1280]{1,0:T(8,128)(2,1)}, u32[]{:S(2)}, u32[]{:S(2)}) collective-permute-start(bf16[256,1280]{1,0:T(8,128)(2,1)} %collective-permute-done.3), channel_id=1, source_target_pairs={{0,1},{1,0},{2,3},{3,2},{4,5},{5,4},{6,7},{7,6},{8,9},{9,8},{10,11... | collective-permute-start | bytes 1966088 | tf_op jit(solution)/shard_map/ppermute | solution.py:49
  89.0 54.1 %all-to-all-start.1 = ((bf16[128,10,320]{2,1,0:T(8,128)(2,1)}), bf16[128,10,320]{2,1,0:T(8,128)(2,1)}, u32[]{:S(2)}, u32[]{:S(2)}) async-start(bf16[128,10,320]{2,1,0:T(8,128)(2,1)} %reshape.216), calls=%async_computation.1 | async-start | bytes 3145728 | tf_op jit(solution)/shard_map/all_to_all | solution.py:98

commit v2 on v1

v2 whole, which is shorter than its diff:
```python
import functools
import math

import jax
import jax.numpy as jnp
from jax import lax
from jax.experimental import pallas as pl
from jax.experimental.pallas import tpu as pltpu
from jax.sharding import Mesh, PartitionSpec as P

PIX = 1024
MICRO = 2
ROWS = 128
LANES = 128
C = 1280
DP = ("yh", "yl", "z", "x", "core")
GROUP = ("yl", "core")
PIECE = 320
SHARE = 32
PARAMS = pltpu.CompilerParams(vmem_limit_bytes=40 * 1024 * 1024)
VMEM = pl.BlockSpec(memory_space=pltpu.VMEM)
SMEM = pl.BlockSpec(memory_space=pltpu.SMEM)


def condition_row(steps_ref, text_ref, number):
    latent = lax.axis_index(DP) * ROWS // PIX
    step = steps_ref[number, latent].astype(jnp.float32)
    lane = lax.broadcasted_iota(jnp.int32, (1, C), 1)
    index = jnp.where(lane < C // 2, lane, lane - C // 2).astype(jnp.float32)
    angle = step * jnp.exp(-math.log(10000.0) * index / (C // 2))
    waves = jnp.where(lane < C // 2, jnp.cos(angle), jnp.sin(angle))
    text = text_ref[number].astype(jnp.float32)
    mine = lax.broadcasted_iota(jnp.int32, text.shape, 0) == latent
    return waves + jnp.sum(jnp.where(mine, text, 0.0), axis=0, keepdims=True)


def normed_rows(hidden, condition, gain):
    shifted = hidden + condition
    inverse = lax.rsqrt(jnp.mean(shifted * shifted, axis=-1, keepdims=True) + 1e-05)
    normed = shifted * inverse * gain
    sigma = 1.0 / (1.0 + jnp.exp(-normed))
    return shifted, inverse, normed, sigma


def down_kernel(number, steps_ref, rows_ref, weight_ref, gain_ref, text_ref, sent_ref, active_ref):
    hidden = rows_ref[0, number].astype(jnp.float32)
    condition = condition_row(steps_ref, text_ref, number)
    _, _, normed, sigma = normed_rows(hidden, condition, gain_ref[...])
    active = (normed * sigma).astype(jnp.bfloat16)
    active_ref[...] = active
    result = hidden + jnp.dot(active, weight_ref[0], preferred_element_type=jnp.float32)
    sent_ref[...] = result.astype(jnp.bfloat16)


def store_pieces(pieces_ref, first, values):
    half = ROWS // 2
    low = lax.broadcasted_iota(jnp.int32, (half, 128), 1) < 64
    rounded = values.astype(jnp.bfloat16)
    for quarter in range(4):
        slot = first + quarter
        pieces_ref[slot, :ROWS] = rounded[:, 256 * quarter : 256 * quarter + 128]
        pieces_ref[slot, ROWS : 2 * ROWS] = rounded[:, 256 * quarter + 128 : 256 * quarter + 256]
        at = 1024 + 128 * (quarter // 2)
        block = values[:, at : at + 128]
        turned = pltpu.roll(block, 64, 1)
        top, bottom = (block, turned) if quarter % 2 == 0 else (turned, block)
        pieces_ref[slot, 2 * ROWS :] = jnp.where(low, top[:half], bottom[half:]).astype(
            jnp.bfloat16
        )


def up_kernel(
    number, steps_ref, arrived_ref, rows_ref, weight_ref, gain_ref, text_ref, sent_ref,
    first_active_ref, out_ref, active_ref, pieces_ref,
):
    down = lax.axis_index("section") == 0
    gain = gain_ref[...]
    hidden = arrived_ref[...].astype(jnp.float32)
    condition = condition_row(steps_ref, text_ref, number)
    shifted, inverse, normed, sigma = normed_rows(hidden, condition, gain)
    active = (normed * sigma).astype(jnp.bfloat16)
    weight = weight_ref[0]
    upper = hidden + jnp.dot(active, weight, preferred_element_type=jnp.float32)

    @pl.when(down)
    def _():
        out_ref[...] = sent_ref[...]
        active_ref[...] = first_active_ref[...]

    @pl.when(jnp.logical_not(down))
    def _():
        out_ref[...] = upper.astype(jnp.bfloat16)
        active_ref[...] = active

    target = rows_ref[0, number].astype(jnp.float32)
    cot = (upper - target) / math.sqrt(MICRO * ROWS * LANES)
    store_pieces(pieces_ref, 4, cot)
    cot = cot.astype(jnp.bfloat16)
    through = lax.dot_general(
        cot, weight, (((1,), (1,)), ((), ())), preferred_element_type=jnp.float32
    )
    scaled = through * sigma * (1.0 + normed * (1.0 - sigma)) * gain
    inner = jnp.mean(scaled * shifted, axis=-1, keepdims=True)
    back = cot.astype(jnp.float32) + inverse * scaled - shifted * inverse**3 * inner
    store_pieces(pieces_ref, 0, back)


def weight_kernel(*refs):
    active_refs, piece_refs, shares_ref = refs[:8], refs[8:10], refs[10]
    first, second, third, staged = refs[11:15]
    yl, core = lax.axis_index("yl"), lax.axis_index("core")
    low = lax.broadcasted_iota(jnp.int32, (ROWS // 2, 128), 1) < 64
    zero = jnp.zeros((ROWS // 2, 128), jnp.bfloat16)
    product = None
    for offset in range(4):
        source = ((yl + offset // 2) % 2) * 2 + (core + offset % 2) % 2
        rows, right = [], []
        for number in range(MICRO):
            rows.append(active_refs[number * 4 + offset][...])
            piece = piece_refs[number].at[4 + source]
            tail = piece[2 * ROWS :]
            right.append(
                jnp.concatenate(
                    [
                        piece[:ROWS],
                        piece[ROWS : 2 * ROWS],
                        jnp.concatenate([jnp.where(low, tail, zero), jnp.where(low, zero, tail)]),
                    ],
                    axis=1,
                )
            )
        term = lax.dot_general(
            jnp.concatenate(rows), jnp.concatenate(right), (((0,), (0,)), ((), ())),
            preferred_element_type=jnp.float32,
        )
        product = term if product is None else product + term
    first[...] = product[:, :128]
    second[...] = product[:, 128:256]
    third[...] = product[:, 256:] + pltpu.roll(product[:, 256:], 64, 1)
    few = lax.broadcasted_iota(jnp.int32, (5, 128), 1) < 64

    def pack(block, carry):
        base = pl.multiple_of(block * 80, 80)
        to = pl.multiple_of(block * 8 * SHARE, 8 * SHARE)
        for lane in range(8):
            at, put = base + 10 * lane, to + SHARE * lane
            staged[pl.ds(put, 10)] = first[pl.ds(at, 10)]
            staged[pl.ds(put + 16, 10)] = second[pl.ds(at, 10)]
            even = third[pl.ds(at, 5, 2)]
            odd = third[pl.ds(at + 1, 5, 2)]
            staged[pl.ds(put + 10, 5)] = jnp.where(few, even, odd)
        return carry

    staged[...] = jnp.zeros_like(staged)
    lax.fori_loop(0, LANES // 8, pack, 0)
    shares_ref[...] = staged[...].astype(jnp.bfloat16).reshape(LANES, SHARE, 128)


def total_kernel(shares_ref, gradient_ref, tail):
    low = lax.broadcasted_iota(jnp.int32, (5, 128), 1) < 64
    sums = []
    for quarter in range(4):
        yl, core = quarter // 2, quarter % 2
        acc = None
        for yh in range(2):
            for zx in range(16):
                lane = ((yh * 2 + yl) * 16 + zx) * 2 + core
                term = shares_ref[lane].astype(jnp.float32)
                acc = term if acc is None else acc + term
        gradient_ref[:, 256 * quarter : 256 * quarter + 128] = acc[:10]
        gradient_ref[:, 256 * quarter + 128 : 256 * quarter + 256] = acc[16:26]
        sums.append(acc[10:15])
    for pair in range(2):
        left, right = sums[2 * pair], sums[2 * pair + 1]
        at = 1024 + 128 * pair
        tail[pl.ds(0, 5, 2)] = jnp.where(low, left, pltpu.roll(right, 64, 1))
        tail[pl.ds(1, 5, 2)] = jnp.where(low, pltpu.roll(left, 64, 1), right)
        gradient_ref[:, at : at + 128] = tail[...]


def swap(block, axis):
    return lax.ppermute(block, axis, [(0, 1), (1, 0)])


def local(inputs, weights, gains, timesteps, text_pooled):
    half = jax.ShapeDtypeStruct((ROWS, C), jnp.bfloat16)
    sent, first_active, received = [], [], []
    for number in range(MICRO):
        out, active = pl.pallas_call(
            functools.partial(down_kernel, number),
            out_shape=(half, half),
            in_specs=[SMEM, VMEM, VMEM, VMEM, VMEM],
            out_specs=(VMEM, VMEM),
            compiler_params=PARAMS,
        )(timesteps, inputs, weights, gains, text_pooled)
        sent.append(out)
        first_active.append(active)
        received.append(lax.ppermute(out, "section", [(0, 1)]))
    outs, actives, arrived = [], [], []
    for number in range(MICRO):
        out, active, pieces = pl.pallas_call(
            functools.partial(up_kernel, number),
            out_shape=(half, half, jax.ShapeDtypeStruct((8, PIECE, 128), jnp.bfloat16)),
            in_specs=[SMEM] + [VMEM] * 7,
            out_specs=(VMEM, VMEM, VMEM),
            compiler_params=PARAMS,
        )(
            timesteps, received[number], inputs, weights, gains, text_pooled,
            sent[number], first_active[number],
        )
        outs.append(out)
        far = swap(active, "yl")
        near = swap(active, "core")
        actives += [active, near, far, swap(far, "core")]
        arrived.append(lax.all_to_all(pieces, ("section",) + GROUP, 0, 0, tiled=True))
    shares = pl.pallas_call(
        weight_kernel,
        out_shape=jax.ShapeDtypeStruct((LANES, SHARE, 128), jnp.bfloat16),
        in_specs=[VMEM] * 10,
        out_specs=VMEM,
        scratch_shapes=[
            pltpu.VMEM((C, 128), jnp.float32),
            pltpu.VMEM((C, 128), jnp.float32),
            pltpu.VMEM((C, 128), jnp.float32),
            pltpu.VMEM((LANES * SHARE, 128), jnp.float32),
        ],
        compiler_params=PARAMS,
    )(*actives, *arrived)
    shares = lax.all_to_all(shares, DP, 0, 0, tiled=True)
    gradient = pl.pallas_call(
        total_kernel,
        out_shape=jax.ShapeDtypeStruct((C // LANES, C), jnp.float32),
        in_specs=[VMEM],
        out_specs=VMEM,
        scratch_shapes=[pltpu.VMEM((C // LANES, 128), jnp.float32)],
        compiler_params=PARAMS,
    )(shares)
    return (jnp.stack(outs)[None], gradient[None])


def solution(mesh):
    fine = Mesh(mesh.devices.reshape(2, 2, 2, 8, 2, 2), ("section",) + DP)
    return jax.shard_map(
        local,
        mesh=fine,
        in_specs=(
            P("section", None, DP, None),
            P("section", None, None),
            P("section", None),
            P(),
            P(),
        ),
        out_specs=(P("section", None, DP, None), P("section", DP, None)),
        check_vma=False,
    )
```

time: 147 us -> 117 us (0.80)
  waiting for transfers between devices: 80.9 us -> 59.6 us
  matrix products: 14.9 us -> 0 us
  Pallas kernels: 0 us -> 13.8 us
  other arithmetic: 13.7 us -> 0.9 us
  starting transfers between devices: 22.6 us -> 30.9 us
    ppermute x3 -> x6, waiting for transfers between devices: 27.1 us -> 5.95 us  [swap(): return lax.ppermute(block, axis, [(0, 1), (1, 0)])]
    dot_general x10 -> x0, matrix products: 14.9 us -> none  [the longest x4 6.8 us: local(): lax.dot_general(block, rows, (((0,), (0,)), ((), ())), preferred_element_...]
    pallas_call x0 -> x6, Pallas kernels: none -> 13.8 us  [the longest x2 6.2 us: local(): pl.pallas_call(functools.partial(up_kernel, number), out_shape=(half, hal...]
    unnamed x8 -> x33, local copies, waits for them, and re-layouts: 0.02 us -> 10.1 us
    all_to_all x1, waiting for transfers between devices: 37.5 us -> 28.6 us  [local(): shares = lax.all_to_all(shares, DP, 0, 0, tiled=True)]
    all_to_all x1 -> x2, starting transfers between devices: 4.78 us -> 10.6 us  [local(): lax.all_to_all(pieces, ('section',) + GROUP, 0, 0, tiled=True)]
    reshape x2 -> x0, local copies, waits for them, and re-layouts: 5.64 us -> none  [the longest x1 3.1 us: local(): partial.astype(jnp.bfloat16).reshape(LANES, width // LANES, quarter)]
    ppermute x2, waiting for transfers between devices: 16.3 us -> 21.9 us  [local(): received.append(lax.ppermute(out, 'section', [(0, 1)]))]
  transfers between devices with their start and end apart: 7 -> 11, of which waited for: 4 -> 5; matrix products, arithmetic and copies ran while one was open for 8% -> 1% of each run, Pallas kernels for 0% -> 4%
where the time goes in v2:
time: 117 us; the launch traced here: 116 us
  waiting for transfers between devices  59.6 us (51%)
  starting transfers between devices  30.9 us (26%)
  Pallas kernels  13.8 us (12%)
  local copies, waits for them, and re-layouts  10.1 us (9%)
    all_to_all x1, waiting for transfers between devices, local(): shares = lax.all_to_all(shares, DP, 0, 0, tiled=True)  28.6 us
    ppermute x2, waiting for transfers between devices, local(): received.append(lax.ppermute(out, 'section', [(0, 1)]))  21.9 us
    all_to_all x1, starting transfers between devices, local(): shares = lax.all_to_all(shares, DP, 0, 0, tiled=True)  13.7 us
    all_to_all x2, starting transfers between devices, local(): lax.all_to_all(pieces, ('section',) + GROUP, 0, 0, tiled=True)  10.6 us
    unnamed x33, local copies, waits for them, and re-layouts  10.1 us
    pallas_call x2, Pallas kernels, local(): pl.pallas_call(functools.partial(up_kernel, number), out_shape=(half, hal...  6.2 us
    ppermute x6, waiting for transfers between devices, swap(): return lax.ppermute(block, axis, [(0, 1), (1, 0)])  5.95 us
    pallas_call x1, Pallas kernels, local(): pl.pallas_call(weight_kernel, out_shape=jax.ShapeDtypeStruct((LANES, SHAR...  4.49 us
  transfers between devices with their start and end apart: 11, of which 5 were waited for; matrix products, arithmetic and copies ran while one was open for 1% of the time, Pallas kernels for 4%

profile of v2, /device:TPU:6, one launch (start us, length us, event | category | flops | bytes accessed | tf_op | source)
XLA Modules:
  0.0 116.2 jit_solution(16724130108929595329)
XLA Ops:
  0.6 1.9 %copy-done = bf16[1,1280,1280]{2,1,0:T(8,128)(2,1)S(1)} copy-done((bf16[1,1280,1280]{2,1,0:T(8,128)(2,1)S(1)}, bf16[1,1280,1280]{2,1,0:T(8,128)(2,1)}, u32[]{:S(2)}) %copy-start) | copy-done | bytes 3276824
  2.6 1.1 copy-done.2
  3.6 0.9 copy-done.4
  4.5 0.7 copy-done.12
  5.2 0.7 copy-done.14
  5.9 1.5 %shard_map.68 = (bf16[128,1280]{1,0:T(8,128)(2,1)S(1)}, bf16[128,1280]{1,0:T(8,128)(2,1)S(1)}) custom-call(s32[2,16]{1,0:T(2,128)S(1)} %copy-done.14, bf16[1,2,128,1280]{3,2,1,0:T(8,128)(2,1)S(1)} %copy-done.2, bf16[1,1280,1280]{2,1,0:T(8,128)(2,1)S(1)} %copy-done, f32[1,1280]{1,0:T(1,128)S(1)} %copy-done.12, bf16[2,16,1280]{2,1,0:T(8,128)(2,1)S(1)} %copy-done.4), custom_call_target="tpu_custom_call" | custom-call | tf_op jit(solution)/shard_map/pallas_call | solution.py:189
  7.4 1.6 %collective-permute-start = (bf16[128,1280]{1,0:T(8,128)(2,1)S(1)}, bf16[128,1280]{1,0:T(8,128)(2,1)S(1)}, u32[]{:S(2)}, u32[]{:S(2)}) collective-permute-start(bf16[128,1280]{1,0:T(8,128)(2,1)S(1)} %get-tuple-element.12.sent_ref), channel_id=1, source_target_pairs={{0,128},{1,129},{2,130},{3,131},{4,132},{5,133},{6,134},{7,135},{8... | collective-permute-start | bytes 983048 | tf_op jit(solution)/shard_map/ppermute | solution.py:198
  9.0 11.5 %collective-permute-done.arrived_ref = bf16[128,1280]{1,0:T(8,128)(2,1)S(1)} collective-permute-done((bf16[128,1280]{1,0:T(8,128)(2,1)S(1)}, bf16[128,1280]{1,0:T(8,128)(2,1)S(1)}, u32[]{:S(2)}, u32[]{:S(2)}) %collective-permute-start) | collective-permute-done | bytes 327712 | tf_op jit(solution)/shard_map/ppermute | solution.py:198
  20.5 3.1 %shard_map.69 = (bf16[128,1280]{1,0:T(8,128)(2,1)S(1)}, bf16[128,1280]{1,0:T(8,128)(2,1)}, bf16[8,320,128]{2,1,0:T(8,128)(2,1)S(1)}) custom-call(s32[2,16]{1,0:T(2,128)S(1)} %copy-done.15, bf16[128,1280]{1,0:T(8,128)(2,1)S(1)} %collective-permute-done.arrived_ref, bf16[1,2,128,1280]{3,2,1,0:T(8,128)(2,1)S(1)} %copy-done.2, ...), custom_call_target="tpu_custom_call" | custom-call | tf_op jit(solution)/shard_map/pallas_call | solution.py:201
  23.6 0.8 copy-done.7
  24.5 0.7 copy-done.8
  25.2 5.8 %all-to-all-start = ((bf16[8,320,128]{2,1,0:T(8,128)(2,1)}), bf16[8,320,128]{2,1,0:T(8,128)(2,1)}, u32[]{:S(2)}, u32[]{:S(2)}) async-start(bf16[8,320,128]{2,1,0:T(8,128)(2,1)} %copy-done.7), calls=%async_computation | async-start | bytes 1310720 | tf_op jit(solution)/shard_map/all_to_all | solution.py:215
  31.0 1.1 copy-done.3
  32.1 1.5 %shard_map.70 = (bf16[128,1280]{1,0:T(8,128)(2,1)S(1)}, bf16[128,1280]{1,0:T(8,128)(2,1)S(1)}) custom-call(s32[2,16]{1,0:T(2,128)S(1)} %copy-done.15, bf16[1,2,128,1280]{3,2,1,0:T(8,128)(2,1)S(1)} %copy-done.3, bf16[1,1280,1280]{2,1,0:T(8,128)(2,1)S(1)} %copy-done.1, f32[1,1280]{1,0:T(1,128)S(1)} %copy-done.13, bf16[2,16,1280]{2,1,0:T(8,128)(2,1)S(1)} %copy-done.5), custom_call_target="tpu_custom_call" | custom-call | tf_op jit(solution)/shard_map/pallas_call | solution.py:189
  33.6 1.3 %collective-permute-start.1 = (bf16[128,1280]{1,0:T(8,128)(2,1)S(1)}, bf16[128,1280]{1,0:T(8,128)(2,1)S(1)}, u32[]{:S(2)}, u32[]{:S(2)}) collective-permute-start(bf16[128,1280]{1,0:T(8,128)(2,1)S(1)} %get-tuple-element.15.sent_ref), channel_id=1, source_target_pairs={{0,128},{1,129},{2,130},{3,131},{4,132},{5,133},{6,134},{7,135},{8... | collective-permute-start | bytes 983048 | tf_op jit(solution)/shard_map/ppermute | solution.py:198
  34.9 1.6 %collective-permute-start.3 = (bf16[128,1280]{1,0:T(8,128)(2,1)}, bf16[128,1280]{1,0:T(8,128)(2,1)}, u32[]{:S(2)}, u32[]{:S(2)}) collective-permute-start(bf16[128,1280]{1,0:T(8,128)(2,1)} %get-tuple-element.18.refs_0_), channel_id=1, source_target_pairs={{0,32},{32,0},{1,33},{33,1},{2,34},{34,2},{3,35},{35,3},{4,36},{36... | collective-permute-start | bytes 983048 | tf_op jit(solution)/shard_map/ppermute | solution.py:182
  36.5 10.3 %collective-permute-done.1.arrived_ref = bf16[128,1280]{1,0:T(8,128)(2,1)S(1)} collective-permute-done((bf16[128,1280]{1,0:T(8,128)(2,1)S(1)}, bf16[128,1280]{1,0:T(8,128)(2,1)S(1)}, u32[]{:S(2)}, u32[]{:S(2)}) %collective-permute-start.1) | collective-permute-done | bytes 327712 | tf_op jit(solution)/shard_map/ppermute | solution.py:198
  46.8 3.1 %shard_map.71 = (bf16[128,1280]{1,0:T(8,128)(2,1)S(1)}, bf16[128,1280]{1,0:T(8,128)(2,1)}, bf16[8,320,128]{2,1,0:T(8,128)(2,1)S(1)}) custom-call(s32[2,16]{1,0:T(2,128)S(1)} %copy-done.15, bf16[128,1280]{1,0:T(8,128)(2,1)S(1)} %collective-permute-done.1.arrived_ref, bf16[1,2,128,1280]{3,2,1,0:T(8,128)(2,1)S(1)} %copy-done.3, ...), custom_call_target="tpu_custom_call" | custom-call | tf_op jit(solution)/shard_map/pallas_call | solution.py:201
  49.9 0.8 copy-done.6
  50.7 0.7 copy-done.10
  51.4 1.5 %collective-permute-start.6 = (bf16[128,1280]{1,0:T(8,128)(2,1)}, bf16[128,1280]{1,0:T(8,128)(2,1)S(1)}, u32[]{:S(2)}, u32[]{:S(2)}) collective-permute-start(bf16[128,1280]{1,0:T(8,128)(2,1)} %get-tuple-element.19.refs_4_), channel_id=1, source_target_pairs={{0,32},{32,0},{1,33},{33,1},{2,34},{34,2},{3,35},{35,3},{4,36},{36... | collective-permute-start | bytes 983048 | tf_op jit(solution)/shard_map/ppermute | solution.py:182
  53.0 4.8 %all-to-all-start.1 = ((bf16[8,320,128]{2,1,0:T(8,128)(2,1)}), bf16[8,320,128]{2,1,0:T(8,128)(2,1)S(1)}, u32[]{:S(2)}, u32[]{:S(2)}) async-start(bf16[8,320,128]{2,1,0:T(8,128)(2,1)} %copy-done.6), calls=%async_computation.1 | async-start | bytes 1310720 | tf_op jit(solution)/shard_map/all_to_all | solution.py:215
  57.9 0.4 collective-permute-start.5
  58.3 0.1 collective-permute-start.4
  58.4 5.9 %collective-permute-done.6.refs_6_ = bf16[128,1280]{1,0:T(8,128)(2,1)S(1)} collective-permute-done((bf16[128,1280]{1,0:T(8,128)(2,1)}, bf16[128,1280]{1,0:T(8,128)(2,1)S(1)}, u32[]{:S(2)}, u32[]{:S(2)}) %collective-permute-start.6) | collective-permute-done | bytes 327712 | tf_op jit(solution)/shard_map/ppermute | solution.py:182
  64.4 3.2 %all-to-all-done.1.refs_9_ = bf16[8,320,128]{2,1,0:T(8,128)(2,1)S(1)} async-done(((bf16[8,320,128]{2,1,0:T(8,128)(2,1)}), bf16[8,320,128]{2,1,0:T(8,128)(2,1)S(1)}, u32[]{:S(2)}, u32[]{:S(2)}) %all-to-all-start.1) | async-done | bytes 655392 | tf_op jit(solution)/shard_map/all_to_all | solution.py:215
  67.6 4.5 %shard_map.72 = bf16[128,32,128]{2,1,0:T(8,128)(2,1)} custom-call(bf16[128,1280]{1,0:T(8,128)(2,1)} %get-tuple-element.18.refs_0_, bf16[128,1280]{1,0:T(8,128)(2,1)S(1)} %collective-permute-done.2.refs_1_, bf16[128,1280]{1,0:T(8,128)(2,1)} %collective-permute-done.3.refs_2_, bf16[128,1280]{1,0:T(8,128)(2,1)S(1)} %collective-permute-done.4.refs_3_, ...), custom_call_target="tpu_custom_call" | custom-call | tf_op jit(solution)/shard_map/pallas_call | solution.py:216
  72.1 13.7 %all-to-all-start.2 = ((bf16[128,32,128]{2,1,0:T(8,128)(2,1)}), bf16[128,32,128]{2,1,0:T(8,128)(2,1)S(1)}, u32[]{:S(2)}, u32[]{:S(2)}) async-start(bf16[128,32,128]{2,1,0:T(8,128)(2,1)} %shard_map.72), calls=%async_computation.2 | async-start | bytes 2097152 | tf_op jit(solution)/shard_map/all_to_all | solution.py:229
  85.8 0.9 maximum_bitcast_fusion
  86.7 28.6 %all-to-all-done.2.shares_ref = bf16[128,32,128]{2,1,0:T(8,128)(2,1)S(1)} async-done(((bf16[128,32,128]{2,1,0:T(8,128)(2,1)}), bf16[128,32,128]{2,1,0:T(8,128)(2,1)S(1)}, u32[]{:S(2)}, u32[]{:S(2)}) %all-to-all-start.2) | async-done | bytes 1048608 | tf_op jit(solution)/shard_map/all_to_all | solution.py:229
  115.3 0.2 shard_map.73
  115.5 0.7 copy.7
  (30 shorter events, 0.2 us)
Async XLA Ops:
  0.6 1.9 %copy-start = (bf16[1,1280,1280]{2,1,0:T(8,128)(2,1)S(1)}, bf16[1,1280,1280]{2,1,0:T(8,128)(2,1)}, u32[]{:S(2)}) copy-start(bf16[1,1280,1280]{2,1,0:T(8,128)(2,1)} %weight_ref.7) | copy-start | bytes 9830404
  2.6 1.1 copy-start.2
  3.6 0.9 copy-start.4
  4.5 0.7 copy-start.12
  5.2 0.7 copy-start.14
  5.9 14.6 %copy-start.13 = (f32[1,1280]{1,0:T(1,128)S(1)}, f32[1,1280]{1,0:T(1,128)}, u32[]{:S(2)}) copy-start(f32[1,1280]{1,0:T(1,128)} %gain_ref.7) | copy-start | bytes 15364
  5.9 14.6 %copy-start.15 = (s32[2,16]{1,0:T(2,128)S(1)}, s32[2,16]{1,0:T(2,128)}, u32[]{:S(2)}) copy-start(s32[2,16]{1,0:T(2,128)} %steps_ref.7) | copy-start | bytes 388
  7.4 23.6 %copy-start.1 = (bf16[1,1280,1280]{2,1,0:T(8,128)(2,1)S(1)}, bf16[1,1280,1280]{2,1,0:T(8,128)(2,1)}, u32[]{:S(2)}) copy-start(bf16[1,1280,1280]{2,1,0:T(8,128)(2,1)} %weight_ref.7) | copy-start | bytes 9830404
  7.4 23.6 %copy-start.5 = (bf16[2,16,1280]{2,1,0:T(8,128)(2,1)S(1)}, bf16[2,16,1280]{2,1,0:T(8,128)(2,1)}, u32[]{:S(2)}) copy-start(bf16[2,16,1280]{2,1,0:T(8,128)(2,1)} %text_ref.7) | copy-start | bytes 245764
  7.4 13.1 %collective-permute-start = (bf16[128,1280]{1,0:T(8,128)(2,1)S(1)}, bf16[128,1280]{1,0:T(8,128)(2,1)S(1)}, u32[]{:S(2)}, u32[]{:S(2)}) collective-permute-start(bf16[128,1280]{1,0:T(8,128)(2,1)S(1)} %get-tuple-element.12.sent_ref), channel_id=1, source_target_pairs={{0,128},{1,129},{2,130},{3,131},{4,132},{5,133},{6,134},{7,135},{8... | collective-permute-start | bytes 983048 | tf_op jit(solution)/shard_map/ppermute | solution.py:198
  23.6 0.8 copy-start.7
  24.5 0.7 copy-start.8
  25.2 27.8 %all-to-all-start = ((bf16[8,320,128]{2,1,0:T(8,128)(2,1)}), bf16[8,320,128]{2,1,0:T(8,128)(2,1)}, u32[]{:S(2)}, u32[]{:S(2)}) async-start(bf16[8,320,128]{2,1,0:T(8,128)(2,1)} %copy-done.7), calls=%async_computation | async-start | bytes 1310720 | tf_op jit(solution)/shard_map/all_to_all | solution.py:215
  31.0 1.1 copy-start.3
  33.6 13.2 %collective-permute-start.1 = (bf16[128,1280]{1,0:T(8,128)(2,1)S(1)}, bf16[128,1280]{1,0:T(8,128)(2,1)S(1)}, u32[]{:S(2)}, u32[]{:S(2)}) collective-permute-start(bf16[128,1280]{1,0:T(8,128)(2,1)S(1)} %get-tuple-element.15.sent_ref), channel_id=1, source_target_pairs={{0,128},{1,129},{2,130},{3,131},{4,132},{5,133},{6,134},{7,135},{8... | collective-permute-start | bytes 983048 | tf_op jit(solution)/shard_map/ppermute | solution.py:198
  34.9 23.4 %collective-permute-start.3 = (bf16[128,1280]{1,0:T(8,128)(2,1)}, bf16[128,1280]{1,0:T(8,128)(2,1)}, u32[]{:S(2)}, u32[]{:S(2)}) collective-permute-start(bf16[128,1280]{1,0:T(8,128)(2,1)} %get-tuple-element.18.refs_0_), channel_id=1, source_target_pairs={{0,32},{32,0},{1,33},{33,1},{2,34},{34,2},{3,35},{35,3},{4,36},{36... | collective-permute-start | bytes 983048 | tf_op jit(solution)/shard_map/ppermute | solution.py:182
  49.9 0.8 copy-start.6
  50.7 0.7 copy-start.10
  51.4 12.9 %collective-permute-start.6 = (bf16[128,1280]{1,0:T(8,128)(2,1)}, bf16[128,1280]{1,0:T(8,128)(2,1)S(1)}, u32[]{:S(2)}, u32[]{:S(2)}) collective-permute-start(bf16[128,1280]{1,0:T(8,128)(2,1)} %get-tuple-element.19.refs_4_), channel_id=1, source_target_pairs={{0,32},{32,0},{1,33},{33,1},{2,34},{34,2},{3,35},{35,3},{4,36},{36... | collective-permute-start | bytes 983048 | tf_op jit(solution)/shard_map/ppermute | solution.py:182
  53.0 14.6 %all-to-all-start.1 = ((bf16[8,320,128]{2,1,0:T(8,128)(2,1)}), bf16[8,320,128]{2,1,0:T(8,128)(2,1)S(1)}, u32[]{:S(2)}, u32[]{:S(2)}) async-start(bf16[8,320,128]{2,1,0:T(8,128)(2,1)} %copy-done.6), calls=%async_computation.1 | async-start | bytes 1310720 | tf_op jit(solution)/shard_map/all_to_all | solution.py:215
  57.8 28.1 %copy-start.9 = (bf16[128,1280]{1,0:T(8,128)(2,1)S(1)}, bf16[128,1280]{1,0:T(8,128)(2,1)}, u32[]{:S(2)}) copy-start(bf16[128,1280]{1,0:T(8,128)(2,1)} %copy-done.8) | copy-start | bytes 983044
  57.8 28.1 %copy-start.11 = (bf16[128,1280]{1,0:T(8,128)(2,1)S(1)}, bf16[128,1280]{1,0:T(8,128)(2,1)}, u32[]{:S(2)}) copy-start(bf16[128,1280]{1,0:T(8,128)(2,1)} %copy-done.10) | copy-start | bytes 983044
  57.8 6.6 %collective-permute-start.2 = (bf16[128,1280]{1,0:T(8,128)(2,1)}, bf16[128,1280]{1,0:T(8,128)(2,1)S(1)}, u32[]{:S(2)}, u32[]{:S(2)}) collective-permute-start(bf16[128,1280]{1,0:T(8,128)(2,1)} %get-tuple-element.18.refs_0_), channel_id=1, source_target_pairs={{0,1},{1,0},{2,3},{3,2},{4,5},{5,4},{6,7},{7,6},{8,9},{9,8},{10,11... | collective-permute-start | bytes 983048 | tf_op jit(solution)/shard_map/ppermute | solution.py:182
  57.9 6.5 %collective-permute-start.5 = (bf16[128,1280]{1,0:T(8,128)(2,1)}, bf16[128,1280]{1,0:T(8,128)(2,1)S(1)}, u32[]{:S(2)}, u32[]{:S(2)}) collective-permute-start(bf16[128,1280]{1,0:T(8,128)(2,1)} %get-tuple-element.19.refs_4_), channel_id=1, source_target_pairs={{0,1},{1,0},{2,3},{3,2},{4,5},{5,4},{6,7},{7,6},{8,9},{9,8},{10,11... | collective-permute-start | bytes 983048 | tf_op jit(solution)/shard_map/ppermute | solution.py:182
  58.3 9.3 %collective-permute-start.4 = (bf16[128,1280]{1,0:T(8,128)(2,1)}, bf16[128,1280]{1,0:T(8,128)(2,1)S(1)}, u32[]{:S(2)}, u32[]{:S(2)}) collective-permute-start(bf16[128,1280]{1,0:T(8,128)(2,1)} %collective-permute-done.3.refs_2_), channel_id=1, source_target_pairs={{0,1},{1,0},{2,3},{3,2},{4,5},{5,4},{6,7},{7,6},{8,9},{9,8},{10,11... | collective-permute-start | bytes 983048 | tf_op jit(solution)/shard_map/ppermute | solution.py:182
  64.4 3.2 %collective-permute-start.7 = (bf16[128,1280]{1,0:T(8,128)(2,1)S(1)}, bf16[128,1280]{1,0:T(8,128)(2,1)S(1)}, u32[]{:S(2)}, u32[]{:S(2)}) collective-permute-start(bf16[128,1280]{1,0:T(8,128)(2,1)S(1)} %collective-permute-done.6.refs_6_), channel_id=1, source_target_pairs={{0,1},{1,0},{2,3},{3,2},{4,5},{5,4},{6,7},{7,6},{8,9},{9,8},{10,11... | collective-permute-start | bytes 983048 | tf_op jit(solution)/shard_map/ppermute | solution.py:182
  72.1 43.2 %all-to-all-start.2 = ((bf16[128,32,128]{2,1,0:T(8,128)(2,1)}), bf16[128,32,128]{2,1,0:T(8,128)(2,1)S(1)}, u32[]{:S(2)}, u32[]{:S(2)}) async-start(bf16[128,32,128]{2,1,0:T(8,128)(2,1)} %shard_map.72), calls=%async_computation.2 | async-start | bytes 2097152 | tf_op jit(solution)/shard_map/all_to_all | solution.py:229

commit v3 on v2

v3 whole, which is shorter than its diff:
```python
import functools
import math

import jax
import jax.numpy as jnp
from jax import lax
from jax.experimental import pallas as pl
from jax.experimental.pallas import tpu as pltpu
from jax.sharding import Mesh, PartitionSpec as P

PIX = 1024
MICRO = 2
ROWS = 128
LANES = 128
C = 1280
DP = ("yh", "yl", "z", "x", "core")
GROUP = ("yl", "core")
PIECE = 320
SHARE = 32
PARAMS = pltpu.CompilerParams(vmem_limit_bytes=40 * 1024 * 1024)
WHOLE = pltpu.CompilerParams(vmem_limit_bytes=61 * 1024 * 1024)
MOST = pltpu.CompilerParams(vmem_limit_bytes=53 * 1024 * 1024)
VMEM = pl.BlockSpec(memory_space=pltpu.VMEM)
HBM = pl.BlockSpec(memory_space=pltpu.HBM)


def condition_row(steps_ref, text_ref, number):
    latent = lax.axis_index(DP) * ROWS // PIX
    step = steps_ref[number, latent].astype(jnp.float32)
    lane = lax.broadcasted_iota(jnp.int32, (1, C), 1)
    index = jnp.where(lane < C // 2, lane, lane - C // 2).astype(jnp.float32)
    angle = step * jnp.exp(-math.log(10000.0) * index / (C // 2))
    waves = jnp.where(lane < C // 2, jnp.cos(angle), jnp.sin(angle))
    text = text_ref[number].astype(jnp.float32)
    mine = lax.broadcasted_iota(jnp.int32, text.shape, 0) == latent
    return waves + jnp.sum(jnp.where(mine, text, 0.0), axis=0, keepdims=True)


def normed_rows(hidden, condition, gain):
    shifted = hidden + condition
    inverse = lax.rsqrt(jnp.mean(shifted * shifted, axis=-1, keepdims=True) + 1e-05)
    normed = shifted * inverse * gain
    sigma = 1.0 / (1.0 + jnp.exp(-normed))
    return shifted, inverse, normed, sigma


def down_kernel(
    steps_hbm, rows_hbm, weight_hbm, gain_hbm, text_hbm, sent_0, sent_1, active_0, active_1, cond_ref,
    steps_ref, rows_ref, weight_ref, gain_ref, text_ref, sems,
):
    copies = [
        pltpu.make_async_copy(source, target, sems.at[at])
        for at, (source, target) in enumerate(
            (
                (steps_hbm, steps_ref),
                (text_hbm, text_ref),
                (rows_hbm.at[0], rows_ref),
                (gain_hbm, gain_ref),
                (weight_hbm.at[0], weight_ref),
            )
        )
    ]
    for copy in copies:
        copy.start()
    copies[0].wait()
    copies[1].wait()
    for number in range(MICRO):
        cond_ref[number] = condition_row(steps_ref, text_ref, number)
    copies[2].wait()
    copies[3].wait()
    for number, sent_ref, active_ref in ((0, sent_0, active_0), (1, sent_1, active_1)):
        hidden = rows_ref[number].astype(jnp.float32)
        _, _, normed, sigma = normed_rows(hidden, cond_ref[number], gain_ref[...])
        active = (normed * sigma).astype(jnp.bfloat16)
        active_ref[...] = active
        if number == 0:
            copies[4].wait()
        result = hidden + jnp.dot(active, weight_ref[...], preferred_element_type=jnp.float32)
        sent_ref[...] = result.astype(jnp.bfloat16)


def store_pieces(pieces_ref, first, values):
    half = ROWS // 2
    low = lax.broadcasted_iota(jnp.int32, (half, 128), 1) < 64
    rounded = values.astype(jnp.bfloat16)
    for quarter in range(4):
        slot = first + quarter
        pieces_ref[slot, :ROWS] = rounded[:, 256 * quarter : 256 * quarter + 128]
        pieces_ref[slot, ROWS : 2 * ROWS] = rounded[:, 256 * quarter + 128 : 256 * quarter + 256]
        at = 1024 + 128 * (quarter // 2)
        block = values[:, at : at + 128]
        turned = pltpu.roll(block, 64, 1)
        top, bottom = (block, turned) if quarter % 2 == 0 else (turned, block)
        pieces_ref[slot, 2 * ROWS :] = jnp.where(low, top[:half], bottom[half:]).astype(
            jnp.bfloat16
        )


def up_kernel(
    number, cond_ref, arrived_ref, rows_hbm, weight_hbm, gain_ref, sent_hbm, first_active_hbm,
    outs_in, outs_hbm, active_ref, pieces_hbm, out_ref, pieces_ref, rows_ref, sent_ref,
    first_active_ref, weight_ref, sems,
):
    del outs_in
    copies = [
        pltpu.make_async_copy(rows_hbm.at[0, number], rows_ref, sems.at[3]),
        pltpu.make_async_copy(sent_hbm, sent_ref, sems.at[4]),
        pltpu.make_async_copy(first_active_hbm, first_active_ref, sems.at[5]),
        pltpu.make_async_copy(weight_hbm.at[0], weight_ref, sems.at[6]),
    ]
    for copy in copies:
        copy.start()
    down = lax.axis_index("section") == 0
    gain = gain_ref[...]
    hidden = arrived_ref[...].astype(jnp.float32)
    shifted, inverse, normed, sigma = normed_rows(hidden, cond_ref[number], gain)
    active = (normed * sigma).astype(jnp.bfloat16)
    for copy in copies:
        copy.wait()
    weight = weight_ref[...]
    upper = hidden + jnp.dot(active, weight, preferred_element_type=jnp.float32)

    @pl.when(down)
    def _():
        out_ref[...] = sent_ref[...]
        active_ref[...] = first_active_ref[...]

    @pl.when(jnp.logical_not(down))
    def _():
        out_ref[...] = upper.astype(jnp.bfloat16)
        active_ref[...] = active

    out_copy = pltpu.make_async_copy(out_ref, outs_hbm.at[0, number], sems.at[0])
    out_copy.start()
    target = rows_ref[...].astype(jnp.float32)
    cot = (upper - target) / math.sqrt(MICRO * ROWS * LANES)
    store_pieces(pieces_ref, 4, cot)
    cot_copy = pltpu.make_async_copy(
        pieces_ref.at[pl.ds(4, 4)], pieces_hbm.at[pl.ds(4, 4)], sems.at[1]
    )
    cot_copy.start()
    cot = cot.astype(jnp.bfloat16)
    through = lax.dot_general(
        cot, weight, (((1,), (1,)), ((), ())), preferred_element_type=jnp.float32
    )
    scaled = through * sigma * (1.0 + normed * (1.0 - sigma)) * gain
    inner = jnp.mean(scaled * shifted, axis=-1, keepdims=True)
    back = cot.astype(jnp.float32) + inverse * scaled - shifted * inverse**3 * inner
    store_pieces(pieces_ref, 0, back)
    back_copy = pltpu.make_async_copy(
        pieces_ref.at[pl.ds(0, 4)], pieces_hbm.at[pl.ds(0, 4)], sems.at[2]
    )
    back_copy.start()
    out_copy.wait()
    cot_copy.wait()
    back_copy.wait()


def weight_product(active_refs, piece_ref):
    yl, core = lax.axis_index("yl"), lax.axis_index("core")
    low = lax.broadcasted_iota(jnp.int32, (ROWS // 2, 128), 1) < 64
    zero = jnp.zeros((ROWS // 2, 128), jnp.bfloat16)
    rows, right = [], []
    for offset in range(4):
        source = ((yl + offset // 2) % 2) * 2 + (core + offset % 2) % 2
        rows.append(active_refs[offset][...])
        piece = piece_ref.at[4 + source]
        tail = piece[2 * ROWS :]
        right.append(
            jnp.concatenate(
                [
                    piece[:ROWS],
                    piece[ROWS : 2 * ROWS],
                    jnp.concatenate([jnp.where(low, tail, zero), jnp.where(low, zero, tail)]),
                ],
                axis=1,
            )
        )
    return lax.dot_general(
        jnp.concatenate(rows), jnp.concatenate(right), (((0,), (0,)), ((), ())),
        preferred_element_type=jnp.float32,
    )


def first_weight_kernel(own, near, far, far_core, piece_ref, product_ref):
    product_ref[...] = weight_product((own, near, far, far_core), piece_ref)


def weight_kernel(
    own, near, far, far_core, piece_ref, earlier_ref, shares_ref, first, second, third, staged
):
    product = weight_product((own, near, far, far_core), piece_ref) + earlier_ref[...]
    first[...] = product[:, :128]
    second[...] = product[:, 128:256]
    third[...] = product[:, 256:] + pltpu.roll(product[:, 256:], 64, 1)
    few = lax.broadcasted_iota(jnp.int32, (5, 128), 1) < 64

    def pack(block, carry):
        base = pl.multiple_of(block * 80, 80)
        to = pl.multiple_of(block * 8 * SHARE, 8 * SHARE)
        for lane in range(8):
            at, put = base + 10 * lane, to + SHARE * lane
            staged[pl.ds(put, 10)] = first[pl.ds(at, 10)]
            staged[pl.ds(put + 16, 10)] = second[pl.ds(at, 10)]
            even = third[pl.ds(at, 5, 2)]
            odd = third[pl.ds(at + 1, 5, 2)]
            staged[pl.ds(put + 10, 5)] = jnp.where(few, even, odd)
        return carry

    staged[...] = jnp.zeros_like(staged)
    lax.fori_loop(0, LANES // 8, pack, 0)
    shares_ref[...] = staged[...].astype(jnp.bfloat16).reshape(LANES, SHARE, 128)


def total_kernel(shares_ref, gradient_ref, tail):
    low = lax.broadcasted_iota(jnp.int32, (5, 128), 1) < 64
    sums = []
    for quarter in range(4):
        yl, core = quarter // 2, quarter % 2
        acc = None
        for yh in range(2):
            for zx in range(16):
                lane = ((yh * 2 + yl) * 16 + zx) * 2 + core
                term = shares_ref[lane].astype(jnp.float32)
                acc = term if acc is None else acc + term
        gradient_ref[:, 0, 256 * quarter : 256 * quarter + 128] = acc[:10]
        gradient_ref[:, 0, 256 * quarter + 128 : 256 * quarter + 256] = acc[16:26]
        sums.append(acc[10:15])
    for pair in range(2):
        left, right = sums[2 * pair], sums[2 * pair + 1]
        at = 1024 + 128 * pair
        tail[pl.ds(0, 5, 2)] = jnp.where(low, left, pltpu.roll(right, 64, 1))
        tail[pl.ds(1, 5, 2)] = jnp.where(low, pltpu.roll(left, 64, 1), right)
        gradient_ref[:, 0, at : at + 128] = tail[...]


def swap(block, axis):
    return lax.ppermute(block, axis, [(0, 1), (1, 0)])


def local(inputs, weights, gains, timesteps, text_pooled):
    half = jax.ShapeDtypeStruct((ROWS, C), jnp.bfloat16)
    *made, condition = pl.pallas_call(
        down_kernel,
        out_shape=(half,) * 4 + (jax.ShapeDtypeStruct((MICRO, 1, C), jnp.float32),),
        in_specs=[HBM] * 5,
        out_specs=(VMEM,) * 5,
        scratch_shapes=[
            pltpu.SMEM(timesteps.shape, jnp.int32),
            pltpu.VMEM(inputs.shape[1:], jnp.bfloat16),
            pltpu.VMEM(weights.shape[1:], jnp.bfloat16),
            pltpu.VMEM(gains.shape, jnp.float32),
            pltpu.VMEM(text_pooled.shape, jnp.bfloat16),
            pltpu.SemaphoreType.DMA((5,)),
        ],
        compiler_params=WHOLE,
    )(timesteps, inputs, weights, gains, text_pooled)
    sent, first_active = made[:2], made[2:]
    received = [lax.ppermute(rows, "section", [(0, 1)]) for rows in sent]
    outs = None
    actives, arrived = [], []
    for number in range(MICRO):
        up = pl.pallas_call(
            functools.partial(up_kernel, number),
            out_shape=(
                jax.ShapeDtypeStruct(inputs.shape, jnp.bfloat16),
                half,
                jax.ShapeDtypeStruct((8, PIECE, 128), jnp.bfloat16),
            ),
            in_specs=[VMEM, VMEM, HBM, HBM, VMEM, HBM, HBM, HBM],
            out_specs=(HBM, VMEM, HBM),
            scratch_shapes=[
                pltpu.VMEM((ROWS, C), jnp.bfloat16),
                pltpu.VMEM((8, PIECE, 128), jnp.bfloat16),
                pltpu.VMEM((ROWS, C), jnp.bfloat16),
                pltpu.VMEM((ROWS, C), jnp.bfloat16),
                pltpu.VMEM((ROWS, C), jnp.bfloat16),
                pltpu.VMEM((C, C), jnp.bfloat16),
                pltpu.SemaphoreType.DMA((7,)),
            ],
            input_output_aliases={7: 0} if number else {},
            compiler_params=MOST,
            cost_estimate=pl.CostEstimate(flops=2_000_000_000, bytes_accessed=4_000_000, transcendentals=0),
        )
        outs, active, pieces = up(
            condition, received[number], inputs, weights, gains, sent[number],
            first_active[number], outs if number else inputs,
        )
        far = swap(active, "yl")
        near = swap(active, "core")
        actives.append((active, near, far, swap(far, "core")))
        arrived.append(lax.all_to_all(pieces, ("section",) + GROUP, 0, 0, tiled=True))
    earlier = pl.pallas_call(
        first_weight_kernel,
        out_shape=jax.ShapeDtypeStruct((C, 384), jnp.float32),
        in_specs=[VMEM] * 5,
        out_specs=VMEM,
        compiler_params=PARAMS,
        cost_estimate=pl.CostEstimate(flops=500_000_000, bytes_accessed=4_000_000, transcendentals=0),
    )(*actives[0], arrived[0])
    shares = pl.pallas_call(
        weight_kernel,
        out_shape=jax.ShapeDtypeStruct((LANES, SHARE, 128), jnp.bfloat16),
        in_specs=[VMEM] * 6,
        out_specs=VMEM,
        scratch_shapes=[
            pltpu.VMEM((C, 128), jnp.float32),
            pltpu.VMEM((C, 128), jnp.float32),
            pltpu.VMEM((C, 128), jnp.float32),
            pltpu.VMEM((LANES * SHARE, 128), jnp.float32),
        ],
        compiler_params=PARAMS,
    )(*actives[1], arrived[1], earlier)
    shares = lax.all_to_all(shares, DP, 0, 0, tiled=True)
    gradient = pl.pallas_call(
        total_kernel,
        out_shape=jax.ShapeDtypeStruct((C // LANES, 1, C), jnp.float32),
        in_specs=[VMEM],
        out_specs=VMEM,
        scratch_shapes=[pltpu.VMEM((C // LANES, 128), jnp.float32)],
        compiler_params=PARAMS,
    )(shares)
    return (outs, jnp.transpose(gradient, (1, 0, 2)))


def solution(mesh):
    fine = Mesh(mesh.devices.reshape(2, 2, 2, 8, 2, 2), ("section",) + DP)
    return jax.shard_map(
        local,
        mesh=fine,
        in_specs=(
            P("section", None, DP, None),
            P("section", None, None),
            P("section", None),
            P(),
            P(),
        ),
        out_specs=(P("section", None, DP, None), P("section", DP, None)),
        check_vma=False,
    )
```

time: 117 us -> 111 us (0.949)
  blocking collectives: 0 us -> 43 us
  waiting for transfers between devices: 59.6 us -> 24.7 us
  starting transfers between devices: 30.9 us -> 16.3 us
  Pallas kernels: 13.8 us -> 19.9 us
  local copies, waits for them, and re-layouts: 10.1 us -> 5.08 us
    all_to_all x0 -> x1, blocking collectives: none -> 43 us  [local(): shares = lax.all_to_all(shares, DP, 0, 0, tiled=True)]
    all_to_all x1 -> x0, waiting for transfers between devices: 28.6 us -> none  [local(): shares = lax.all_to_all(shares, DP, 0, 0, tiled=True)]
    all_to_all x1 -> x0, starting transfers between devices: 13.7 us -> none  [local(): shares = lax.all_to_all(shares, DP, 0, 0, tiled=True)]
    ppermute x2, waiting for transfers between devices: 21.9 us -> 11.6 us  [local(): received = [lax.ppermute(rows, 'section', [(0, 1)]) for rows in sent]]
    pallas_call x4, Pallas kernels: 9.16 us -> 16.5 us  [the longest x2 11.5 us: local(): up(condition, received[number], inputs, weights, gains, sent[number], fir...]
    ppermute x6, waiting for transfers between devices: 5.95 us -> 11.2 us  [swap(): return lax.ppermute(block, axis, [(0, 1), (1, 0)])]
    unnamed x33 -> x18, local copies, waits for them, and re-layouts: 10.1 us -> 5.08 us
    pallas_call x1, Pallas kernels: 4.49 us -> 2.61 us  [local(): pl.pallas_call(weight_kernel, out_shape=jax.ShapeDtypeStruct((LANES, SHAR...]
  transfers between devices with their start and end apart: 11 -> 10, of which waited for: 5 -> 4; matrix products, arithmetic and copies ran while one was open for 1% -> 0% of each run, Pallas kernels for 4% -> 11%
where the time goes in v3:
time: 111 us; the launch traced here: 110 us
  blocking collectives  43 us (39%)
  waiting for transfers between devices  24.7 us (22%)
  Pallas kernels  19.9 us (18%)
  starting transfers between devices  16.3 us (15%)
  local copies, waits for them, and re-layouts  5.08 us (5%)
    all_to_all x1, blocking collectives, local(): shares = lax.all_to_all(shares, DP, 0, 0, tiled=True)  43 us
    ppermute x2, waiting for transfers between devices, local(): received = [lax.ppermute(rows, 'section', [(0, 1)]) for rows in sent]  11.6 us
    pallas_call x2, Pallas kernels, local(): up(condition, received[number], inputs, weights, gains, sent[number], fir...  11.5 us
    ppermute x6, waiting for transfers between devices, swap(): return lax.ppermute(block, axis, [(0, 1), (1, 0)])  11.2 us
    all_to_all x2, starting transfers between devices, local(): lax.all_to_all(pieces, ('section',) + GROUP, 0, 0, tiled=True)  10.9 us
    unnamed x18, local copies, waits for them, and re-layouts  5.08 us
    pallas_call x1, Pallas kernels, local(): pl.pallas_call(down_kernel, out_shape=(half,) * 4 + (jax.ShapeDtypeStruct...  4.13 us
    ppermute x6, starting transfers between devices, swap(): return lax.ppermute(block, axis, [(0, 1), (1, 0)])  2.78 us
  transfers between devices with their start and end apart: 10, of which 4 were waited for; matrix products, arithmetic and copies ran while one was open for 0% of the time, Pallas kernels for 11%

profile of v3, /device:TPU:6, one launch (start us, length us, event | category | flops | bytes accessed | tf_op | source)
XLA Modules:
  0.0 109.7 jit_solution(13252091562281487523)
XLA Ops:
  0.6 4.1 %shard_map.68 = (bf16[128,1280]{1,0:T(8,128)(2,1)}, bf16[128,1280]{1,0:T(8,128)(2,1)}, bf16[128,1280]{1,0:T(8,128)(2,1)}, bf16[128,1280]{1,0:T(8,128)(2,1)}, f32[2,1,1280]{2,1,0:T(1,128)}) custom-call(s32[2,16]{1,0:T(2,128)} %steps_hbm.1, bf16[1,2,128,1280]{3,2,1,0:T(8,128)(2,1)} %rows_hbm.5, bf16[1,1280,1280]{2,1,0:T(8,128)(2,1)} %weight_hbm.5, ...), custom_call_target="tpu_custom_call" | custom-call | tf_op jit(solution)/shard_map/pallas_call | solution.py:243
  4.8 1.3 %collective-permute-start.1 = (bf16[128,1280]{1,0:T(8,128)(2,1)}, bf16[128,1280]{1,0:T(8,128)(2,1)S(1)}, u32[]{:S(2)}, u32[]{:S(2)}) collective-permute-start(bf16[128,1280]{1,0:T(8,128)(2,1)} %get-tuple-element.16.sent_hbm), channel_id=1, source_target_pairs={{0,128},{1,129},{2,130},{3,131},{4,132},{5,133},{6,134},{7,135},{8... | collective-permute-start | bytes 983048 | tf_op jit(solution)/shard_map/ppermute | solution.py:259
  6.1 1.3 %collective-permute-start = (bf16[128,1280]{1,0:T(8,128)(2,1)}, bf16[128,1280]{1,0:T(8,128)(2,1)S(1)}, u32[]{:S(2)}, u32[]{:S(2)}) collective-permute-start(bf16[128,1280]{1,0:T(8,128)(2,1)} %get-tuple-element.14.sent_hbm), channel_id=1, source_target_pairs={{0,128},{1,129},{2,130},{3,131},{4,132},{5,133},{6,134},{7,135},{8... | collective-permute-start | bytes 983048 | tf_op jit(solution)/shard_map/ppermute | solution.py:259
  7.4 11.6 %collective-permute-done.1.arrived_ref = bf16[128,1280]{1,0:T(8,128)(2,1)S(1)} collective-permute-done((bf16[128,1280]{1,0:T(8,128)(2,1)}, bf16[128,1280]{1,0:T(8,128)(2,1)S(1)}, u32[]{:S(2)}, u32[]{:S(2)}) %collective-permute-start.1) | collective-permute-done | bytes 327712 | tf_op jit(solution)/shard_map/ppermute | solution.py:259
  19.0 0.7 copy-done.7
  19.7 5.3 %shard_map.69 = (bf16[1,2,128,1280]{3,2,1,0:T(8,128)(2,1)}, bf16[128,1280]{1,0:T(8,128)(2,1)S(1)}, bf16[8,320,128]{2,1,0:T(8,128)(2,1)}) custom-call(f32[2,1,1280]{2,1,0:T(1,128)S(1)} %copy-done.7, bf16[128,1280]{1,0:T(8,128)(2,1)S(1)} %collective-permute-done.1.arrived_ref, bf16[1,2,128,1280]{3,2,1,0:T(8,128)(2,1)} %rows_hbm.5, ...), custom_call_target="tpu_custom_call" | custom-call | flops 2000000000 | bytes 4000000 | tf_op jit(solution)/shard_map/pallas_call | solution.py:285
  25.0 5.8 %all-to-all-start.1 = ((bf16[8,320,128]{2,1,0:T(8,128)(2,1)}), bf16[8,320,128]{2,1,0:T(8,128)(2,1)S(1)}, u32[]{:S(2)}, u32[]{:S(2)}) async-start(bf16[8,320,128]{2,1,0:T(8,128)(2,1)} %get-tuple-element.23), calls=%async_computation.1 | async-start | bytes 1310720 | tf_op jit(solution)/shard_map/all_to_all | solution.py:292
  30.9 1.5 %collective-permute-start.6 = (bf16[128,1280]{1,0:T(8,128)(2,1)S(1)}, bf16[128,1280]{1,0:T(8,128)(2,1)S(1)}, u32[]{:S(2)}, u32[]{:S(2)}) collective-permute-start(bf16[128,1280]{1,0:T(8,128)(2,1)S(1)} %get-tuple-element.22.own), channel_id=1, source_target_pairs={{0,32},{32,0},{1,33},{33,1},{2,34},{34,2},{3,35},{35,3},{4,36},{36... | collective-permute-start | bytes 983048 | tf_op jit(solution)/shard_map/ppermute | solution.py:238
  32.3 0.0 collective-permute-done.arrived_ref
  32.3 6.1 %shard_map.70 = (bf16[1,2,128,1280]{3,2,1,0:T(8,128)(2,1)}, bf16[128,1280]{1,0:T(8,128)(2,1)}, bf16[8,320,128]{2,1,0:T(8,128)(2,1)}) custom-call(f32[2,1,1280]{2,1,0:T(1,128)S(1)} %copy-done.8, bf16[128,1280]{1,0:T(8,128)(2,1)S(1)} %collective-permute-done.arrived_ref, bf16[1,2,128,1280]{3,2,1,0:T(8,128)(2,1)} %rows_hbm.5, ...), custom_call_target="tpu_custom_call", output_to_operand_aliasing={{0}: (7, {})} | custom-call | flops 2000000000 | bytes 4000000 | tf_op jit(solution)/shard_map/pallas_call | solution.py:285
  38.5 0.7 collective-permute-start.3
  39.1 1.9 %all-to-all-done.1.piece_ref = bf16[8,320,128]{2,1,0:T(8,128)(2,1)S(1)} async-done(((bf16[8,320,128]{2,1,0:T(8,128)(2,1)}), bf16[8,320,128]{2,1,0:T(8,128)(2,1)S(1)}, u32[]{:S(2)}, u32[]{:S(2)}) %all-to-all-start.1) | async-done | bytes 655392 | tf_op jit(solution)/shard_map/all_to_all | solution.py:292
  41.0 5.1 %all-to-all-start = ((bf16[8,320,128]{2,1,0:T(8,128)(2,1)}), bf16[8,320,128]{2,1,0:T(8,128)(2,1)S(1)}, u32[]{:S(2)}, u32[]{:S(2)}) async-start(bf16[8,320,128]{2,1,0:T(8,128)(2,1)} %get-tuple-element.21), calls=%async_computation | async-start | bytes 1310720 | tf_op jit(solution)/shard_map/all_to_all | solution.py:292
  46.1 0.1 collective-permute-start.5
  46.2 1.8 %collective-permute-done.6.far = bf16[128,1280]{1,0:T(8,128)(2,1)S(1)} collective-permute-done((bf16[128,1280]{1,0:T(8,128)(2,1)S(1)}, bf16[128,1280]{1,0:T(8,128)(2,1)S(1)}, u32[]{:S(2)}, u32[]{:S(2)}) %collective-permute-start.6) | collective-permute-done | bytes 327712 | tf_op jit(solution)/shard_map/ppermute | solution.py:238
  48.1 0.0 collective-permute-start.7
  48.1 0.7 copy-done.4
  48.8 0.5 collective-permute-start.2
  49.3 9.4 %collective-permute-done.3.far = bf16[128,1280]{1,0:T(8,128)(2,1)} collective-permute-done((bf16[128,1280]{1,0:T(8,128)(2,1)}, bf16[128,1280]{1,0:T(8,128)(2,1)}, u32[]{:S(2)}, u32[]{:S(2)}) %collective-permute-start.3) | collective-permute-done | bytes 327712 | tf_op jit(solution)/shard_map/ppermute | solution.py:238
  58.7 0.0 collective-permute-start.4
  58.7 0.0 collective-permute-done.5.near
  58.7 0.0 collective-permute-done.7.far_core
  58.7 1.0 copy-done.3
  59.7 1.0 copy-done.5
  60.7 0.9 shard_map.71.earlier_ref
  61.5 0.0 collective-permute-done.2.near
  61.5 0.7 copy-done
  62.3 0.0 collective-permute-done.4.far_core
  62.3 1.0 copy-done.1
  63.3 2.6 %shard_map.72 = bf16[128,32,128]{2,1,0:T(8,128)(2,1)S(1)} custom-call(bf16[128,1280]{1,0:T(8,128)(2,1)} %get-tuple-element.20.own, bf16[128,1280]{1,0:T(8,128)(2,1)S(1)} %copy-done.1, bf16[128,1280]{1,0:T(8,128)(2,1)} %collective-permute-done.3.far, bf16[128,1280]{1,0:T(8,128)(2,1)} %collective-permute-done.4.far_core, ...), custom_call_target="tpu_custom_call" | custom-call | tf_op jit(solution)/shard_map/pallas_call | solution.py:301
  65.9 43.0 %all_to_all.15.shares_ref = bf16[128,32,128]{2,1,0:T(8,128)(2,1)S(1)} all-to-all(bf16[128,32,128]{2,1,0:T(8,128)(2,1)S(1)} %shard_map.72), channel_id=1, replica_groups=mesh['section'=2,'yh'=2,'yl'=2,'z'=8,'x'=2,'core'=2] {'yh','yl','z','x',..., dimensions={0} | all-to-all | bytes 2097152 | tf_op jit(solution)/shard_map/all_to_all | solution.py:314
  108.9 0.8 shard_map.73
  (13 shorter events, 0.0 us)
Async XLA Ops:
  0.6 18.4 %copy-start.6 = (f32[1,1280]{1,0:T(1,128)S(1)}, f32[1,1280]{1,0:T(1,128)}, u32[]{:S(2)}) copy-start(f32[1,1280]{1,0:T(1,128)} %gain_ref.3) | copy-start | bytes 15364
  4.8 14.2 %collective-permute-start.1 = (bf16[128,1280]{1,0:T(8,128)(2,1)}, bf16[128,1280]{1,0:T(8,128)(2,1)S(1)}, u32[]{:S(2)}, u32[]{:S(2)}) collective-permute-start(bf16[128,1280]{1,0:T(8,128)(2,1)} %get-tuple-element.16.sent_hbm), channel_id=1, source_target_pairs={{0,128},{1,129},{2,130},{3,131},{4,132},{5,133},{6,134},{7,135},{8... | collective-permute-start | bytes 983048 | tf_op jit(solution)/shard_map/ppermute | solution.py:259
  6.1 26.3 %collective-permute-start = (bf16[128,1280]{1,0:T(8,128)(2,1)}, bf16[128,1280]{1,0:T(8,128)(2,1)S(1)}, u32[]{:S(2)}, u32[]{:S(2)}) collective-permute-start(bf16[128,1280]{1,0:T(8,128)(2,1)} %get-tuple-element.14.sent_hbm), channel_id=1, source_target_pairs={{0,128},{1,129},{2,130},{3,131},{4,132},{5,133},{6,134},{7,135},{8... | collective-permute-start | bytes 983048 | tf_op jit(solution)/shard_map/ppermute | solution.py:259
  19.0 0.7 copy-start.7
  19.7 12.7 %copy-start.8 = (f32[2,1,1280]{2,1,0:T(1,128)S(1)}, f32[2,1,1280]{2,1,0:T(1,128)}, u32[]{:S(2)}) copy-start(f32[2,1,1280]{2,1,0:T(1,128)} %get-tuple-element.13.cond_ref) | copy-start | bytes 30724
  25.0 21.1 %copy-start.2 = (bf16[128,1280]{1,0:T(8,128)(2,1)}, bf16[128,1280]{1,0:T(8,128)(2,1)S(1)}, u32[]{:S(2)}) copy-start(bf16[128,1280]{1,0:T(8,128)(2,1)S(1)} %get-tuple-element.22.own) | copy-start | bytes 983044
  25.0 16.0 %all-to-all-start.1 = ((bf16[8,320,128]{2,1,0:T(8,128)(2,1)}), bf16[8,320,128]{2,1,0:T(8,128)(2,1)S(1)}, u32[]{:S(2)}, u32[]{:S(2)}) async-start(bf16[8,320,128]{2,1,0:T(8,128)(2,1)} %get-tuple-element.23), calls=%async_computation.1 | async-start | bytes 1310720 | tf_op jit(solution)/shard_map/all_to_all | solution.py:292
  30.9 17.2 %collective-permute-start.6 = (bf16[128,1280]{1,0:T(8,128)(2,1)S(1)}, bf16[128,1280]{1,0:T(8,128)(2,1)S(1)}, u32[]{:S(2)}, u32[]{:S(2)}) collective-permute-start(bf16[128,1280]{1,0:T(8,128)(2,1)S(1)} %get-tuple-element.22.own), channel_id=1, source_target_pairs={{0,32},{32,0},{1,33},{33,1},{2,34},{34,2},{3,35},{35,3},{4,36},{36... | collective-permute-start | bytes 983048 | tf_op jit(solution)/shard_map/ppermute | solution.py:238
  38.5 20.2 %collective-permute-start.3 = (bf16[128,1280]{1,0:T(8,128)(2,1)}, bf16[128,1280]{1,0:T(8,128)(2,1)}, u32[]{:S(2)}, u32[]{:S(2)}) collective-permute-start(bf16[128,1280]{1,0:T(8,128)(2,1)} %get-tuple-element.20.own), channel_id=1, source_target_pairs={{0,32},{32,0},{1,33},{33,1},{2,34},{34,2},{3,35},{35,3},{4,36},{36... | collective-permute-start | bytes 983048 | tf_op jit(solution)/shard_map/ppermute | solution.py:238
  41.0 21.2 %all-to-all-start = ((bf16[8,320,128]{2,1,0:T(8,128)(2,1)}), bf16[8,320,128]{2,1,0:T(8,128)(2,1)S(1)}, u32[]{:S(2)}, u32[]{:S(2)}) async-start(bf16[8,320,128]{2,1,0:T(8,128)(2,1)} %get-tuple-element.21), calls=%async_computation | async-start | bytes 1310720 | tf_op jit(solution)/shard_map/all_to_all | solution.py:292
  46.1 12.6 %collective-permute-start.5 = (bf16[128,1280]{1,0:T(8,128)(2,1)S(1)}, bf16[128,1280]{1,0:T(8,128)(2,1)S(1)}, u32[]{:S(2)}, u32[]{:S(2)}) collective-permute-start(bf16[128,1280]{1,0:T(8,128)(2,1)S(1)} %get-tuple-element.22.own), channel_id=1, source_target_pairs={{0,1},{1,0},{2,3},{3,2},{4,5},{5,4},{6,7},{7,6},{8,9},{9,8},{10,11... | collective-permute-start | bytes 983048 | tf_op jit(solution)/shard_map/ppermute | solution.py:238
  48.1 10.6 %collective-permute-start.7 = (bf16[128,1280]{1,0:T(8,128)(2,1)S(1)}, bf16[128,1280]{1,0:T(8,128)(2,1)S(1)}, u32[]{:S(2)}, u32[]{:S(2)}) collective-permute-start(bf16[128,1280]{1,0:T(8,128)(2,1)S(1)} %collective-permute-done.6.far), channel_id=1, source_target_pairs={{0,1},{1,0},{2,3},{3,2},{4,5},{5,4},{6,7},{7,6},{8,9},{9,8},{10,11... | collective-permute-start | bytes 983048 | tf_op jit(solution)/shard_map/ppermute | solution.py:238
  48.1 0.7 copy-start.4
  48.8 12.7 %collective-permute-start.2 = (bf16[128,1280]{1,0:T(8,128)(2,1)}, bf16[128,1280]{1,0:T(8,128)(2,1)S(1)}, u32[]{:S(2)}, u32[]{:S(2)}) collective-permute-start(bf16[128,1280]{1,0:T(8,128)(2,1)} %get-tuple-element.20.own), channel_id=1, source_target_pairs={{0,1},{1,0},{2,3},{3,2},{4,5},{5,4},{6,7},{7,6},{8,9},{9,8},{10,11... | collective-permute-start | bytes 983048 | tf_op jit(solution)/shard_map/ppermute | solution.py:238
  58.7 3.6 %collective-permute-start.4 = (bf16[128,1280]{1,0:T(8,128)(2,1)}, bf16[128,1280]{1,0:T(8,128)(2,1)}, u32[]{:S(2)}, u32[]{:S(2)}) collective-permute-start(bf16[128,1280]{1,0:T(8,128)(2,1)} %collective-permute-done.3.far), channel_id=1, source_target_pairs={{0,1},{1,0},{2,3},{3,2},{4,5},{5,4},{6,7},{7,6},{8,9},{9,8},{10,11... | collective-permute-start | bytes 983048 | tf_op jit(solution)/shard_map/ppermute | solution.py:238
  58.7 1.0 copy-start.3
  59.7 1.0 copy-start.5
  61.5 0.7 copy-start
  62.3 1.0 copy-start.1

commit v4 on v2

v4 whole, which is shorter than its diff:
```python
import functools
import math

import jax
import jax.numpy as jnp
from jax import lax
from jax.experimental import pallas as pl
from jax.experimental.pallas import tpu as pltpu
from jax.sharding import Mesh, PartitionSpec as P

PIX = 1024
MICRO = 2
ROWS = 128
LANES = 128
C = 1280
DP = ("y", "z", "x", "core")
PIECE = 320
SHARE = 16
TAIL = C + 8
PARAMS = pltpu.CompilerParams(vmem_limit_bytes=40 * 1024 * 1024)
WHOLE = pltpu.CompilerParams(vmem_limit_bytes=52 * 1024 * 1024)
MOST = pltpu.CompilerParams(vmem_limit_bytes=51 * 1024 * 1024)
VMEM = pl.BlockSpec(memory_space=pltpu.VMEM)
HBM = pl.BlockSpec(memory_space=pltpu.HBM)


def condition_row(steps_ref, text_ref, number):
    latent = lax.axis_index(DP) * ROWS // PIX
    step = steps_ref[number, latent].astype(jnp.float32)
    lane = lax.broadcasted_iota(jnp.int32, (1, C), 1)
    index = jnp.where(lane < C // 2, lane, lane - C // 2).astype(jnp.float32)
    angle = step * jnp.exp(-math.log(10000.0) * index / (C // 2))
    waves = jnp.where(lane < C // 2, jnp.cos(angle), jnp.sin(angle))
    text = text_ref[number].astype(jnp.float32)
    mine = lax.broadcasted_iota(jnp.int32, text.shape, 0) == latent
    return waves + jnp.sum(jnp.where(mine, text, 0.0), axis=0, keepdims=True)


def normed_rows(hidden, condition, gain):
    shifted = hidden + condition
    inverse = lax.rsqrt(jnp.mean(shifted * shifted, axis=-1, keepdims=True) + 1e-05)
    normed = shifted * inverse * gain
    sigma = 1.0 / (1.0 + jnp.exp(-normed))
    return shifted, inverse, normed, sigma


def down_kernel(
    steps_hbm, rows_hbm, weight_hbm, gain_hbm, text_hbm,
    sent_0, sent_1, active_0, active_1, cond_ref, weight_ref,
    steps_ref, rows_ref, gain_ref, text_ref, sems,
):
    copies = [
        pltpu.make_async_copy(source, target, sems.at[at])
        for at, (source, target) in enumerate(
            (
                (steps_hbm, steps_ref),
                (text_hbm, text_ref),
                (rows_hbm.at[0], rows_ref),
                (gain_hbm, gain_ref),
                (weight_hbm.at[0], weight_ref),
            )
        )
    ]
    for copy in copies:
        copy.start()
    copies[0].wait()
    copies[1].wait()
    for number in range(MICRO):
        cond_ref[number] = condition_row(steps_ref, text_ref, number)
    copies[2].wait()
    copies[3].wait()
    for number, sent_ref, active_ref in ((0, sent_0, active_0), (1, sent_1, active_1)):
        hidden = rows_ref[number].astype(jnp.float32)
        _, _, normed, sigma = normed_rows(hidden, cond_ref[number], gain_ref[...])
        active = (normed * sigma).astype(jnp.bfloat16)
        active_ref[...] = active
        if number == 0:
            copies[4].wait()
        result = hidden + jnp.dot(active, weight_ref[...], preferred_element_type=jnp.float32)
        sent_ref[...] = result.astype(jnp.bfloat16)


def store_pieces(pieces_ref, first, values):
    half = ROWS // 2
    low = lax.broadcasted_iota(jnp.int32, (half, 128), 1) < 64
    rounded = values.astype(jnp.bfloat16)
    y = lax.axis_index("y")
    for quarter in range(4):
        slot = first + lax.rem(quarter + 4 - y, 4)
        pieces_ref[slot, :ROWS] = rounded[:, 256 * quarter : 256 * quarter + 128]
        pieces_ref[slot, ROWS : 2 * ROWS] = rounded[:, 256 * quarter + 128 : 256 * quarter + 256]
        at = 1024 + 128 * (quarter // 2)
        block = values[:, at : at + 128]
        turned = pltpu.roll(block, 64, 1)
        top, bottom = (block, turned) if quarter % 2 == 0 else (turned, block)
        pieces_ref[slot, 2 * ROWS :] = jnp.where(low, top[:half], bottom[half:]).astype(
            jnp.bfloat16
        )


def up_kernel(number, *refs):
    cond_ref, arrived_ref, rows_hbm, weight_ref, gain_ref, sent_hbm, first_active_hbm = refs[:7]
    before = refs[7 : 7 + 9 * number]
    outs_hbm, active_hbm, *send_refs = refs[7 + 9 * number : 17 + 9 * number]
    out_ref, active_ref, pieces_ref, rows_ref, sems = refs[17 + 9 * number :]
    rows_copy = pltpu.make_async_copy(rows_hbm.at[0, number], rows_ref, sems.at[0])
    rows_copy.start()
    down = lax.axis_index("section") == 0
    kept = [
        pltpu.make_async_copy(sent_hbm, outs_hbm.at[0, number], sems.at[1]),
        pltpu.make_async_copy(first_active_hbm, active_hbm, sems.at[2]),
    ]
    made = [
        pltpu.make_async_copy(out_ref, outs_hbm.at[0, number], sems.at[1]),
        pltpu.make_async_copy(active_ref, active_hbm, sems.at[2]),
    ]

    @pl.when(down)
    def _():
        for copy in kept:
            copy.start()

    gain = gain_ref[...]
    hidden = arrived_ref[...].astype(jnp.float32)
    shifted, inverse, normed, sigma = normed_rows(hidden, cond_ref[number], gain)
    active = (normed * sigma).astype(jnp.bfloat16)
    active_ref[...] = active
    weight = weight_ref[...]
    upper = hidden + jnp.dot(active, weight, preferred_element_type=jnp.float32)
    out_ref[...] = upper.astype(jnp.bfloat16)

    @pl.when(jnp.logical_not(down))
    def _():
        for copy in made:
            copy.start()

    rows_copy.wait()
    cot = (upper - rows_ref[...].astype(jnp.float32)) / math.sqrt(MICRO * ROWS * LANES)
    store_pieces(pieces_ref, 4, cot)
    cot = cot.astype(jnp.bfloat16)
    through = lax.dot_general(
        cot, weight, (((1,), (1,)), ((), ())), preferred_element_type=jnp.float32
    )
    scaled = through * sigma * (1.0 + normed * (1.0 - sigma)) * gain
    inner = jnp.mean(scaled * shifted, axis=-1, keepdims=True)
    back = cot.astype(jnp.float32) + inverse * scaled - shifted * inverse**3 * inner
    store_pieces(pieces_ref, 0, back)
    for slot in range(8):
        if number:
            send_refs[slot][:PIECE] = before[1 + slot][...]
        send_refs[slot][PIECE * number :] = pieces_ref[slot]

    @pl.when(down)
    def _():
        for copy in kept:
            copy.wait()

    @pl.when(jnp.logical_not(down))
    def _():
        for copy in made:
            copy.wait()


def pack(main, tail, staged):
    group = lax.broadcasted_iota(jnp.int32, (3, 128), 1) // 32
    staged[...] = jnp.zeros_like(staged)

    def lanes(block, carry):
        base = pl.multiple_of(block * 80, 80)
        to = pl.multiple_of(block * 8 * SHARE, 8 * SHARE)
        for lane in range(8):
            at, put = base + 10 * lane, to + SHARE * lane
            staged[pl.ds(put, 10)] = main[pl.ds(at, 10)]
            row = tail[pl.ds(at, 3, 4)]
            for q in range(1, 4):
                row = jnp.where(group == q, tail[pl.ds(at + q, 3, 4)], row)
            staged[pl.ds(put + 10, 3)] = row
        return carry

    lax.fori_loop(0, LANES // 8, lanes, 0)


def weight_kernel(*refs):
    active_refs, back_refs, cot_refs = refs[:8], refs[8:12], refs[12:16]
    main_ref, tail_ref, away_ref, main, tail, staged = refs[16:]
    down, core = lax.axis_index("section") == 0, lax.axis_index("core")
    low = lax.broadcasted_iota(jnp.int32, (ROWS // 2, 128), 1) < 64
    zero = jnp.zeros((ROWS // 2, 128), jnp.bfloat16)
    product = None
    for offset in range(4):
        turn = (4 - offset) % 4
        rows, right = [], []
        for number in range(MICRO):
            rows.append(active_refs[number * 4 + offset][...])
            mine = pl.ds(PIECE * number, PIECE)
            piece = jnp.where(down, back_refs[turn][mine], cot_refs[turn][mine])
            end = piece[2 * ROWS :]
            right.append(
                jnp.concatenate(
                    [
                        piece[:ROWS],
                        piece[ROWS : 2 * ROWS],
                        jnp.concatenate([jnp.where(low, end, zero), jnp.where(low, zero, end)]),
                    ],
                    axis=1,
                )
            )
        term = lax.dot_general(
            jnp.concatenate(rows), jnp.concatenate(right), (((0,), (0,)), ((), ())),
            preferred_element_type=jnp.float32,
        )
        product = term if product is None else product + term
    first, second = product[:, :128], product[:, 128:256]
    both = product[:, 256:] + pltpu.roll(product[:, 256:], 64, 1)
    turned = pltpu.roll(both, 32, 1)
    even = (lax.broadcasted_iota(jnp.int32, both.shape, 1) // 32) % 2 == 0
    lower, upper = jnp.where(even, both, turned), jnp.where(even, turned, both)
    zeroth = core == 0
    main_ref[...] = jnp.where(zeroth, first, second)
    tail_ref[...] = jnp.where(zeroth, lower, upper)
    main[...] = jnp.where(zeroth, second, first)
    tail[:C] = jnp.where(zeroth, upper, lower)
    tail[C:] = jnp.zeros((TAIL - C, 128), jnp.float32)
    pack(main, tail, staged)
    away_ref[...] = staged[...].astype(jnp.bfloat16).reshape(LANES, SHARE, 128)


def pair_kernel(main_ref, tail_ref, other_ref, shares_ref, main, tail, staged):
    main[...] = main_ref[...]
    tail[:C] = tail_ref[...]
    tail[C:] = jnp.zeros((TAIL - C, 128), jnp.float32)
    pack(main, tail, staged)
    total = staged[...].reshape(LANES, SHARE, 128) + other_ref[...].astype(jnp.float32)
    shares_ref[...] = total.astype(jnp.bfloat16)


def total_kernel(shares_ref, gradient_ref, tail):
    group = lax.broadcasted_iota(jnp.int32, (3, 128), 1) // 32
    ends = []
    for y in range(4):
        for core in range(2):
            acc = None
            for zx in range(16):
                term = shares_ref[(y * 16 + zx) * 2 + core].astype(jnp.float32)
                acc = term if acc is None else acc + term
            at = 128 * (2 * y + core)
            gradient_ref[:, 0, at : at + 128] = acc[:10]
            ends.append(acc[10:13])
    for block in range(2):
        for q in range(4):
            row = None
            for g in range(4):
                end = ends[4 * block + g]
                end = end if g == q else pltpu.roll(end, (32 * (g - q)) % 128, 1)
                row = end if row is None else jnp.where(group == g, end, row)
            tail[pl.ds(q, 3, 4)] = row
        at = 1024 + 128 * block
        gradient_ref[:, 0, at : at + 128] = tail[:10]


def from_y(block, distance):
    return lax.ppermute(block, "y", [((i + distance) % 4, i) for i in range(4)])


def local(inputs, weights, gains, timesteps, text_pooled):
    half = jax.ShapeDtypeStruct((ROWS, C), jnp.bfloat16)
    whole = jax.ShapeDtypeStruct(inputs.shape, jnp.bfloat16)
    sent_0, sent_1, active_0, active_1, condition, weight = pl.pallas_call(
        down_kernel,
        out_shape=(half,) * 4
        + (
            jax.ShapeDtypeStruct((MICRO, 1, C), jnp.float32),
            jax.ShapeDtypeStruct((C, C), jnp.bfloat16),
        ),
        in_specs=[HBM] * 5,
        out_specs=(VMEM,) * 6,
        scratch_shapes=[
            pltpu.SMEM(timesteps.shape, jnp.int32),
            pltpu.VMEM(inputs.shape[1:], jnp.bfloat16),
            pltpu.VMEM(gains.shape, jnp.float32),
            pltpu.VMEM(text_pooled.shape, jnp.bfloat16),
            pltpu.SemaphoreType.DMA((5,)),
        ],
        compiler_params=WHOLE,
    )(timesteps, inputs, weights, gains, text_pooled)
    sent, first_active = (sent_0, sent_1), (active_0, active_1)
    received = [lax.ppermute(rows, "section", [(0, 1)]) for rows in sent]
    outs, pieces, actives = None, [], []
    for number in range(MICRO):
        piece = jax.ShapeDtypeStruct(((number + 1) * PIECE, 128), jnp.bfloat16)
        outs, active, *pieces = pl.pallas_call(
            functools.partial(up_kernel, number),
            out_shape=(whole, half) + (piece,) * 8,
            in_specs=[VMEM, VMEM, HBM, VMEM, VMEM, HBM, HBM] + ([HBM] + [VMEM] * 8) * number,
            out_specs=(HBM, HBM) + (VMEM,) * 8,
            scratch_shapes=[
                pltpu.VMEM((ROWS, C), jnp.bfloat16),
                pltpu.VMEM((ROWS, C), jnp.bfloat16),
                pltpu.VMEM((8, PIECE, 128), jnp.bfloat16),
                pltpu.VMEM((ROWS, C), jnp.bfloat16),
                pltpu.SemaphoreType.DMA((3,)),
            ],
            input_output_aliases={7: 0} if number else {},
            compiler_params=MOST,
            cost_estimate=pl.CostEstimate(
                flops=2_000_000_000, bytes_accessed=4_000_000, transcendentals=0
            ),
        )(
            condition, received[number], inputs, weight, gains, sent[number],
            first_active[number], *([outs, *pieces] if number else []),
        )
        ahead, behind = from_y(active, 1), from_y(active, -1)
        across = from_y(ahead, 1) if number == 0 else from_y(behind, -1)
        actives += [active, ahead, across, behind]
    returned = [
        lax.ppermute(pieces[r], ("section", "y"), [(4 + y, (y + r) % 4) for y in range(4)])
        for r in range(4)
    ]
    turned = [pieces[4]] + [
        lax.ppermute(pieces[4 + r], ("section", "y"), [(4 + y, 4 + (y + r) % 4) for y in range(4)])
        for r in range(1, 4)
    ]
    packed = [
        pltpu.VMEM((C, 128), jnp.float32),
        pltpu.VMEM((TAIL, 128), jnp.float32),
        pltpu.VMEM((LANES * SHARE, 128), jnp.float32),
    ]
    share = jax.ShapeDtypeStruct((LANES, SHARE, 128), jnp.bfloat16)
    main, tail, away = pl.pallas_call(
        weight_kernel,
        out_shape=(jax.ShapeDtypeStruct((C, 128), jnp.float32),) * 2 + (share,),
        in_specs=[VMEM] * 16,
        out_specs=(VMEM,) * 3,
        scratch_shapes=packed,
        compiler_params=PARAMS,
    )(*actives, *returned, *turned)
    other = lax.ppermute(away, "core", [(0, 1), (1, 0)])
    shares = pl.pallas_call(
        pair_kernel,
        out_shape=share,
        in_specs=[VMEM] * 3,
        out_specs=VMEM,
        scratch_shapes=packed,
        compiler_params=PARAMS,
    )(main, tail, other)
    shares = lax.all_to_all(shares, DP, 0, 0, tiled=True)
    gradient = pl.pallas_call(
        total_kernel,
        out_shape=jax.ShapeDtypeStruct((C // LANES, 1, C), jnp.float32),
        in_specs=[VMEM],
        out_specs=VMEM,
        scratch_shapes=[pltpu.VMEM((12, 128), jnp.float32)],
        compiler_params=PARAMS,
    )(shares)
    return (outs, jnp.transpose(gradient, (1, 0, 2)))


def solution(mesh):
    fine = Mesh(mesh.devices.reshape(2, 4, 8, 2, 2), ("section",) + DP)
    return jax.shard_map(
        local,
        mesh=fine,
        in_specs=(
            P("section", None, DP, None),
            P("section", None, None),
            P("section", None),
            P(),
            P(),
        ),
        out_specs=(P("section", None, DP, None), P("section", DP, None)),
        check_vma=False,
    )
```

time: 117 us -> 110 us (0.940)
  waiting for transfers between devices: 59.6 us -> 25.2 us
  blocking collectives: 0 us -> 32.2 us
  local copies, waits for them, and re-layouts: 10.1 us -> 3.02 us
  Pallas kernels: 13.8 us -> 16.5 us
    all_to_all x0 -> x1, blocking collectives: none -> 32.2 us  [local(): shares = lax.all_to_all(shares, DP, 0, 0, tiled=True)]
    all_to_all x3 -> x0, waiting for transfers between devices: 31.8 us -> none  [the longest x1 28.6 us: local(): shares = lax.all_to_all(shares, DP, 0, 0, tiled=True)]
    ppermute x8 -> x16, starting transfers between devices: 6.58 us -> 31.5 us  [the longest x4 11.1 us: local(): lax.ppermute(pieces[r], ('section', 'y'), [(4 + y, (y + r) % 4) for y in...]
    all_to_all x3 -> x0, starting transfers between devices: 24.3 us -> none  [the longest x1 13.7 us: local(): shares = lax.all_to_all(shares, DP, 0, 0, tiled=True)]
    unnamed x33 -> x12, local copies, waits for them, and re-layouts: 10.1 us -> 3.02 us
    ppermute x8 -> x16, waiting for transfers between devices: 27.8 us -> 25.2 us  [the longest x2 12.7 us: local(): received = [lax.ppermute(rows, 'section', [(0, 1)]) for rows in sent]]
    pallas_call x5, Pallas kernels: 13.6 us -> 15.7 us  [the longest x2 9.15 us: local(): pl.pallas_call(functools.partial(up_kernel, number), out_shape=(whole, ha...]
  transfers between devices with their start and end apart: 11 -> 16, of which waited for: 5 -> 5; matrix products, arithmetic and copies ran while one was open for 1% -> 0% of each run, Pallas kernels for 4% -> 4%
where the time goes in v4:
time: 110 us; the launch traced here: 109 us
  blocking collectives  32.2 us (29%)
  starting transfers between devices  31.5 us (29%)
  waiting for transfers between devices  25.2 us (23%)
  Pallas kernels  16.5 us (15%)
  local copies, waits for them, and re-layouts  3.02 us (3%)
    all_to_all x1, blocking collectives, local(): shares = lax.all_to_all(shares, DP, 0, 0, tiled=True)  32.2 us
    ppermute x2, waiting for transfers between devices, local(): received = [lax.ppermute(rows, 'section', [(0, 1)]) for rows in sent]  12.7 us
    ppermute x4, starting transfers between devices, local(): lax.ppermute(pieces[r], ('section', 'y'), [(4 + y, (y + r) % 4) for y in...  11.1 us
    ppermute x3, waiting for transfers between devices, local(): lax.ppermute(pieces[4 + r], ('section', 'y'), [(4 + y, 4 + (y + r) % 4) f...  10.6 us
    ppermute x3, starting transfers between devices, local(): lax.ppermute(pieces[4 + r], ('section', 'y'), [(4 + y, 4 + (y + r) % 4) f...  9.95 us
    pallas_call x2, Pallas kernels, local(): pl.pallas_call(functools.partial(up_kernel, number), out_shape=(whole, ha...  9.15 us
    ppermute x6, starting transfers between devices, from_y(): return lax.ppermute(block, 'y', [((i + distance) % 4, i) for i in range(4)])  7.84 us
    pallas_call x1, Pallas kernels, local(): pl.pallas_call(down_kernel, out_shape=(half,) * 4 + (jax.ShapeDtypeStruct...  3.94 us
  transfers between devices with their start and end apart: 16, of which 5 were waited for; matrix products, arithmetic and copies ran while one was open for 0% of the time, Pallas kernels for 4%

profile of v4, /device:TPU:6, one launch (start us, length us, event | category | flops | bytes accessed | tf_op | source)
XLA Modules:
  0.0 109.3 jit_solution(8967528053438519517)
XLA Ops:
  0.6 0.0 copy-start
  0.7 0.9 copy-done.1
  1.6 0.7 copy-done.2
  2.3 0.7 copy-done.4
  3.0 3.9 %shard_map.68 = (bf16[128,1280]{1,0:T(8,128)(2,1)S(1)}, bf16[128,1280]{1,0:T(8,128)(2,1)S(1)}, bf16[128,1280]{1,0:T(8,128)(2,1)S(1)}, bf16[128,1280]{1,0:T(8,128...) custom-call(s32[2,16]{1,0:T(2,128)S(1)} %copy-done.4, bf16[1,2,128,1280]{3,2,1,0:T(8,128)(2,1)} %refs_2_.3, ...), custom_call_target="tpu_custom_call" | custom-call | tf_op jit(solution)/shard_map/pallas_call | solution.py:268
  6.9 0.7 copy-done.5
  7.6 1.3 %collective-permute-start.1 = (bf16[128,1280]{1,0:T(8,128)(2,1)S(1)}, bf16[128,1280]{1,0:T(8,128)(2,1)S(1)}, u32[]{:S(2)}, u32[]{:S(2)}) collective-permute-start(bf16[128,1280]{1,0:T(8,128)(2,1)S(1)} %get-tuple-element.35.refs_5_), channel_id=1, source_target_pairs={{0,128},{1,129},{2,130},{3,131},{4,132},{5,133},{6,134},{7,135},{8... | collective-permute-start | bytes 983048 | tf_op jit(solution)/shard_map/ppermute | solution.py:287
  8.9 1.3 %collective-permute-start = (bf16[128,1280]{1,0:T(8,128)(2,1)S(1)}, bf16[128,1280]{1,0:T(8,128)(2,1)S(1)}, u32[]{:S(2)}, u32[]{:S(2)}) collective-permute-start(bf16[128,1280]{1,0:T(8,128)(2,1)S(1)} %get-tuple-element.32.refs_5_), channel_id=1, source_target_pairs={{0,128},{1,129},{2,130},{3,131},{4,132},{5,133},{6,134},{7,135},{8... | collective-permute-start | bytes 983048 | tf_op jit(solution)/shard_map/ppermute | solution.py:287
  10.2 11.4 %collective-permute-done.1.refs_1_ = bf16[128,1280]{1,0:T(8,128)(2,1)S(1)} collective-permute-done((bf16[128,1280]{1,0:T(8,128)(2,1)S(1)}, bf16[128,1280]{1,0:T(8,128)(2,1)S(1)}, u32[]{:S(2)}, u32[]{:S(2)}) %collective-permute-start.1) | collective-permute-done | bytes 327712 | tf_op jit(solution)/shard_map/ppermute | solution.py:287
  21.6 4.6 %shard_map.69 = (bf16[1,2,128,1280]{3,2,1,0:T(8,128)(2,1)}, bf16[128,1280]{1,0:T(8,128)(2,1)S(1)}, bf16[320,128]{1,0:T(8,128)(2,1)S(1)}, bf16[320,128]{1,0:T(8,1...) custom-call(f32[2,1,1280]{2,1,0:T(1,128)S(1)} %get-tuple-element.31., ...), custom_call_target="tpu_custom_call" | custom-call | flops 2000000000 | bytes 4000000 | tf_op jit(solution)/shard_map/pallas_call | solution.py:291
  26.2 1.3 %collective-permute-done.refs_1_ = bf16[128,1280]{1,0:T(8,128)(2,1)S(1)} collective-permute-done((bf16[128,1280]{1,0:T(8,128)(2,1)S(1)}, bf16[128,1280]{1,0:T(8,128)(2,1)S(1)}, u32[]{:S(2)}, u32[]{:S(2)}) %collective-permute-start) | collective-permute-done | bytes 327712 | tf_op jit(solution)/shard_map/ppermute | solution.py:287
  27.5 4.6 %shard_map.70 = (bf16[1,2,128,1280]{3,2,1,0:T(8,128)(2,1)}, bf16[128,1280]{1,0:T(8,128)(2,1)S(1)}, bf16[640,128]{1,0:T(8,128)(2,1)S(1)}, bf16[640,128]{1,0:T(8,1...) custom-call(f32[2,1,1280]{2,1,0:T(1,128)S(1)} %get-tuple-element.31., ...), custom_call_target="tpu_custom_call", output_to_operand_aliasing={{0}: (7, {})} | custom-call | flops 2000000000 | bytes 4000000 | tf_op jit(solution)/shard_map/pallas_call | solution.py:291
  32.1 1.5 %collective-permute-start.8 = (bf16[640,128]{1,0:T(8,128)(2,1)S(1)}, bf16[640,128]{1,0:T(8,128)(2,1)S(1)}, u32[]{:S(2)}, u32[]{:S(2)}) collective-permute-start(bf16[640,128]{1,0:T(8,128)(2,1)S(1)} %get-tuple-element.49), channel_id=1, source_target_pairs={{128,0},{160,32},{192,64},{224,96},{129,1},{161,33},{193,65},{225,... | collective-permute-start | bytes 491528 | tf_op jit(solution)/shard_map/ppermute | solution.py:316
  33.5 2.3 %collective-permute-start.9 = (bf16[640,128]{1,0:T(8,128)(2,1)S(1)}, bf16[640,128]{1,0:T(8,128)(2,1)S(1)}, u32[]{:S(2)}, u32[]{:S(2)}) collective-permute-start(bf16[640,128]{1,0:T(8,128)(2,1)S(1)} %get-tuple-element.50), channel_id=1, source_target_pairs={{128,32},{160,64},{192,96},{224,0},{129,33},{161,65},{193,97},{225... | collective-permute-start | bytes 491528 | tf_op jit(solution)/shard_map/ppermute | solution.py:316
  35.9 1.7 %collective-permute-start.6 = (bf16[128,1280]{1,0:T(8,128)(2,1)S(1)}, bf16[128,1280]{1,0:T(8,128)(2,1)S(1)}, u32[]{:S(2)}, u32[]{:S(2)}) collective-permute-start(bf16[128,1280]{1,0:T(8,128)(2,1)S(1)} %get-tuple-element.48.refs_4_), channel_id=1, source_target_pairs={{96,0},{0,32},{32,64},{64,96},{97,1},{1,33},{33,65},{65,97},{98,2}... | collective-permute-start | bytes 983048 | tf_op jit(solution)/shard_map/ppermute | solution.py:262
  37.5 1.7 %collective-permute-start.2 = (bf16[128,1280]{1,0:T(8,128)(2,1)S(1)}, bf16[128,1280]{1,0:T(8,128)(2,1)S(1)}, u32[]{:S(2)}, u32[]{:S(2)}) collective-permute-start(bf16[128,1280]{1,0:T(8,128)(2,1)S(1)} %get-tuple-element.47.refs_0_), channel_id=1, source_target_pairs={{32,0},{64,32},{96,64},{0,96},{33,1},{65,33},{97,65},{1,97},{34,2}... | collective-permute-start | bytes 983048 | tf_op jit(solution)/shard_map/ppermute | solution.py:262
  39.2 1.7 %collective-permute-start.10 = (bf16[640,128]{1,0:T(8,128)(2,1)S(1)}, bf16[640,128]{1,0:T(8,128)(2,1)S(1)}, u32[]{:S(2)}, u32[]{:S(2)}) collective-permute-start(bf16[640,128]{1,0:T(8,128)(2,1)S(1)} %get-tuple-element.51), channel_id=1, source_target_pairs={{128,64},{160,96},{192,0},{224,32},{129,65},{161,97},{193,1},{225,... | collective-permute-start | bytes 491528 | tf_op jit(solution)/shard_map/ppermute | solution.py:316
  40.9 0.0 collective-permute-done.8.refs_8_
  40.9 5.6 %collective-permute-start.11 = (bf16[640,128]{1,0:T(8,128)(2,1)S(1)}, bf16[640,128]{1,0:T(8,128)(2,1)S(1)}, u32[]{:S(2)}, u32[]{:S(2)}) collective-permute-start(bf16[640,128]{1,0:T(8,128)(2,1)S(1)} %get-tuple-element.52), channel_id=1, source_target_pairs={{128,96},{160,0},{192,32},{224,64},{129,97},{161,1},{193,33},{225,... | collective-permute-start | bytes 491528 | tf_op jit(solution)/shard_map/ppermute | solution.py:316
  46.5 1.9 %collective-permute-start.12 = (bf16[640,128]{1,0:T(8,128)(2,1)S(1)}, bf16[640,128]{1,0:T(8,128)(2,1)S(1)}, u32[]{:S(2)}, u32[]{:S(2)}) collective-permute-start(bf16[640,128]{1,0:T(8,128)(2,1)S(1)} %get-tuple-element.54), channel_id=1, source_target_pairs={{128,160},{160,192},{192,224},{224,128},{129,161},{161,193},{193,2... | collective-permute-start | bytes 491528 | tf_op jit(solution)/shard_map/ppermute | solution.py:320
  48.5 4.0 %collective-permute-start.13 = (bf16[640,128]{1,0:T(8,128)(2,1)S(1)}, bf16[640,128]{1,0:T(8,128)(2,1)S(1)}, u32[]{:S(2)}, u32[]{:S(2)}) collective-permute-start(bf16[640,128]{1,0:T(8,128)(2,1)S(1)} %get-tuple-element.55), channel_id=1, source_target_pairs={{128,192},{160,224},{192,128},{224,160},{129,193},{161,225},{193,1... | collective-permute-start | bytes 491528 | tf_op jit(solution)/shard_map/ppermute | solution.py:320
  52.5 1.2 %collective-permute-start.5 = (bf16[128,1280]{1,0:T(8,128)(2,1)S(1)}, bf16[128,1280]{1,0:T(8,128)(2,1)S(1)}, u32[]{:S(2)}, u32[]{:S(2)}) collective-permute-start(bf16[128,1280]{1,0:T(8,128)(2,1)S(1)} %get-tuple-element.48.refs_4_), channel_id=1, source_target_pairs={{32,0},{64,32},{96,64},{0,96},{33,1},{65,33},{97,65},{1,97},{34,2}... | collective-permute-start | bytes 983048 | tf_op jit(solution)/shard_map/ppermute | solution.py:262
  53.7 3.7 %collective-permute-done.12.refs_13_ = bf16[640,128]{1,0:T(8,128)(2,1)S(1)} collective-permute-done((bf16[640,128]{1,0:T(8,128)(2,1)S(1)}, bf16[640,128]{1,0:T(8,128)(2,1)S(1)}, u32[]{:S(2)}, u32[]{:S(2)}) %collective-permute-start.12) | collective-permute-done | bytes 163872 | tf_op jit(solution)/shard_map/ppermute | solution.py:320
  57.4 3.3 %collective-permute-start.3 = (bf16[128,1280]{1,0:T(8,128)(2,1)S(1)}, bf16[128,1280]{1,0:T(8,128)(2,1)S(1)}, u32[]{:S(2)}, u32[]{:S(2)}) collective-permute-start(bf16[128,1280]{1,0:T(8,128)(2,1)S(1)} %collective-permute-done.2.refs_1_), channel_id=1, source_target_pairs={{32,0},{64,32},{96,64},{0,96},{33,1},{65,33},{97,65},{1,97},{34,2}... | collective-permute-start | bytes 983048 | tf_op jit(solution)/shard_map/ppermute | solution.py:262
  60.7 4.0 %collective-permute-start.14 = (bf16[640,128]{1,0:T(8,128)(2,1)S(1)}, bf16[640,128]{1,0:T(8,128)(2,1)S(1)}, u32[]{:S(2)}, u32[]{:S(2)}) collective-permute-start(bf16[640,128]{1,0:T(8,128)(2,1)S(1)} %get-tuple-element.56), channel_id=1, source_target_pairs={{128,224},{160,128},{192,160},{224,192},{129,225},{161,129},{193,1... | collective-permute-start | bytes 491528 | tf_op jit(solution)/shard_map/ppermute | solution.py:320
  64.8 6.9 %collective-permute-done.14.refs_15_ = bf16[640,128]{1,0:T(8,128)(2,1)S(1)} collective-permute-done((bf16[640,128]{1,0:T(8,128)(2,1)S(1)}, bf16[640,128]{1,0:T(8,128)(2,1)S(1)}, u32[]{:S(2)}, u32[]{:S(2)}) %collective-permute-start.14) | collective-permute-done | bytes 163872 | tf_op jit(solution)/shard_map/ppermute | solution.py:320
  71.7 2.1 %shard_map.71 = (f32[1280,128]{1,0:T(8,128)S(1)}, f32[1280,128]{1,0:T(8,128)S(1)}, bf16[128,16,128]{2,1,0:T(8,128)(2,1)S(1)}) custom-call(bf16[128,1280]{1,0:T(8,128)(2,1)S(1)} %get-tuple-element.47.refs_0_, bf16[128,1280]{1,0:T(8,128)(2,1)S(1)} %collective-permute-done.2.refs_1_, bf16[128,1280]{1,0:T(8,128)(2,1)S(1)} %collective-permute-done.3.refs_2_, ...), custom_call_target="tpu_custom_call" | custom-call | tf_op jit(solution)/shard_map/pallas_call | solution.py:329
  73.8 0.1 collective-permute-start.15
  73.9 1.9 %collective-permute-done.15.other_ref = bf16[128,16,128]{2,1,0:T(8,128)(2,1)S(1)} collective-permute-done((bf16[128,16,128]{2,1,0:T(8,128)(2,1)S(1)}, bf16[128,16,128]{2,1,0:T(8,128)(2,1)S(1)}, u32[]{:S(2)}, u32[]{:S(2)}) %collective-permute-start.15) | collective-permute-done | bytes 524320 | tf_op jit(solution)/shard_map/ppermute | solution.py:337
  75.8 0.5 shard_map.72
  76.3 32.2 %all_to_all.5.shares_ref = bf16[128,16,128]{2,1,0:T(8,128)(2,1)S(1)} all-to-all(bf16[128,16,128]{2,1,0:T(8,128)(2,1)S(1)} %shard_map.72), channel_id=1, replica_groups=mesh['section'=2,'y'=4,'z'=8,'x'=2,'core'=2] {'y','z','x','core'}, dimensions={0} | all-to-all | bytes 1048576 | tf_op jit(solution)/shard_map/all_to_all | solution.py:346
  108.5 0.8 shard_map.73
  (19 shorter events, 0.0 us)
Async XLA Ops:
  0.6 21.0 %copy-start = (bf16[1,2,128,1280]{3,2,1,0:T(8,128)(2,1)S(1)}, bf16[1,2,128,1280]{3,2,1,0:T(8,128)(2,1)}, u32[]{:S(2)}) copy-start(bf16[1,2,128,1280]{3,2,1,0:T(8,128)(2,1)} %refs_2_.3) | copy-start | bytes 1966084
  0.6 1.0 copy-start.1
  1.6 0.7 copy-start.2
  2.3 0.7 copy-start.4
  3.0 18.6 %copy-start.3 = (f32[1,1280]{1,0:T(1,128)S(1)}, f32[1,1280]{1,0:T(1,128)}, u32[]{:S(2)}) copy-start(f32[1,1280]{1,0:T(1,128)} %refs_4_.3) | copy-start | bytes 15364
  6.9 0.7 copy-start.5
  7.6 14.0 %collective-permute-start.1 = (bf16[128,1280]{1,0:T(8,128)(2,1)S(1)}, bf16[128,1280]{1,0:T(8,128)(2,1)S(1)}, u32[]{:S(2)}, u32[]{:S(2)}) collective-permute-start(bf16[128,1280]{1,0:T(8,128)(2,1)S(1)} %get-tuple-element.35.refs_5_), channel_id=1, source_target_pairs={{0,128},{1,129},{2,130},{3,131},{4,132},{5,133},{6,134},{7,135},{8... | collective-permute-start | bytes 983048 | tf_op jit(solution)/shard_map/ppermute | solution.py:287
  8.9 18.6 %collective-permute-start = (bf16[128,1280]{1,0:T(8,128)(2,1)S(1)}, bf16[128,1280]{1,0:T(8,128)(2,1)S(1)}, u32[]{:S(2)}, u32[]{:S(2)}) collective-permute-start(bf16[128,1280]{1,0:T(8,128)(2,1)S(1)} %get-tuple-element.32.refs_5_), channel_id=1, source_target_pairs={{0,128},{1,129},{2,130},{3,131},{4,132},{5,133},{6,134},{7,135},{8... | collective-permute-start | bytes 983048 | tf_op jit(solution)/shard_map/ppermute | solution.py:287
  32.1 8.8 %collective-permute-start.8 = (bf16[640,128]{1,0:T(8,128)(2,1)S(1)}, bf16[640,128]{1,0:T(8,128)(2,1)S(1)}, u32[]{:S(2)}, u32[]{:S(2)}) collective-permute-start(bf16[640,128]{1,0:T(8,128)(2,1)S(1)} %get-tuple-element.49), channel_id=1, source_target_pairs={{128,0},{160,32},{192,64},{224,96},{129,1},{161,33},{193,65},{225,... | collective-permute-start | bytes 491528 | tf_op jit(solution)/shard_map/ppermute | solution.py:316
  33.5 13.0 %collective-permute-start.9 = (bf16[640,128]{1,0:T(8,128)(2,1)S(1)}, bf16[640,128]{1,0:T(8,128)(2,1)S(1)}, u32[]{:S(2)}, u32[]{:S(2)}) collective-permute-start(bf16[640,128]{1,0:T(8,128)(2,1)S(1)} %get-tuple-element.50), channel_id=1, source_target_pairs={{128,32},{160,64},{192,96},{224,0},{129,33},{161,65},{193,97},{225... | collective-permute-start | bytes 491528 | tf_op jit(solution)/shard_map/ppermute | solution.py:316
  35.9 21.6 %collective-permute-start.6 = (bf16[128,1280]{1,0:T(8,128)(2,1)S(1)}, bf16[128,1280]{1,0:T(8,128)(2,1)S(1)}, u32[]{:S(2)}, u32[]{:S(2)}) collective-permute-start(bf16[128,1280]{1,0:T(8,128)(2,1)S(1)} %get-tuple-element.48.refs_4_), channel_id=1, source_target_pairs={{96,0},{0,32},{32,64},{64,96},{97,1},{1,33},{33,65},{65,97},{98,2}... | collective-permute-start | bytes 983048 | tf_op jit(solution)/shard_map/ppermute | solution.py:262
  37.5 19.9 %collective-permute-start.2 = (bf16[128,1280]{1,0:T(8,128)(2,1)S(1)}, bf16[128,1280]{1,0:T(8,128)(2,1)S(1)}, u32[]{:S(2)}, u32[]{:S(2)}) collective-permute-start(bf16[128,1280]{1,0:T(8,128)(2,1)S(1)} %get-tuple-element.47.refs_0_), channel_id=1, source_target_pairs={{32,0},{64,32},{96,64},{0,96},{33,1},{65,33},{97,65},{1,97},{34,2}... | collective-permute-start | bytes 983048 | tf_op jit(solution)/shard_map/ppermute | solution.py:262
  39.2 9.3 %collective-permute-start.10 = (bf16[640,128]{1,0:T(8,128)(2,1)S(1)}, bf16[640,128]{1,0:T(8,128)(2,1)S(1)}, u32[]{:S(2)}, u32[]{:S(2)}) collective-permute-start(bf16[640,128]{1,0:T(8,128)(2,1)S(1)} %get-tuple-element.51), channel_id=1, source_target_pairs={{128,64},{160,96},{192,0},{224,32},{129,65},{161,97},{193,1},{225,... | collective-permute-start | bytes 491528 | tf_op jit(solution)/shard_map/ppermute | solution.py:316
  40.9 11.6 %collective-permute-start.11 = (bf16[640,128]{1,0:T(8,128)(2,1)S(1)}, bf16[640,128]{1,0:T(8,128)(2,1)S(1)}, u32[]{:S(2)}, u32[]{:S(2)}) collective-permute-start(bf16[640,128]{1,0:T(8,128)(2,1)S(1)} %get-tuple-element.52), channel_id=1, source_target_pairs={{128,96},{160,0},{192,32},{224,64},{129,97},{161,1},{193,33},{225,... | collective-permute-start | bytes 491528 | tf_op jit(solution)/shard_map/ppermute | solution.py:316
  46.5 10.9 %collective-permute-start.12 = (bf16[640,128]{1,0:T(8,128)(2,1)S(1)}, bf16[640,128]{1,0:T(8,128)(2,1)S(1)}, u32[]{:S(2)}, u32[]{:S(2)}) collective-permute-start(bf16[640,128]{1,0:T(8,128)(2,1)S(1)} %get-tuple-element.54), channel_id=1, source_target_pairs={{128,160},{160,192},{192,224},{224,128},{129,161},{161,193},{193,2... | collective-permute-start | bytes 491528 | tf_op jit(solution)/shard_map/ppermute | solution.py:320
  48.5 12.3 %collective-permute-start.13 = (bf16[640,128]{1,0:T(8,128)(2,1)S(1)}, bf16[640,128]{1,0:T(8,128)(2,1)S(1)}, u32[]{:S(2)}, u32[]{:S(2)}) collective-permute-start(bf16[640,128]{1,0:T(8,128)(2,1)S(1)} %get-tuple-element.55), channel_id=1, source_target_pairs={{128,192},{160,224},{192,128},{224,160},{129,193},{161,225},{193,1... | collective-permute-start | bytes 491528 | tf_op jit(solution)/shard_map/ppermute | solution.py:320
  52.5 19.2 %collective-permute-start.5 = (bf16[128,1280]{1,0:T(8,128)(2,1)S(1)}, bf16[128,1280]{1,0:T(8,128)(2,1)S(1)}, u32[]{:S(2)}, u32[]{:S(2)}) collective-permute-start(bf16[128,1280]{1,0:T(8,128)(2,1)S(1)} %get-tuple-element.48.refs_4_), channel_id=1, source_target_pairs={{32,0},{64,32},{96,64},{0,96},{33,1},{65,33},{97,65},{1,97},{34,2}... | collective-permute-start | bytes 983048 | tf_op jit(solution)/shard_map/ppermute | solution.py:262
  57.4 14.3 %collective-permute-start.4 = (bf16[128,1280]{1,0:T(8,128)(2,1)S(1)}, bf16[128,1280]{1,0:T(8,128)(2,1)S(1)}, u32[]{:S(2)}, u32[]{:S(2)}) collective-permute-start(bf16[128,1280]{1,0:T(8,128)(2,1)S(1)} %get-tuple-element.47.refs_0_), channel_id=1, source_target_pairs={{96,0},{0,32},{32,64},{64,96},{97,1},{1,33},{33,65},{65,97},{98,2}... | collective-permute-start | bytes 983048 | tf_op jit(solution)/shard_map/ppermute | solution.py:262
  57.4 14.3 %collective-permute-start.7 = (bf16[128,1280]{1,0:T(8,128)(2,1)S(1)}, bf16[128,1280]{1,0:T(8,128)(2,1)S(1)}, u32[]{:S(2)}, u32[]{:S(2)}) collective-permute-start(bf16[128,1280]{1,0:T(8,128)(2,1)S(1)} %collective-permute-done.6.refs_7_), channel_id=1, source_target_pairs={{96,0},{0,32},{32,64},{64,96},{97,1},{1,33},{33,65},{65,97},{98,2}... | collective-permute-start | bytes 983048 | tf_op jit(solution)/shard_map/ppermute | solution.py:262
  57.4 14.3 %collective-permute-start.3 = (bf16[128,1280]{1,0:T(8,128)(2,1)S(1)}, bf16[128,1280]{1,0:T(8,128)(2,1)S(1)}, u32[]{:S(2)}, u32[]{:S(2)}) collective-permute-start(bf16[128,1280]{1,0:T(8,128)(2,1)S(1)} %collective-permute-done.2.refs_1_), channel_id=1, source_target_pairs={{32,0},{64,32},{96,64},{0,96},{33,1},{65,33},{97,65},{1,97},{34,2}... | collective-permute-start | bytes 983048 | tf_op jit(solution)/shard_map/ppermute | solution.py:262
  60.7 11.0 %collective-permute-start.14 = (bf16[640,128]{1,0:T(8,128)(2,1)S(1)}, bf16[640,128]{1,0:T(8,128)(2,1)S(1)}, u32[]{:S(2)}, u32[]{:S(2)}) collective-permute-start(bf16[640,128]{1,0:T(8,128)(2,1)S(1)} %get-tuple-element.56), channel_id=1, source_target_pairs={{128,224},{160,128},{192,160},{224,192},{129,225},{161,129},{193,1... | collective-permute-start | bytes 491528 | tf_op jit(solution)/shard_map/ppermute | solution.py:320
  73.8 2.0 %collective-permute-start.15 = (bf16[128,16,128]{2,1,0:T(8,128)(2,1)S(1)}, bf16[128,16,128]{2,1,0:T(8,128)(2,1)S(1)}, u32[]{:S(2)}, u32[]{:S(2)}) collective-permute-start(bf16[128,16,128]{2,1,0:T(8,128)(2,1)S(1)} %get-tuple-element.59), channel_id=1, source_target_pairs={{0,1},{1,0},{2,3},{3,2},{4,5},{5,4},{6,7},{7,6},{8,9},{9,8},{10,11... | collective-permute-start | bytes 1572872 | tf_op jit(solution)/shard_map/ppermute | solution.py:337

commit v5 on v4

--- a/solution.py
+++ b/solution.py
@@ -14,6 +14,7 @@
 LANES = 128
 C = 1280
 DP = ("y", "z", "x", "core")
+COST = 50_000_000_000
 PIECE = 320
 SHARE = 16
 TAIL = C + 8
@@ -84,9 +85,8 @@
     half = ROWS // 2
     low = lax.broadcasted_iota(jnp.int32, (half, 128), 1) < 64
     rounded = values.astype(jnp.bfloat16)
-    y = lax.axis_index("y")
     for quarter in range(4):
-        slot = first + lax.rem(quarter + 4 - y, 4)
+        slot = first + quarter
         pieces_ref[slot, :ROWS] = rounded[:, 256 * quarter : 256 * quarter + 128]
         pieces_ref[slot, ROWS : 2 * ROWS] = rounded[:, 256 * quarter + 128 : 256 * quarter + 256]
         at = 1024 + 128 * (quarter // 2)
@@ -100,9 +100,9 @@
 
 def up_kernel(number, *refs):
     cond_ref, arrived_ref, rows_hbm, weight_ref, gain_ref, sent_hbm, first_active_hbm = refs[:7]
-    before = refs[7 : 7 + 9 * number]
-    outs_hbm, active_hbm, *send_refs = refs[7 + 9 * number : 17 + 9 * number]
-    out_ref, active_ref, pieces_ref, rows_ref, sems = refs[17 + 9 * number :]
+    outs_hbm, actives_hbm, pieces_hbm = refs[7 + 3 * number : 10 + 3 * number]
+    out_ref, active_ref, pieces_ref, rows_ref, sems = refs[10 + 3 * number :]
+    active_hbm = actives_hbm.at[pl.ds(ROWS * number, ROWS)]
     rows_copy = pltpu.make_async_copy(rows_hbm.at[0, number], rows_ref, sems.at[0])
     rows_copy.start()
     down = lax.axis_index("section") == 0
@@ -137,6 +137,14 @@
     rows_copy.wait()
     cot = (upper - rows_ref[...].astype(jnp.float32)) / math.sqrt(MICRO * ROWS * LANES)
     store_pieces(pieces_ref, 4, cot)
+    mine = pl.ds(PIECE * number, PIECE)
+    sends = [
+        pltpu.make_async_copy(
+            pieces_ref.at[pl.ds(at, 4)], pieces_hbm.at[pl.ds(at, 4), mine], sems.at[sem]
+        )
+        for at, sem in ((4, 3), (0, 4))
+    ]
+    sends[0].start()
     cot = cot.astype(jnp.bfloat16)
     through = lax.dot_general(
         cot, weight, (((1,), (1,)), ((), ())), preferred_element_type=jnp.float32
@@ -145,10 +153,9 @@
     inner = jnp.mean(scaled * shifted, axis=-1, keepdims=True)
     back = cot.astype(jnp.float32) + inverse * scaled - shifted * inverse**3 * inner
     store_pieces(pieces_ref, 0, back)
-    for slot in range(8):
-        if number:
-            send_refs[slot][:PIECE] = before[1 + slot][...]
-        send_refs[slot][PIECE * number :] = pieces_ref[slot]
+    sends[1].start()
+    for send in sends:
+        send.wait()
 
     @pl.when(down)
     def _():
@@ -180,20 +187,23 @@
     lax.fori_loop(0, LANES // 8, lanes, 0)
 
 
+def gathered_kernel(*refs):
+    refs[-1][...] = jnp.zeros_like(refs[-1])
+
+
 def weight_kernel(*refs):
-    active_refs, back_refs, cot_refs = refs[:8], refs[8:12], refs[12:16]
-    main_ref, tail_ref, away_ref, main, tail, staged = refs[16:]
-    down, core = lax.axis_index("section") == 0, lax.axis_index("core")
+    active_refs, piece_ref = refs[:4], refs[4]
+    main_ref, tail_ref, away_ref, main, tail, staged = refs[6:]
+    core = lax.axis_index("core")
+    own = 2 * lax.rem(lax.axis_index("y"), 2) + lax.rem(lax.axis_index("z"), 2)
     low = lax.broadcasted_iota(jnp.int32, (ROWS // 2, 128), 1) < 64
     zero = jnp.zeros((ROWS // 2, 128), jnp.bfloat16)
     product = None
-    for offset in range(4):
-        turn = (4 - offset) % 4
-        rows, right = [], []
+    for turn in range(4):
+        right = []
         for number in range(MICRO):
-            rows.append(active_refs[number * 4 + offset][...])
             mine = pl.ds(PIECE * number, PIECE)
-            piece = jnp.where(down, back_refs[turn][mine], cot_refs[turn][mine])
+            piece = piece_ref[4 + lax.bitwise_xor(own, turn), mine]
             end = piece[2 * ROWS :]
             right.append(
                 jnp.concatenate(
@@ -206,7 +216,7 @@
                 )
             )
         term = lax.dot_general(
-            jnp.concatenate(rows), jnp.concatenate(right), (((0,), (0,)), ((), ())),
+            active_refs[turn][...], jnp.concatenate(right), (((0,), (0,)), ((), ())),
             preferred_element_type=jnp.float32,
         )
         product = term if product is None else product + term
@@ -237,13 +247,15 @@
 def total_kernel(shares_ref, gradient_ref, tail):
     group = lax.broadcasted_iota(jnp.int32, (3, 128), 1) // 32
     ends = []
-    for y in range(4):
+    for quarter in range(4):
         for core in range(2):
             acc = None
-            for zx in range(16):
-                term = shares_ref[(y * 16 + zx) * 2 + core].astype(jnp.float32)
+            for k in range(16):
+                y, z, x = quarter // 2 + 2 * (k // 8), quarter % 2 + 2 * (k // 2 % 4), k % 2
+                lane = ((y * 8 + z) * 2 + x) * 2 + core
+                term = shares_ref[lane].astype(jnp.float32)
                 acc = term if acc is None else acc + term
-            at = 128 * (2 * y + core)
+            at = 128 * (2 * quarter + core)
             gradient_ref[:, 0, at : at + 128] = acc[:10]
             ends.append(acc[10:13])
     for block in range(2):
@@ -258,8 +270,36 @@
         gradient_ref[:, 0, at : at + 128] = tail[:10]
 
 
-def from_y(block, distance):
-    return lax.ppermute(block, "y", [((i + distance) % 4, i) for i in range(4)])
+def partner(y, z, core, t):
+    y = ((y + core) % 4 ^ 1) - core if t & 2 else y
+    z = ((z + core) % 8 ^ 1) - core if t & 1 else z
+    return ((y % 4) * 8 + z % 8) * 2 + core
+
+
+def squares():
+    groups = []
+    for x in range(2):
+        for core in range(2):
+            for y in range(0, 4, 2):
+                for z in range(0, 8, 2):
+                    group = []
+                    for section in range(2):
+                        for quarter in range(4):
+                            near = (y + core + (quarter // 2 + core) % 2) % 4
+                            side = (z + core + (quarter % 2 + core) % 2) % 8
+                            group.append((((section * 4 + near) * 8 + side) * 2 + x) * 2 + core)
+                    groups.append(group)
+    return groups
+
+
+def exchange(block, t, moves):
+    at = [(y, z, core) for y in range(4) for z in range(8) for core in range(2)]
+    route = [
+        (64 * source + partner(*place, 0), 64 * target + partner(*place, t))
+        for source, target in moves
+        for place in at
+    ]
+    return lax.ppermute(block, ("section", "y", "z", "core"), route)
 
 
 def local(inputs, weights, gains, timesteps, text_pooled):
@@ -285,55 +325,57 @@
     )(timesteps, inputs, weights, gains, text_pooled)
     sent, first_active = (sent_0, sent_1), (active_0, active_1)
     received = [lax.ppermute(rows, "section", [(0, 1)]) for rows in sent]
-    outs, pieces, actives = None, [], []
+    outs, actives, pieces = None, None, None
+    slots = jax.ShapeDtypeStruct((8, MICRO * PIECE, 128), jnp.bfloat16)
+    both = jax.ShapeDtypeStruct((MICRO * ROWS, C), jnp.bfloat16)
     for number in range(MICRO):
-        piece = jax.ShapeDtypeStruct(((number + 1) * PIECE, 128), jnp.bfloat16)
-        outs, active, *pieces = pl.pallas_call(
+        outs, actives, pieces = pl.pallas_call(
             functools.partial(up_kernel, number),
-            out_shape=(whole, half) + (piece,) * 8,
-            in_specs=[VMEM, VMEM, HBM, VMEM, VMEM, HBM, HBM] + ([HBM] + [VMEM] * 8) * number,
-            out_specs=(HBM, HBM) + (VMEM,) * 8,
+            out_shape=(whole, both, slots),
+            in_specs=[VMEM, VMEM, HBM, VMEM, VMEM, HBM, HBM] + [HBM] * (3 * number),
+            out_specs=(HBM,) * 3,
             scratch_shapes=[
                 pltpu.VMEM((ROWS, C), jnp.bfloat16),
                 pltpu.VMEM((ROWS, C), jnp.bfloat16),
                 pltpu.VMEM((8, PIECE, 128), jnp.bfloat16),
                 pltpu.VMEM((ROWS, C), jnp.bfloat16),
-                pltpu.SemaphoreType.DMA((3,)),
+                pltpu.SemaphoreType.DMA((5,)),
             ],
-            input_output_aliases={7: 0} if number else {},
+            input_output_aliases={7: 0, 8: 1, 9: 2} if number else {},
             compiler_params=MOST,
             cost_estimate=pl.CostEstimate(
                 flops=2_000_000_000, bytes_accessed=4_000_000, transcendentals=0
             ),
         )(
             condition, received[number], inputs, weight, gains, sent[number],
-            first_active[number], *([outs, *pieces] if number else []),
+            first_active[number], *([outs, actives, pieces] if number else []),
         )
-        ahead, behind = from_y(active, 1), from_y(active, -1)
-        across = from_y(ahead, 1) if number == 0 else from_y(behind, -1)
-        actives += [active, ahead, across, behind]
-    returned = [
-        lax.ppermute(pieces[r], ("section", "y"), [(4 + y, (y + r) % 4) for y in range(4)])
-        for r in range(4)
-    ]
-    turned = [pieces[4]] + [
-        lax.ppermute(pieces[4 + r], ("section", "y"), [(4 + y, 4 + (y + r) % 4) for y in range(4)])
-        for r in range(1, 4)
-    ]
+    others = [exchange(actives, t, ((0, 0), (1, 1))) for t in range(1, 4)]
+    arrived = lax.all_to_all(
+        pieces, ("section",) + DP, 0, 0, axis_index_groups=squares(), tiled=True
+    )
     packed = [
         pltpu.VMEM((C, 128), jnp.float32),
         pltpu.VMEM((TAIL, 128), jnp.float32),
         pltpu.VMEM((LANES * SHARE, 128), jnp.float32),
     ]
     share = jax.ShapeDtypeStruct((LANES, SHARE, 128), jnp.bfloat16)
+    gathered = pl.pallas_call(
+        gathered_kernel,
+        out_shape=jax.ShapeDtypeStruct((8, 128), jnp.float32),
+        in_specs=[HBM] * 3,
+        out_specs=VMEM,
+        compiler_params=PARAMS,
+        cost_estimate=pl.CostEstimate(flops=COST, bytes_accessed=2_000_000, transcendentals=0),
+    )(*others)
     main, tail, away = pl.pallas_call(
         weight_kernel,
         out_shape=(jax.ShapeDtypeStruct((C, 128), jnp.float32),) * 2 + (share,),
-        in_specs=[VMEM] * 16,
+        in_specs=[VMEM] * 5 + [HBM],
         out_specs=(VMEM,) * 3,
         scratch_shapes=packed,
         compiler_params=PARAMS,
-    )(*actives, *returned, *turned)
+    )(actives, *others, arrived, gathered)
     other = lax.ppermute(away, "core", [(0, 1), (1, 0)])
     shares = pl.pallas_call(
         pair_kernel,

time: 110 us -> 100 us (0.909)
  starting transfers between devices: 31.5 us -> 15.8 us
  waiting for transfers between devices: 25.2 us -> 29.5 us
  Pallas kernels: 16.5 us -> 19 us
    ppermute x13 -> x3, starting transfers between devices: 28.9 us -> 3.69 us  [exchange(): return lax.ppermute(block, ('section', 'y', 'z', 'core'), route)]
    all_to_all x0 -> x1, starting transfers between devices: none -> 7.06 us  [local(): lax.all_to_all(pieces, ('section',) + DP, 0, 0, axis_index_groups=squares...]
    all_to_all x0 -> x1, waiting for transfers between devices: none -> 6.35 us  [local(): lax.all_to_all(pieces, ('section',) + DP, 0, 0, axis_index_groups=squares...]
    ppermute x1, starting transfers between devices: 0.09 us -> 2.51 us  [local(): other = lax.ppermute(away, 'core', [(0, 1), (1, 0)])]
    pallas_call x2 -> x3, Pallas kernels: 9.15 us -> 10.6 us  [the longest x2 10.6 us: local(): pl.pallas_call(functools.partial(up_kernel, number), out_shape=(whole, bo...]
    ppermute x13 -> x3, waiting for transfers between devices: 10.6 us -> 9.62 us  [exchange(): return lax.ppermute(block, ('section', 'y', 'z', 'core'), route)]
    unnamed x12 -> x10, local copies, waits for them, and re-layouts: 3.02 us -> 2.32 us
  transfers between devices with their start and end apart: 16 -> 7, of which waited for: 5 -> 6; matrix products, arithmetic and copies ran while one was open for 0% -> 0% of each run, Pallas kernels for 4% -> 5%
where the time goes in v5:
time: 100 us; the launch traced here: 98.8 us
  blocking collectives  31.5 us (32%)
  waiting for transfers between devices  29.5 us (30%)
  Pallas kernels  19 us (19%)
  starting transfers between devices  15.8 us (16%)
  local copies, waits for them, and re-layouts  2.32 us (2%)
    all_to_all x1, blocking collectives, local(): shares = lax.all_to_all(shares, DP, 0, 0, tiled=True)  31.5 us
    ppermute x2, waiting for transfers between devices, local(): received = [lax.ppermute(rows, 'section', [(0, 1)]) for rows in sent]  12 us
    pallas_call x2, Pallas kernels, local(): pl.pallas_call(functools.partial(up_kernel, number), out_shape=(whole, bo...  10.6 us
    ppermute x3, waiting for transfers between devices, exchange(): return lax.ppermute(block, ('section', 'y', 'z', 'core'), route)  9.62 us
    all_to_all x1, starting transfers between devices, local(): lax.all_to_all(pieces, ('section',) + DP, 0, 0, axis_index_groups=squares...  7.06 us
    all_to_all x1, waiting for transfers between devices, local(): lax.all_to_all(pieces, ('section',) + DP, 0, 0, axis_index_groups=squares...  6.35 us
    pallas_call x1, Pallas kernels, local(): pl.pallas_call(down_kernel, out_shape=(half,) * 4 + (jax.ShapeDtypeStruct...  3.94 us
    ppermute x3, starting transfers between devices, exchange(): return lax.ppermute(block, ('section', 'y', 'z', 'core'), route)  3.69 us
  transfers between devices with their start and end apart: 7, of which 6 were waited for; matrix products, arithmetic and copies ran while one was open for 0% of the time, Pallas kernels for 5%

profile of v5, /device:TPU:6, one launch (start us, length us, event | category | flops | bytes accessed | tf_op | source)
XLA Modules:
  0.0 98.8 jit_solution(1708945756762657697)
XLA Ops:
  0.6 0.0 copy-start
  0.6 0.0 copy-start.1
  0.7 0.9 copy-done.1
  1.6 0.0 copy-start.2
  1.6 0.7 copy-done.2
  2.3 0.0 copy-start.4
  2.3 0.7 copy-done.4
  3.0 0.0 copy-start.3
  3.0 3.9 %shard_map.68 = (bf16[128,1280]{1,0:T(8,128)(2,1)S(1)}, bf16[128,1280]{1,0:T(8,128)(2,1)S(1)}, bf16[128,1280]{1,0:T(8,128)(2,1)S(1)}, bf16[128,1280]{1,0:T(8,128...) custom-call(s32[2,16]{1,0:T(2,128)S(1)} %copy-done.4, bf16[1,2,128,1280]{3,2,1,0:T(8,128)(2,1)} %refs_2_.3, ...), custom_call_target="tpu_custom_call" | custom-call | tf_op jit(solution)/shard_map/pallas_call | solution.py:308
  6.9 1.3 %collective-permute-start.1 = (bf16[128,1280]{1,0:T(8,128)(2,1)S(1)}, bf16[128,1280]{1,0:T(8,128)(2,1)S(1)}, u32[]{:S(2)}, u32[]{:S(2)}) collective-permute-start(bf16[128,1280]{1,0:T(8,128)(2,1)S(1)} %get-tuple-element.21.refs_5_), channel_id=1, source_target_pairs={{0,128},{1,129},{2,130},{3,131},{4,132},{5,133},{6,134},{7,135},{8... | collective-permute-start | bytes 983048 | tf_op jit(solution)/shard_map/ppermute | solution.py:327
  8.2 1.3 %collective-permute-start = (bf16[128,1280]{1,0:T(8,128)(2,1)S(1)}, bf16[128,1280]{1,0:T(8,128)(2,1)S(1)}, u32[]{:S(2)}, u32[]{:S(2)}) collective-permute-start(bf16[128,1280]{1,0:T(8,128)(2,1)S(1)} %get-tuple-element.18.refs_5_), channel_id=1, source_target_pairs={{0,128},{1,129},{2,130},{3,131},{4,132},{5,133},{6,134},{7,135},{8... | collective-permute-start | bytes 983048 | tf_op jit(solution)/shard_map/ppermute | solution.py:327
  9.5 11.4 %collective-permute-done.1.refs_1_ = bf16[128,1280]{1,0:T(8,128)(2,1)S(1)} collective-permute-done((bf16[128,1280]{1,0:T(8,128)(2,1)S(1)}, bf16[128,1280]{1,0:T(8,128)(2,1)S(1)}, u32[]{:S(2)}, u32[]{:S(2)}) %collective-permute-start.1) | collective-permute-done | bytes 327712 | tf_op jit(solution)/shard_map/ppermute | solution.py:327
  20.9 0.0 copy-done
  20.9 0.0 copy-done.3
  20.9 5.3 %shard_map.69 = (bf16[1,2,128,1280]{3,2,1,0:T(8,128)(2,1)}, bf16[256,1280]{1,0:T(8,128)(2,1)S(1)}, bf16[8,640,128]{2,1,0:T(8,128)(2,1)}) custom-call(f32[2,1,1280]{2,1,0:T(1,128)S(1)} %get-tuple-element.17.refs_0_, bf16[128,1280]{1,0:T(8,128)(2,1)S(1)} %collective-permute-done.1.refs_1_, bf16[1,2,128,1280]{3,2,1,0:T(8,128)(2,1)S(1)} %copy-done, ...), custom_call_target="tpu_custom_call" | custom-call | flops 2000000000 | bytes 4000000 | tf_op jit(solution)/shard_map/pallas_call | solution.py:332
  26.2 0.6 collective-permute-done.refs_1_
  26.8 5.3 %shard_map.70 = (bf16[1,2,128,1280]{3,2,1,0:T(8,128)(2,1)}, bf16[256,1280]{1,0:T(8,128)(2,1)S(1)}, bf16[8,640,128]{2,1,0:T(8,128)(2,1)}) custom-call(f32[2,1,1280]{2,1,0:T(1,128)S(1)} %get-tuple-element.17.refs_0_, bf16[128,1280]{1,0:T(8,128)(2,1)S(1)} %collective-permute-done.refs_1_, ...), custom_call_target="tpu_custom_call", output_to_operand_aliasing={{0}: (7, {}), {1}: (8, {}), {2}: (9, {})} | custom-call | flops 2000000000 | bytes 4000000 | tf_op jit(solution)/shard_map/pallas_call | solution.py:332
  32.1 3.0 %collective-permute-start.4 = (bf16[256,1280]{1,0:T(8,128)(2,1)S(1)}, bf16[256,1280]{1,0:T(8,128)(2,1)S(1)}, u32[]{:S(2)}, u32[]{:S(2)}) collective-permute-start(bf16[256,1280]{1,0:T(8,128)(2,1)S(1)} %get-tuple-element.27.refs_0_), channel_id=1, source_target_pairs={{0,36},{1,125},{4,32},{5,105},{8,44},{9,101},{12,40},{13,113},{16,... | collective-permute-start | bytes 1966088 | tf_op jit(solution)/shard_map/ppermute | solution.py:302
  35.1 0.4 collective-permute-start.3
  35.5 0.2 collective-permute-start.2
  35.8 7.1 %all-to-all-start = ((bf16[8,640,128]{2,1,0:T(8,128)(2,1)}), bf16[8,640,128]{2,1,0:T(8,128)(2,1)S(1)}, u32[]{:S(2)}, u32[]{:S(2)}) async-start(bf16[8,640,128]{2,1,0:T(8,128)(2,1)} %get-tuple-element.28), calls=%async_computation | async-start | bytes 2621440 | tf_op jit(solution)/shard_map/all_to_all | solution.py:354
  42.8 0.9 collective-permute-done.4.refs_2_.refs_3_
  43.8 8.7 %collective-permute-done.3.refs_1_.refs_2_ = bf16[256,1280]{1,0:T(8,128)(2,1)S(1)} collective-permute-done((bf16[256,1280]{1,0:T(8,128)(2,1)S(1)}, bf16[256,1280]{1,0:T(8,128)(2,1)S(1)}, u32[]{:S(2)}, u32[]{:S(2)}) %collective-permute-start.3) | collective-permute-done | bytes 655392 | tf_op jit(solution)/shard_map/ppermute | solution.py:302
  52.4 0.0 collective-permute-done.2.refs_0_.refs_1_
  52.4 6.3 %all-to-all-done.refs_4_ = bf16[8,640,128]{2,1,0:T(8,128)(2,1)S(1)} async-done(((bf16[8,640,128]{2,1,0:T(8,128)(2,1)}), bf16[8,640,128]{2,1,0:T(8,128)(2,1)S(1)}, u32[]{:S(2)}, u32[]{:S(2)}) %all-to-all-start) | async-done | bytes 1310752 | tf_op jit(solution)/shard_map/all_to_all | solution.py:354
  58.8 3.1 %shard_map.72 = (f32[1280,128]{1,0:T(8,128)S(1)}, f32[1280,128]{1,0:T(8,128)S(1)}, bf16[128,16,128]{2,1,0:T(8,128)(2,1)S(1)}) custom-call(bf16[256,1280]{1,0:T(8,128)(2,1)S(1)} %get-tuple-element.27.refs_0_, bf16[256,1280]{1,0:T(8,128)(2,1)} %collective-permute-done.2.refs_0_.refs_1_, bf16[256,1280]{1,0:T(8,128)(2,1)S(1)} %collective-permute-done.3.refs_1_.refs_2_, ...), custom_call_target="tpu_custom_call" | custom-call | tf_op jit(solution)/shard_map/pallas_call | solution.py:371
  62.0 2.5 %collective-permute-start.5 = (bf16[128,16,128]{2,1,0:T(8,128)(2,1)S(1)}, bf16[128,16,128]{2,1,0:T(8,128)(2,1)S(1)}, u32[]{:S(2)}, u32[]{:S(2)}) collective-permute-start(bf16[128,16,128]{2,1,0:T(8,128)(2,1)S(1)} %get-tuple-element.31), channel_id=1, source_target_pairs={{0,1},{1,0},{2,3},{3,2},{4,5},{5,4},{6,7},{7,6},{8,9},{9,8},{10,11... | collective-permute-start | bytes 1572872 | tf_op jit(solution)/shard_map/ppermute | solution.py:379
  64.5 1.5 %collective-permute-done.5.other_ref = bf16[128,16,128]{2,1,0:T(8,128)(2,1)S(1)} collective-permute-done((bf16[128,16,128]{2,1,0:T(8,128)(2,1)S(1)}, bf16[128,16,128]{2,1,0:T(8,128)(2,1)S(1)}, u32[]{:S(2)}, u32[]{:S(2)}) %collective-permute-start.5) | collective-permute-done | bytes 524320 | tf_op jit(solution)/shard_map/ppermute | solution.py:379
  66.0 0.5 shard_map.73
  66.5 31.5 %all_to_all.10.shares_ref = bf16[128,16,128]{2,1,0:T(8,128)(2,1)S(1)} all-to-all(bf16[128,16,128]{2,1,0:T(8,128)(2,1)S(1)} %shard_map.73), channel_id=1, replica_groups=mesh['section'=2,'y'=4,'z'=8,'x'=2,'core'=2] {'y','z','x','core'}, dimensions={0} | all-to-all | bytes 1048576 | tf_op jit(solution)/shard_map/all_to_all | solution.py:388
  98.0 0.8 shard_map.74
  (1 shorter events, 0.0 us)
Async XLA Ops:
  0.6 20.3 %copy-start = (bf16[1,2,128,1280]{3,2,1,0:T(8,128)(2,1)S(1)}, bf16[1,2,128,1280]{3,2,1,0:T(8,128)(2,1)}, u32[]{:S(2)}) copy-start(bf16[1,2,128,1280]{3,2,1,0:T(8,128)(2,1)} %refs_2_.3) | copy-start | bytes 1966084
  0.6 1.0 copy-start.1
  1.6 0.7 copy-start.2
  2.3 0.7 copy-start.4
  3.0 18.0 %copy-start.3 = (f32[1,1280]{1,0:T(1,128)S(1)}, f32[1,1280]{1,0:T(1,128)}, u32[]{:S(2)}) copy-start(f32[1,1280]{1,0:T(1,128)} %refs_4_.3) | copy-start | bytes 15364
  6.9 14.0 %collective-permute-start.1 = (bf16[128,1280]{1,0:T(8,128)(2,1)S(1)}, bf16[128,1280]{1,0:T(8,128)(2,1)S(1)}, u32[]{:S(2)}, u32[]{:S(2)}) collective-permute-start(bf16[128,1280]{1,0:T(8,128)(2,1)S(1)} %get-tuple-element.21.refs_5_), channel_id=1, source_target_pairs={{0,128},{1,129},{2,130},{3,131},{4,132},{5,133},{6,134},{7,135},{8... | collective-permute-start | bytes 983048 | tf_op jit(solution)/shard_map/ppermute | solution.py:327
  8.2 18.6 %collective-permute-start = (bf16[128,1280]{1,0:T(8,128)(2,1)S(1)}, bf16[128,1280]{1,0:T(8,128)(2,1)S(1)}, u32[]{:S(2)}, u32[]{:S(2)}) collective-permute-start(bf16[128,1280]{1,0:T(8,128)(2,1)S(1)} %get-tuple-element.18.refs_5_), channel_id=1, source_target_pairs={{0,128},{1,129},{2,130},{3,131},{4,132},{5,133},{6,134},{7,135},{8... | collective-permute-start | bytes 983048 | tf_op jit(solution)/shard_map/ppermute | solution.py:327
  32.1 11.7 %collective-permute-start.4 = (bf16[256,1280]{1,0:T(8,128)(2,1)S(1)}, bf16[256,1280]{1,0:T(8,128)(2,1)S(1)}, u32[]{:S(2)}, u32[]{:S(2)}) collective-permute-start(bf16[256,1280]{1,0:T(8,128)(2,1)S(1)} %get-tuple-element.27.refs_0_), channel_id=1, source_target_pairs={{0,36},{1,125},{4,32},{5,105},{8,44},{9,101},{12,40},{13,113},{16,... | collective-permute-start | bytes 1966088 | tf_op jit(solution)/shard_map/ppermute | solution.py:302
  35.1 17.3 %collective-permute-start.3 = (bf16[256,1280]{1,0:T(8,128)(2,1)S(1)}, bf16[256,1280]{1,0:T(8,128)(2,1)S(1)}, u32[]{:S(2)}, u32[]{:S(2)}) collective-permute-start(bf16[256,1280]{1,0:T(8,128)(2,1)S(1)} %get-tuple-element.27.refs_0_), channel_id=1, source_target_pairs={{0,32},{1,97},{4,36},{5,101},{8,40},{9,105},{12,44},{13,109},{16,4... | collective-permute-start | bytes 1966088 | tf_op jit(solution)/shard_map/ppermute | solution.py:302
  35.5 16.9 %collective-permute-start.2 = (bf16[256,1280]{1,0:T(8,128)(2,1)S(1)}, bf16[256,1280]{1,0:T(8,128)(2,1)}, u32[]{:S(2)}, u32[]{:S(2)}) collective-permute-start(bf16[256,1280]{1,0:T(8,128)(2,1)S(1)} %get-tuple-element.27.refs_0_), channel_id=1, source_target_pairs={{0,4},{1,29},{4,0},{5,9},{8,12},{9,5},{12,8},{13,17},{16,20},{17,1... | collective-permute-start | bytes 1966088 | tf_op jit(solution)/shard_map/ppermute | solution.py:302
  35.8 23.0 %all-to-all-start = ((bf16[8,640,128]{2,1,0:T(8,128)(2,1)}), bf16[8,640,128]{2,1,0:T(8,128)(2,1)S(1)}, u32[]{:S(2)}, u32[]{:S(2)}) async-start(bf16[8,640,128]{2,1,0:T(8,128)(2,1)} %get-tuple-element.28), calls=%async_computation | async-start | bytes 2621440 | tf_op jit(solution)/shard_map/all_to_all | solution.py:354
  62.0 4.0 %collective-permute-start.5 = (bf16[128,16,128]{2,1,0:T(8,128)(2,1)S(1)}, bf16[128,16,128]{2,1,0:T(8,128)(2,1)S(1)}, u32[]{:S(2)}, u32[]{:S(2)}) collective-permute-start(bf16[128,16,128]{2,1,0:T(8,128)(2,1)S(1)} %get-tuple-element.31), channel_id=1, source_target_pairs={{0,1},{1,0},{2,3},{3,2},{4,5},{5,4},{6,7},{7,6},{8,9},{9,8},{10,11... | collective-permute-start | bytes 1572872 | tf_op jit(solution)/shard_map/ppermute | solution.py:379

commit v6 on v5

--- a/solution.py
+++ b/solution.py
@@ -81,6 +81,10 @@
         sent_ref[...] = result.astype(jnp.bfloat16)
 
 
+def own_quarter():
+    return 2 * lax.rem(lax.axis_index("y"), 2) + lax.rem(lax.axis_index("z"), 2)
+
+
 def store_pieces(pieces_ref, first, values):
     half = ROWS // 2
     low = lax.broadcasted_iota(jnp.int32, (half, 128), 1) < 64
@@ -100,8 +104,8 @@
 
 def up_kernel(number, *refs):
     cond_ref, arrived_ref, rows_hbm, weight_ref, gain_ref, sent_hbm, first_active_hbm = refs[:7]
-    outs_hbm, actives_hbm, pieces_hbm = refs[7 + 3 * number : 10 + 3 * number]
-    out_ref, active_ref, pieces_ref, rows_ref, sems = refs[10 + 3 * number :]
+    outs_hbm, actives_hbm, *send_refs = refs[7 + 2 * number : -5]
+    out_ref, active_ref, pieces_ref, rows_ref, sems = refs[-5:]
     active_hbm = actives_hbm.at[pl.ds(ROWS * number, ROWS)]
     rows_copy = pltpu.make_async_copy(rows_hbm.at[0, number], rows_ref, sems.at[0])
     rows_copy.start()
@@ -136,15 +140,20 @@
 
     rows_copy.wait()
     cot = (upper - rows_ref[...].astype(jnp.float32)) / math.sqrt(MICRO * ROWS * LANES)
-    store_pieces(pieces_ref, 4, cot)
-    mine = pl.ds(PIECE * number, PIECE)
-    sends = [
-        pltpu.make_async_copy(
-            pieces_ref.at[pl.ds(at, 4)], pieces_hbm.at[pl.ds(at, 4), mine], sems.at[sem]
-        )
-        for at, sem in ((4, 3), (0, 4))
-    ]
-    sends[0].start()
+    if number:
+        store_pieces(pieces_ref, 4, cot)
+        sends = [
+            pltpu.make_async_copy(
+                pieces_ref.at[pl.ds(at, 4)], send_refs[0].at[pl.ds(at, 4)], sems.at[sem]
+            )
+            for at, sem in ((4, 3), (0, 4))
+        ]
+        sends[0].start()
+    else:
+        store_pieces(pieces_ref, 4, cot)
+        own = own_quarter()
+        for turn in range(4):
+            send_refs[turn][...] = pieces_ref[4 + lax.bitwise_xor(own, turn)]
     cot = cot.astype(jnp.bfloat16)
     through = lax.dot_general(
         cot, weight, (((1,), (1,)), ((), ())), preferred_element_type=jnp.float32
@@ -152,10 +161,13 @@
     scaled = through * sigma * (1.0 + normed * (1.0 - sigma)) * gain
     inner = jnp.mean(scaled * shifted, axis=-1, keepdims=True)
     back = cot.astype(jnp.float32) + inverse * scaled - shifted * inverse**3 * inner
-    store_pieces(pieces_ref, 0, back)
-    sends[1].start()
-    for send in sends:
-        send.wait()
+    if number:
+        store_pieces(pieces_ref, 0, back)
+        sends[1].start()
+        for send in sends:
+            send.wait()
+    else:
+        send_refs[4][...] = back.astype(jnp.bfloat16)
 
     @pl.when(down)
     def _():
@@ -187,23 +199,35 @@
     lax.fori_loop(0, LANES // 8, lanes, 0)
 
 
+def returned_kernel(rows_ref, pieces_in, pieces_hbm, pieces_ref, sem):
+    del pieces_in
+
+    @pl.when(lax.axis_index("section") == 0)
+    def _():
+        store_pieces(pieces_ref, 0, rows_ref[...].astype(jnp.float32))
+        copy = pltpu.make_async_copy(pieces_ref, pieces_hbm.at[pl.ds(0, 4)], sem)
+        copy.start()
+        copy.wait()
+
+
 def gathered_kernel(*refs):
     refs[-1][...] = jnp.zeros_like(refs[-1])
 
 
 def weight_kernel(*refs):
-    active_refs, piece_ref = refs[:4], refs[4]
-    main_ref, tail_ref, away_ref, main, tail, staged = refs[6:]
-    core = lax.axis_index("core")
-    own = 2 * lax.rem(lax.axis_index("y"), 2) + lax.rem(lax.axis_index("z"), 2)
+    active_refs, piece_ref, cot_refs = refs[:4], refs[4], refs[5:9]
+    main_ref, tail_ref, away_ref, main, tail, staged = refs[10:]
+    down, core = lax.axis_index("section") == 0, lax.axis_index("core")
+    own = own_quarter()
     low = lax.broadcasted_iota(jnp.int32, (ROWS // 2, 128), 1) < 64
     zero = jnp.zeros((ROWS // 2, 128), jnp.bfloat16)
     product = None
     for turn in range(4):
         right = []
         for number in range(MICRO):
-            mine = pl.ds(PIECE * number, PIECE)
-            piece = piece_ref[4 + lax.bitwise_xor(own, turn), mine]
+            piece = piece_ref[4 * number + lax.bitwise_xor(own, turn)]
+            if number == 0:
+                piece = jnp.where(down, piece, cot_refs[turn][...])
             end = piece[2 * ROWS :]
             right.append(
                 jnp.concatenate(
@@ -325,15 +349,16 @@
     )(timesteps, inputs, weights, gains, text_pooled)
     sent, first_active = (sent_0, sent_1), (active_0, active_1)
     received = [lax.ppermute(rows, "section", [(0, 1)]) for rows in sent]
-    outs, actives, pieces = None, None, None
-    slots = jax.ShapeDtypeStruct((8, MICRO * PIECE, 128), jnp.bfloat16)
     both = jax.ShapeDtypeStruct((MICRO * ROWS, C), jnp.bfloat16)
-    for number in range(MICRO):
-        outs, actives, pieces = pl.pallas_call(
+    piece = jax.ShapeDtypeStruct((PIECE, 128), jnp.bfloat16)
+    slots = jax.ShapeDtypeStruct((8, PIECE, 128), jnp.bfloat16)
+
+    def up(number, more, specs, *before):
+        return pl.pallas_call(
             functools.partial(up_kernel, number),
-            out_shape=(whole, both, slots),
-            in_specs=[VMEM, VMEM, HBM, VMEM, VMEM, HBM, HBM] + [HBM] * (3 * number),
-            out_specs=(HBM,) * 3,
+            out_shape=(whole, both) + more,
+            in_specs=[VMEM, VMEM, HBM, VMEM, VMEM] + [HBM] * (2 + 2 * number),
+            out_specs=(HBM, HBM) + specs,
             scratch_shapes=[
                 pltpu.VMEM((ROWS, C), jnp.bfloat16),
                 pltpu.VMEM((ROWS, C), jnp.bfloat16),
@@ -341,16 +366,31 @@
                 pltpu.VMEM((ROWS, C), jnp.bfloat16),
                 pltpu.SemaphoreType.DMA((5,)),
             ],
-            input_output_aliases={7: 0, 8: 1, 9: 2} if number else {},
+            input_output_aliases={7: 0, 8: 1} if number else {},
             compiler_params=MOST,
             cost_estimate=pl.CostEstimate(
                 flops=2_000_000_000, bytes_accessed=4_000_000, transcendentals=0
             ),
         )(
             condition, received[number], inputs, weight, gains, sent[number],
-            first_active[number], *([outs, actives, pieces] if number else []),
+            first_active[number], *before,
         )
+
+    outs, actives, *cots, back = up(0, (piece,) * 4 + (half,), (VMEM,) * 5)
+    returned = lax.ppermute(back, "section", [(1, 0)])
+    outs, actives, pieces = up(1, (slots,), (HBM,), outs, actives)
+    pieces = pl.pallas_call(
+        returned_kernel,
+        out_shape=slots,
+        in_specs=[VMEM, HBM],
+        out_specs=HBM,
+        scratch_shapes=[pltpu.VMEM((4, PIECE, 128), jnp.bfloat16), pltpu.SemaphoreType.DMA],
+        input_output_aliases={1: 0},
+        compiler_params=MOST,
+        cost_estimate=pl.CostEstimate(flops=COST, bytes_accessed=2_000_000, transcendentals=0),
+    )(returned, pieces)
     others = [exchange(actives, t, ((0, 0), (1, 1))) for t in range(1, 4)]
+    turned = [exchange(cots[t], t, ((1, 1),)) for t in range(1, 4)]
     arrived = lax.all_to_all(
         pieces, ("section",) + DP, 0, 0, axis_index_groups=squares(), tiled=True
     )
@@ -371,11 +411,11 @@
     main, tail, away = pl.pallas_call(
         weight_kernel,
         out_shape=(jax.ShapeDtypeStruct((C, 128), jnp.float32),) * 2 + (share,),
-        in_specs=[VMEM] * 5 + [HBM],
+        in_specs=[VMEM] * 9 + [HBM],
         out_specs=(VMEM,) * 3,
         scratch_shapes=packed,
         compiler_params=PARAMS,
-    )(actives, *others, arrived, gathered)
+    )(actives, *others, arrived, cots[0], *turned, gathered)
     other = lax.ppermute(away, "core", [(0, 1), (1, 0)])
     shares = pl.pallas_call(
         pair_kernel,

time: 100 us -> 99 us (0.990)
  starting transfers between devices: 15.8 us -> 29.6 us
  waiting for transfers between devices: 29.5 us -> 17.2 us
  blocking collectives: 31.5 us -> 27.9 us
  local copies, waits for them, and re-layouts: 2.32 us -> 3.84 us
  Pallas kernels: 19 us -> 17.7 us
    ppermute x3 -> x6, starting transfers between devices: 3.69 us -> 15.1 us  [exchange(): return lax.ppermute(block, ('section', 'y', 'z', 'core'), route)]
    all_to_all x1, waiting for transfers between devices: 6.35 us -> 0.01 us  [local(): lax.all_to_all(pieces, ('section',) + DP, 0, 0, axis_index_groups=squares...]
    ppermute x3 -> x6, waiting for transfers between devices: 9.62 us -> 4.29 us  [exchange(): return lax.ppermute(block, ('section', 'y', 'z', 'core'), route)]
    all_to_all x1, blocking collectives: 31.5 us -> 27.9 us  [local(): shares = lax.all_to_all(shares, DP, 0, 0, tiled=True)]
    ppermute x1, starting transfers between devices: 2.51 us -> 5.61 us  [local(): other = lax.ppermute(away, 'core', [(0, 1), (1, 0)])]
    all_to_all x1, starting transfers between devices: 7.06 us -> 4.82 us  [local(): lax.all_to_all(pieces, ('section',) + DP, 0, 0, axis_index_groups=squares...]
    unnamed x10 -> x16, local copies, waits for them, and re-layouts: 2.32 us -> 3.84 us
    ppermute x0 -> x1, starting transfers between devices: none -> 1.47 us  [local(): returned = lax.ppermute(back, 'section', [(1, 0)])]
  transfers between devices with their start and end apart: 7 -> 11, of which waited for: 6 -> 4; matrix products, arithmetic and copies ran while one was open for 0% -> 0% of each run, Pallas kernels for 5% -> 11%
where the time goes in v6:
time: 99 us; the launch traced here: 97.1 us
  starting transfers between devices  29.6 us (30%)
  blocking collectives  27.9 us (28%)
  Pallas kernels  17.7 us (18%)
  waiting for transfers between devices  17.2 us (17%)
  local copies, waits for them, and re-layouts  3.84 us (4%)
    all_to_all x1, blocking collectives, local(): shares = lax.all_to_all(shares, DP, 0, 0, tiled=True)  27.9 us
    ppermute x6, starting transfers between devices, exchange(): return lax.ppermute(block, ('section', 'y', 'z', 'core'), route)  15.1 us
    ppermute x2, waiting for transfers between devices, local(): received = [lax.ppermute(rows, 'section', [(0, 1)]) for rows in sent]  11.4 us
    pallas_call x2, Pallas kernels, up(): pl.pallas_call(functools.partial(up_kernel, number), out_shape=(whole, bo...  10.3 us
    ppermute x1, starting transfers between devices, local(): other = lax.ppermute(away, 'core', [(0, 1), (1, 0)])  5.61 us
    all_to_all x1, starting transfers between devices, local(): lax.all_to_all(pieces, ('section',) + DP, 0, 0, axis_index_groups=squares...  4.82 us
    ppermute x6, waiting for transfers between devices, exchange(): return lax.ppermute(block, ('section', 'y', 'z', 'core'), route)  4.29 us
    pallas_call x1, Pallas kernels, local(): pl.pallas_call(down_kernel, out_shape=(half,) * 4 + (jax.ShapeDtypeStruct...  3.95 us
  transfers between devices with their start and end apart: 11, of which 4 were waited for; matrix products, arithmetic and copies ran while one was open for 0% of the time, Pallas kernels for 11%

profile of v6, /device:TPU:6, one launch (start us, length us, event | category | flops | bytes accessed | tf_op | source)
XLA Modules:
  0.0 97.1 jit_solution(13987066124303454473)
XLA Ops:
  0.7 0.9 copy-done.1
  1.6 0.7 copy-done.4
  2.3 0.7 copy-done.6
  3.0 3.9 %shard_map.68 = (bf16[128,1280]{1,0:T(8,128)(2,1)S(1)}, bf16[128,1280]{1,0:T(8,128)(2,1)S(1)}, bf16[128,1280]{1,0:T(8,128)(2,1)S(1)}, bf16[128,1280]{1,0:T(8,128...) custom-call(s32[2,16]{1,0:T(2,128)S(1)} %copy-done.6, bf16[1,2,128,1280]{3,2,1,0:T(8,128)(2,1)} %refs_2_.3, ...), custom_call_target="tpu_custom_call" | custom-call | tf_op jit(solution)/shard_map/pallas_call | solution.py:332
  6.9 1.3 %collective-permute-start.1 = (bf16[128,1280]{1,0:T(8,128)(2,1)S(1)}, bf16[128,1280]{1,0:T(8,128)(2,1)S(1)}, u32[]{:S(2)}, u32[]{:S(2)}) collective-permute-start(bf16[128,1280]{1,0:T(8,128)(2,1)S(1)} %get-tuple-element.25.refs_5_), channel_id=1, source_target_pairs={{0,128},{1,129},{2,130},{3,131},{4,132},{5,133},{6,134},{7,135},{8... | collective-permute-start | bytes 983048 | tf_op jit(solution)/shard_map/ppermute | solution.py:351
  8.2 1.3 %collective-permute-start = (bf16[128,1280]{1,0:T(8,128)(2,1)S(1)}, bf16[128,1280]{1,0:T(8,128)(2,1)S(1)}, u32[]{:S(2)}, u32[]{:S(2)}) collective-permute-start(bf16[128,1280]{1,0:T(8,128)(2,1)S(1)} %get-tuple-element.22.refs_5_), channel_id=1, source_target_pairs={{0,128},{1,129},{2,130},{3,131},{4,132},{5,133},{6,134},{7,135},{8... | collective-permute-start | bytes 983048 | tf_op jit(solution)/shard_map/ppermute | solution.py:351
  9.5 11.4 %collective-permute-done.1.refs_1_ = bf16[128,1280]{1,0:T(8,128)(2,1)S(1)} collective-permute-done((bf16[128,1280]{1,0:T(8,128)(2,1)S(1)}, bf16[128,1280]{1,0:T(8,128)(2,1)S(1)}, u32[]{:S(2)}, u32[]{:S(2)}) %collective-permute-start.1) | collective-permute-done | bytes 327712 | tf_op jit(solution)/shard_map/ppermute | solution.py:351
  20.9 5.1 %shard_map.69 = (bf16[1,2,128,1280]{3,2,1,0:T(8,128)(2,1)}, bf16[256,1280]{1,0:T(8,128)(2,1)S(1)}, bf16[320,128]{1,0:T(8,128)(2,1)S(1)}, bf16[320,128]{1,0:T(8,1...) custom-call(f32[2,1,1280]{2,1,0:T(1,128)S(1)} %get-tuple-element.21.refs_0_, ...), custom_call_target="tpu_custom_call" | custom-call | flops 2000000000 | bytes 4000000 | tf_op jit(solution)/shard_map/pallas_call | solution.py:357
  26.0 1.5 %collective-permute-start.5 = (bf16[128,1280]{1,0:T(8,128)(2,1)S(1)}, bf16[128,1280]{1,0:T(8,128)(2,1)S(1)}, u32[]{:S(2)}, u32[]{:S(2)}) collective-permute-start(bf16[128,1280]{1,0:T(8,128)(2,1)S(1)} %get-tuple-element.31), channel_id=1, source_target_pairs={{128,0},{129,1},{130,2},{131,3},{132,4},{133,5},{134,6},{135,7},{1... | collective-permute-start | bytes 983048 | tf_op jit(solution)/shard_map/ppermute | solution.py:380
  27.5 0.0 collective-permute-done.refs_1_
  27.5 5.3 %shard_map.70 = (bf16[1,2,128,1280]{3,2,1,0:T(8,128)(2,1)}, bf16[256,1280]{1,0:T(8,128)(2,1)S(1)}, bf16[8,320,128]{2,1,0:T(8,128)(2,1)}) custom-call(f32[2,1,1280]{2,1,0:T(1,128)S(1)} %get-tuple-element.21.refs_0_, bf16[128,1280]{1,0:T(8,128)(2,1)S(1)} %collective-permute-done.refs_1_, ...), custom_call_target="tpu_custom_call", output_to_operand_aliasing={{0}: (7, {}), {1}: (8, {})} | custom-call | flops 2000000000 | bytes 4000000 | tf_op jit(solution)/shard_map/pallas_call | solution.py:357
  32.8 3.0 %collective-permute-start.4 = (bf16[256,1280]{1,0:T(8,128)(2,1)S(1)}, bf16[256,1280]{1,0:T(8,128)(2,1)S(1)}, u32[]{:S(2)}, u32[]{:S(2)}) collective-permute-start(bf16[256,1280]{1,0:T(8,128)(2,1)S(1)} %get-tuple-element.30.refs_0_), channel_id=1, source_target_pairs={{0,36},{1,125},{4,32},{5,105},{8,44},{9,101},{12,40},{13,113},{16,... | collective-permute-start | bytes 1966088 | tf_op jit(solution)/shard_map/ppermute | solution.py:326
  35.8 0.4 collective-permute-start.3
  36.3 0.2 collective-permute-start.2
  36.5 3.7 %collective-permute-start.6 = (bf16[320,128]{1,0:T(8,128)(2,1)}, bf16[320,128]{1,0:T(8,128)(2,1)S(1)}, u32[]{:S(2)}, u32[]{:S(2)}) collective-permute-start(bf16[320,128]{1,0:T(8,128)(2,1)} %get-tuple-element.34), channel_id=1, source_target_pairs={{128,132},{129,157},{132,128},{133,137},{136,140},{137,133},{140,1... | collective-permute-start | bytes 245768 | tf_op jit(solution)/shard_map/ppermute | solution.py:326
  40.2 0.0 collective-permute-done.5.rows_ref
  40.2 3.5 %collective-permute-start.7 = (bf16[320,128]{1,0:T(8,128)(2,1)}, bf16[320,128]{1,0:T(8,128)(2,1)S(1)}, u32[]{:S(2)}, u32[]{:S(2)}) collective-permute-start(bf16[320,128]{1,0:T(8,128)(2,1)} %get-tuple-element.35), channel_id=1, source_target_pairs={{128,160},{129,225},{132,164},{133,229},{136,168},{137,233},{140,1... | collective-permute-start | bytes 245768 | tf_op jit(solution)/shard_map/ppermute | solution.py:326
  43.7 4.8 %all-to-all-start = ((bf16[8,320,128]{2,1,0:T(8,128)(2,1)}), bf16[8,320,128]{2,1,0:T(8,128)(2,1)S(1)}, u32[]{:S(2)}, u32[]{:S(2)}) async-start(bf16[8,320,128]{2,1,0:T(8,128)(2,1)} %shard_map.71), calls=%async_computation | async-start | bytes 1310720 | tf_op jit(solution)/shard_map/all_to_all | solution.py:394
  48.6 0.0 collective-permute-done.4.refs_2_.refs_3_
  48.6 4.3 %collective-permute-start.8 = (bf16[320,128]{1,0:T(8,128)(2,1)}, bf16[320,128]{1,0:T(8,128)(2,1)S(1)}, u32[]{:S(2)}, u32[]{:S(2)}) collective-permute-start(bf16[320,128]{1,0:T(8,128)(2,1)} %copy-done.7), channel_id=1, source_target_pairs={{128,164},{129,253},{132,160},{133,233},{136,172},{137,229},{140,1... | collective-permute-start | bytes 245768 | tf_op jit(solution)/shard_map/ppermute | solution.py:326
  52.8 0.0 collective-permute-done.3.refs_1_.refs_2_
  52.8 0.0 collective-permute-done.2.refs_0_.refs_1_
  52.9 0.3 collective-permute-done.7.refs_7_
  53.2 4.0 %collective-permute-done.8.refs_8_ = bf16[320,128]{1,0:T(8,128)(2,1)S(1)} collective-permute-done((bf16[320,128]{1,0:T(8,128)(2,1)}, bf16[320,128]{1,0:T(8,128)(2,1)S(1)}, u32[]{:S(2)}, u32[]{:S(2)}) %collective-permute-start.8) | collective-permute-done | bytes 81952 | tf_op jit(solution)/shard_map/ppermute | solution.py:326
  57.2 0.6 copy-done.2
  57.8 0.9 copy-done.3
  58.7 2.0 %shard_map.73 = (f32[1280,128]{1,0:T(8,128)S(1)}, f32[1280,128]{1,0:T(8,128)S(1)}, bf16[128,16,128]{2,1,0:T(8,128)(2,1)S(1)}) custom-call(bf16[256,1280]{1,0:T(8,128)(2,1)S(1)} %get-tuple-element.30.refs_0_, bf16[256,1280]{1,0:T(8,128)(2,1)S(1)} %collective-permute-done.2.refs_0_.refs_1_, bf16[256,1280]{1,0:T(8,128)(2,1)S(1)} %collective-permute-done.3.refs_1_.refs_2_, ...), custom_call_target="tpu_custom_call" | custom-call | tf_op jit(solution)/shard_map/pallas_call | solution.py:411
  60.7 5.6 %collective-permute-start.9 = (bf16[128,16,128]{2,1,0:T(8,128)(2,1)S(1)}, bf16[128,16,128]{2,1,0:T(8,128)(2,1)S(1)}, u32[]{:S(2)}, u32[]{:S(2)}) collective-permute-start(bf16[128,16,128]{2,1,0:T(8,128)(2,1)S(1)} %get-tuple-element.39), channel_id=1, source_target_pairs={{0,1},{1,0},{2,3},{3,2},{4,5},{5,4},{6,7},{7,6},{8,9},{9,8},{10,11... | collective-permute-start | bytes 1572872 | tf_op jit(solution)/shard_map/ppermute | solution.py:419
  66.3 1.5 %collective-permute-done.9.other_ref = bf16[128,16,128]{2,1,0:T(8,128)(2,1)S(1)} collective-permute-done((bf16[128,16,128]{2,1,0:T(8,128)(2,1)S(1)}, bf16[128,16,128]{2,1,0:T(8,128)(2,1)S(1)}, u32[]{:S(2)}, u32[]{:S(2)}) %collective-permute-start.9) | collective-permute-done | bytes 524320 | tf_op jit(solution)/shard_map/ppermute | solution.py:419
  67.9 0.5 shard_map.74
  68.4 27.9 %all_to_all.10.shares_ref = bf16[128,16,128]{2,1,0:T(8,128)(2,1)S(1)} all-to-all(bf16[128,16,128]{2,1,0:T(8,128)(2,1)S(1)} %shard_map.74), channel_id=1, replica_groups=mesh['section'=2,'y'=4,'z'=8,'x'=2,'core'=2] {'y','z','x','core'}, dimensions={0} | all-to-all | bytes 1048576 | tf_op jit(solution)/shard_map/all_to_all | solution.py:428
  96.3 0.8 shard_map.75
  (15 shorter events, 0.1 us)
Async XLA Ops:
  0.6 20.3 %copy-start = (bf16[1,2,128,1280]{3,2,1,0:T(8,128)(2,1)S(1)}, bf16[1,2,128,1280]{3,2,1,0:T(8,128)(2,1)}, u32[]{:S(2)}) copy-start(bf16[1,2,128,1280]{3,2,1,0:T(8,128)(2,1)} %refs_2_.3) | copy-start | bytes 1966084
  0.6 1.0 copy-start.1
  1.6 0.7 copy-start.4
  2.3 0.7 copy-start.6
  3.0 18.0 %copy-start.5 = (f32[1,1280]{1,0:T(1,128)S(1)}, f32[1,1280]{1,0:T(1,128)}, u32[]{:S(2)}) copy-start(f32[1,1280]{1,0:T(1,128)} %refs_4_.3) | copy-start | bytes 15364
  6.9 14.0 %collective-permute-start.1 = (bf16[128,1280]{1,0:T(8,128)(2,1)S(1)}, bf16[128,1280]{1,0:T(8,128)(2,1)S(1)}, u32[]{:S(2)}, u32[]{:S(2)}) collective-permute-start(bf16[128,1280]{1,0:T(8,128)(2,1)S(1)} %get-tuple-element.25.refs_5_), channel_id=1, source_target_pairs={{0,128},{1,129},{2,130},{3,131},{4,132},{5,133},{6,134},{7,135},{8... | collective-permute-start | bytes 983048 | tf_op jit(solution)/shard_map/ppermute | solution.py:351
  8.2 19.3 %collective-permute-start = (bf16[128,1280]{1,0:T(8,128)(2,1)S(1)}, bf16[128,1280]{1,0:T(8,128)(2,1)S(1)}, u32[]{:S(2)}, u32[]{:S(2)}) collective-permute-start(bf16[128,1280]{1,0:T(8,128)(2,1)S(1)} %get-tuple-element.22.refs_5_), channel_id=1, source_target_pairs={{0,128},{1,129},{2,130},{3,131},{4,132},{5,133},{6,134},{7,135},{8... | collective-permute-start | bytes 983048 | tf_op jit(solution)/shard_map/ppermute | solution.py:351
  26.0 6.8 %copy-start.7 = (bf16[320,128]{1,0:T(8,128)(2,1)}, bf16[320,128]{1,0:T(8,128)(2,1)S(1)}, u32[]{:S(2)}) copy-start(bf16[320,128]{1,0:T(8,128)(2,1)S(1)} %get-tuple-element.36) | copy-start | bytes 245764
  26.0 14.2 %collective-permute-start.5 = (bf16[128,1280]{1,0:T(8,128)(2,1)S(1)}, bf16[128,1280]{1,0:T(8,128)(2,1)S(1)}, u32[]{:S(2)}, u32[]{:S(2)}) collective-permute-start(bf16[128,1280]{1,0:T(8,128)(2,1)S(1)} %get-tuple-element.31), channel_id=1, source_target_pairs={{128,0},{129,1},{130,2},{131,3},{132,4},{133,5},{134,6},{135,7},{1... | collective-permute-start | bytes 983048 | tf_op jit(solution)/shard_map/ppermute | solution.py:380
  32.8 15.8 %collective-permute-start.4 = (bf16[256,1280]{1,0:T(8,128)(2,1)S(1)}, bf16[256,1280]{1,0:T(8,128)(2,1)S(1)}, u32[]{:S(2)}, u32[]{:S(2)}) collective-permute-start(bf16[256,1280]{1,0:T(8,128)(2,1)S(1)} %get-tuple-element.30.refs_0_), channel_id=1, source_target_pairs={{0,36},{1,125},{4,32},{5,105},{8,44},{9,101},{12,40},{13,113},{16,... | collective-permute-start | bytes 1966088 | tf_op jit(solution)/shard_map/ppermute | solution.py:326
  35.8 17.0 %collective-permute-start.3 = (bf16[256,1280]{1,0:T(8,128)(2,1)S(1)}, bf16[256,1280]{1,0:T(8,128)(2,1)S(1)}, u32[]{:S(2)}, u32[]{:S(2)}) collective-permute-start(bf16[256,1280]{1,0:T(8,128)(2,1)S(1)} %get-tuple-element.30.refs_0_), channel_id=1, source_target_pairs={{0,32},{1,97},{4,36},{5,101},{8,40},{9,105},{12,44},{13,109},{16,4... | collective-permute-start | bytes 1966088 | tf_op jit(solution)/shard_map/ppermute | solution.py:326
  36.3 16.6 %collective-permute-start.2 = (bf16[256,1280]{1,0:T(8,128)(2,1)S(1)}, bf16[256,1280]{1,0:T(8,128)(2,1)S(1)}, u32[]{:S(2)}, u32[]{:S(2)}) collective-permute-start(bf16[256,1280]{1,0:T(8,128)(2,1)S(1)} %get-tuple-element.30.refs_0_), channel_id=1, source_target_pairs={{0,4},{1,29},{4,0},{5,9},{8,12},{9,5},{12,8},{13,17},{16,20},{17,1... | collective-permute-start | bytes 1966088 | tf_op jit(solution)/shard_map/ppermute | solution.py:326
  36.5 16.4 %collective-permute-start.6 = (bf16[320,128]{1,0:T(8,128)(2,1)}, bf16[320,128]{1,0:T(8,128)(2,1)S(1)}, u32[]{:S(2)}, u32[]{:S(2)}) collective-permute-start(bf16[320,128]{1,0:T(8,128)(2,1)} %get-tuple-element.34), channel_id=1, source_target_pairs={{128,132},{129,157},{132,128},{133,137},{136,140},{137,133},{140,1... | collective-permute-start | bytes 245768 | tf_op jit(solution)/shard_map/ppermute | solution.py:326
  40.2 13.0 %collective-permute-start.7 = (bf16[320,128]{1,0:T(8,128)(2,1)}, bf16[320,128]{1,0:T(8,128)(2,1)S(1)}, u32[]{:S(2)}, u32[]{:S(2)}) collective-permute-start(bf16[320,128]{1,0:T(8,128)(2,1)} %get-tuple-element.35), channel_id=1, source_target_pairs={{128,160},{129,225},{132,164},{133,229},{136,168},{137,233},{140,1... | collective-permute-start | bytes 245768 | tf_op jit(solution)/shard_map/ppermute | solution.py:326
  43.7 14.0 %all-to-all-start = ((bf16[8,320,128]{2,1,0:T(8,128)(2,1)}), bf16[8,320,128]{2,1,0:T(8,128)(2,1)S(1)}, u32[]{:S(2)}, u32[]{:S(2)}) async-start(bf16[8,320,128]{2,1,0:T(8,128)(2,1)} %shard_map.71), calls=%async_computation | async-start | bytes 1310720 | tf_op jit(solution)/shard_map/all_to_all | solution.py:394
  48.6 8.6 %collective-permute-start.8 = (bf16[320,128]{1,0:T(8,128)(2,1)}, bf16[320,128]{1,0:T(8,128)(2,1)S(1)}, u32[]{:S(2)}, u32[]{:S(2)}) collective-permute-start(bf16[320,128]{1,0:T(8,128)(2,1)} %copy-done.7), channel_id=1, source_target_pairs={{128,164},{129,253},{132,160},{133,233},{136,172},{137,229},{140,1... | collective-permute-start | bytes 245768 | tf_op jit(solution)/shard_map/ppermute | solution.py:326
  57.1 0.6 copy-start.2
  57.8 0.9 copy-start.3
  60.7 7.1 %collective-permute-start.9 = (bf16[128,16,128]{2,1,0:T(8,128)(2,1)S(1)}, bf16[128,16,128]{2,1,0:T(8,128)(2,1)S(1)}, u32[]{:S(2)}, u32[]{:S(2)}) collective-permute-start(bf16[128,16,128]{2,1,0:T(8,128)(2,1)S(1)} %get-tuple-element.39), channel_id=1, source_target_pairs={{0,1},{1,0},{2,3},{3,2},{4,5},{5,4},{6,7},{7,6},{8,9},{9,8},{10,11... | collective-permute-start | bytes 1572872 | tf_op jit(solution)/shard_map/ppermute | solution.py:419

commit v7 on v6

--- a/solution.py
+++ b/solution.py
@@ -104,8 +104,8 @@
 
 def up_kernel(number, *refs):
     cond_ref, arrived_ref, rows_hbm, weight_ref, gain_ref, sent_hbm, first_active_hbm = refs[:7]
-    outs_hbm, actives_hbm, *send_refs = refs[7 + 2 * number : -5]
-    out_ref, active_ref, pieces_ref, rows_ref, sems = refs[-5:]
+    outs_hbm, actives_hbm, cot_ref, back_ref = refs[7 + 2 * number : -4]
+    out_ref, active_ref, rows_ref, sems = refs[-4:]
     active_hbm = actives_hbm.at[pl.ds(ROWS * number, ROWS)]
     rows_copy = pltpu.make_async_copy(rows_hbm.at[0, number], rows_ref, sems.at[0])
     rows_copy.start()
@@ -140,34 +140,15 @@
 
     rows_copy.wait()
     cot = (upper - rows_ref[...].astype(jnp.float32)) / math.sqrt(MICRO * ROWS * LANES)
-    if number:
-        store_pieces(pieces_ref, 4, cot)
-        sends = [
-            pltpu.make_async_copy(
-                pieces_ref.at[pl.ds(at, 4)], send_refs[0].at[pl.ds(at, 4)], sems.at[sem]
-            )
-            for at, sem in ((4, 3), (0, 4))
-        ]
-        sends[0].start()
-    else:
-        store_pieces(pieces_ref, 4, cot)
-        own = own_quarter()
-        for turn in range(4):
-            send_refs[turn][...] = pieces_ref[4 + lax.bitwise_xor(own, turn)]
     cot = cot.astype(jnp.bfloat16)
+    cot_ref[...] = cot
     through = lax.dot_general(
         cot, weight, (((1,), (1,)), ((), ())), preferred_element_type=jnp.float32
     )
     scaled = through * sigma * (1.0 + normed * (1.0 - sigma)) * gain
     inner = jnp.mean(scaled * shifted, axis=-1, keepdims=True)
     back = cot.astype(jnp.float32) + inverse * scaled - shifted * inverse**3 * inner
-    if number:
-        store_pieces(pieces_ref, 0, back)
-        sends[1].start()
-        for send in sends:
-            send.wait()
-    else:
-        send_refs[4][...] = back.astype(jnp.bfloat16)
+    back_ref[...] = back.astype(jnp.bfloat16)
 
     @pl.when(down)
     def _():
@@ -199,24 +180,38 @@
     lax.fori_loop(0, LANES // 8, lanes, 0)
 
 
-def returned_kernel(rows_ref, pieces_in, pieces_hbm, pieces_ref, sem):
-    del pieces_in
-
-    @pl.when(lax.axis_index("section") == 0)
-    def _():
-        store_pieces(pieces_ref, 0, rows_ref[...].astype(jnp.float32))
-        copy = pltpu.make_async_copy(pieces_ref, pieces_hbm.at[pl.ds(0, 4)], sem)
-        copy.start()
+def pieces_kernel(returned_ref, cot_ref, back_ref, pieces_hbm, pieces_ref, sems):
+    copies = [
+        pltpu.make_async_copy(pieces_ref.at[pl.ds(at, 4)], pieces_hbm.at[pl.ds(at, 4)], sem)
+        for at, sem in ((0, sems.at[0]), (4, sems.at[1]))
+    ]
+    store_pieces(pieces_ref, 4, cot_ref[...].astype(jnp.float32))
+    copies[1].start()
+    down = lax.axis_index("section") == 0
+    rows = jnp.where(down, returned_ref[...], back_ref[...])
+    store_pieces(pieces_ref, 0, rows.astype(jnp.float32))
+    copies[0].start()
+    for copy in copies:
         copy.wait()
 
 
-def gathered_kernel(*refs):
-    refs[-1][...] = jnp.zeros_like(refs[-1])
+def cots_kernel(cot_ref, pieces_hbm, *refs):
+    del pieces_hbm
+    store_pieces(refs[3], 0, cot_ref[...].astype(jnp.float32))
+    own = own_quarter()
+    for turn in range(1, 4):
+        refs[turn - 1][...] = refs[3][lax.bitwise_xor(own, turn)]
+
+
+def own_kernel(cot_ref, *refs):
+    own_ref, pieces_ref = refs[3:]
+    store_pieces(pieces_ref, 0, cot_ref[...].astype(jnp.float32))
+    own_ref[...] = pieces_ref[own_quarter()]
 
 
 def weight_kernel(*refs):
     active_refs, piece_ref, cot_refs = refs[:4], refs[4], refs[5:9]
-    main_ref, tail_ref, away_ref, main, tail, staged = refs[10:]
+    main_ref, tail_ref, away_ref, main, tail, staged = refs[9:]
     down, core = lax.axis_index("section") == 0, lax.axis_index("core")
     own = own_quarter()
     low = lax.broadcasted_iota(jnp.int32, (ROWS // 2, 128), 1) < 64
@@ -353,18 +348,17 @@
     piece = jax.ShapeDtypeStruct((PIECE, 128), jnp.bfloat16)
     slots = jax.ShapeDtypeStruct((8, PIECE, 128), jnp.bfloat16)
 
-    def up(number, more, specs, *before):
+    def up(number, *before):
         return pl.pallas_call(
             functools.partial(up_kernel, number),
-            out_shape=(whole, both) + more,
+            out_shape=(whole, both, half, half),
             in_specs=[VMEM, VMEM, HBM, VMEM, VMEM] + [HBM] * (2 + 2 * number),
-            out_specs=(HBM, HBM) + specs,
+            out_specs=(HBM, HBM, VMEM, VMEM),
             scratch_shapes=[
                 pltpu.VMEM((ROWS, C), jnp.bfloat16),
                 pltpu.VMEM((ROWS, C), jnp.bfloat16),
-                pltpu.VMEM((8, PIECE, 128), jnp.bfloat16),
                 pltpu.VMEM((ROWS, C), jnp.bfloat16),
-                pltpu.SemaphoreType.DMA((5,)),
+                pltpu.SemaphoreType.DMA((3,)),
             ],
             input_output_aliases={7: 0, 8: 1} if number else {},
             compiler_params=MOST,
@@ -376,21 +370,31 @@
             first_active[number], *before,
         )
 
-    outs, actives, *cots, back = up(0, (piece,) * 4 + (half,), (VMEM,) * 5)
-    returned = lax.ppermute(back, "section", [(1, 0)])
-    outs, actives, pieces = up(1, (slots,), (HBM,), outs, actives)
+    outs, actives, cot_0, back_0 = up(0)
+    returned = lax.ppermute(back_0, "section", [(1, 0)])
+    outs, actives, cot_1, back_1 = up(1, outs, actives)
     pieces = pl.pallas_call(
-        returned_kernel,
+        pieces_kernel,
         out_shape=slots,
-        in_specs=[VMEM, HBM],
+        in_specs=[VMEM] * 3,
         out_specs=HBM,
-        scratch_shapes=[pltpu.VMEM((4, PIECE, 128), jnp.bfloat16), pltpu.SemaphoreType.DMA],
-        input_output_aliases={1: 0},
+        scratch_shapes=[
+            pltpu.VMEM((8, PIECE, 128), jnp.bfloat16),
+            pltpu.SemaphoreType.DMA((2,)),
+        ],
         compiler_params=MOST,
         cost_estimate=pl.CostEstimate(flops=COST, bytes_accessed=2_000_000, transcendentals=0),
-    )(returned, pieces)
+    )(returned, cot_1, back_1)
+    cots = pl.pallas_call(
+        cots_kernel,
+        out_shape=(piece,) * 3,
+        in_specs=[VMEM, HBM],
+        out_specs=(VMEM,) * 3,
+        scratch_shapes=[pltpu.VMEM((4, PIECE, 128), jnp.bfloat16)],
+        compiler_params=PARAMS,
+    )(cot_0, pieces)
     others = [exchange(actives, t, ((0, 0), (1, 1))) for t in range(1, 4)]
-    turned = [exchange(cots[t], t, ((1, 1),)) for t in range(1, 4)]
+    turned = [exchange(cots[t - 1], t, ((1, 1),)) for t in range(1, 4)]
     arrived = lax.all_to_all(
         pieces, ("section",) + DP, 0, 0, axis_index_groups=squares(), tiled=True
     )
@@ -400,22 +404,23 @@
         pltpu.VMEM((LANES * SHARE, 128), jnp.float32),
     ]
     share = jax.ShapeDtypeStruct((LANES, SHARE, 128), jnp.bfloat16)
-    gathered = pl.pallas_call(
-        gathered_kernel,
-        out_shape=jax.ShapeDtypeStruct((8, 128), jnp.float32),
-        in_specs=[HBM] * 3,
+    own = pl.pallas_call(
+        own_kernel,
+        out_shape=piece,
+        in_specs=[VMEM] + [HBM] * 3,
         out_specs=VMEM,
+        scratch_shapes=[pltpu.VMEM((4, PIECE, 128), jnp.bfloat16)],
         compiler_params=PARAMS,
         cost_estimate=pl.CostEstimate(flops=COST, bytes_accessed=2_000_000, transcendentals=0),
-    )(*others)
+    )(cot_0, *others)
     main, tail, away = pl.pallas_call(
         weight_kernel,
         out_shape=(jax.ShapeDtypeStruct((C, 128), jnp.float32),) * 2 + (share,),
-        in_specs=[VMEM] * 9 + [HBM],
+        in_specs=[VMEM] * 9,
         out_specs=(VMEM,) * 3,
         scratch_shapes=packed,
         compiler_params=PARAMS,
-    )(actives, *others, arrived, cots[0], *turned, gathered)
+    )(actives, *others, arrived, own, *turned)
     other = lax.ppermute(away, "core", [(0, 1), (1, 0)])
     shares = pl.pallas_call(
         pair_kernel,

time: 99 us -> 98 us (0.990); the launches traced: 97.1 us -> 97.4 us
  starting transfers between devices: 29.6 us -> 32.6 us
  blocking collectives: 27.9 us -> 25 us
    ppermute x1, starting transfers between devices: 5.61 us -> 8.54 us  [local(): other = lax.ppermute(away, 'core', [(0, 1), (1, 0)])]
    all_to_all x1, blocking collectives: 27.9 us -> 25 us  [local(): shares = lax.all_to_all(shares, DP, 0, 0, tiled=True)]
    all_to_all x1, starting transfers between devices: 4.82 us -> 7.08 us  [local(): lax.all_to_all(pieces, ('section',) + DP, 0, 0, axis_index_groups=squares...]
    ppermute x6, starting transfers between devices: 15.1 us -> 12.9 us  [exchange(): return lax.ppermute(block, ('section', 'y', 'z', 'core'), route)]
    pallas_call x2, Pallas kernels: 10.3 us -> 8.81 us  [up(): pl.pallas_call(functools.partial(up_kernel, number), out_shape=(whole, bo...]
    pallas_call x2 -> x3, Pallas kernels: 0.03 us -> 1.17 us  [the longest x1 0.97 us: local(): pl.pallas_call(pieces_kernel, out_shape=slots, in_specs=[VMEM] * 3, out_s...]
    unnamed x16 -> x18, local copies, waits for them, and re-layouts: 3.84 us -> 4.81 us
  transfers between devices with their start and end apart: 11 -> 11, of which waited for: 4 -> 4; matrix products, arithmetic and copies ran while one was open for 0% -> 0% of each run, Pallas kernels for 11% -> 10%
where the time goes in v7:
time: 98 us; the launch traced here: 97.4 us
  starting transfers between devices  32.6 us (33%)
  blocking collectives  25 us (26%)
  Pallas kernels  17.3 us (18%)
  waiting for transfers between devices  17 us (17%)
  local copies, waits for them, and re-layouts  4.81 us (5%)
    all_to_all x1, blocking collectives, local(): shares = lax.all_to_all(shares, DP, 0, 0, tiled=True)  25 us
    ppermute x6, starting transfers between devices, exchange(): return lax.ppermute(block, ('section', 'y', 'z', 'core'), route)  12.9 us
    ppermute x2, waiting for transfers between devices, local(): received = [lax.ppermute(rows, 'section', [(0, 1)]) for rows in sent]  11.4 us
    pallas_call x2, Pallas kernels, up(): pl.pallas_call(functools.partial(up_kernel, number), out_shape=(whole, bo...  8.81 us
    ppermute x1, starting transfers between devices, local(): other = lax.ppermute(away, 'core', [(0, 1), (1, 0)])  8.54 us
    all_to_all x1, starting transfers between devices, local(): lax.all_to_all(pieces, ('section',) + DP, 0, 0, axis_index_groups=squares...  7.08 us
    unnamed x18, local copies, waits for them, and re-layouts  4.81 us
    ppermute x6, waiting for transfers between devices, exchange(): return lax.ppermute(block, ('section', 'y', 'z', 'core'), route)  4.02 us
  transfers between devices with their start and end apart: 11, of which 4 were waited for; matrix products, arithmetic and copies ran while one was open for 0% of the time, Pallas kernels for 10%

profile of v7, /device:TPU:6, one launch (start us, length us, event | category | flops | bytes accessed | tf_op | source)
XLA Modules:
  0.0 97.4 jit_solution(14003300419657445328)
XLA Ops:
  0.7 0.9 copy-done.3
  1.6 0.7 copy-done.6
  2.3 0.7 copy-done.8
  3.0 3.9 %shard_map.68 = (bf16[128,1280]{1,0:T(8,128)(2,1)S(1)}, bf16[128,1280]{1,0:T(8,128)(2,1)S(1)}, bf16[128,1280]{1,0:T(8,128)(2,1)S(1)}, bf16[128,1280]{1,0:T(8,128...) custom-call(s32[2,16]{1,0:T(2,128)S(1)} %copy-done.8, bf16[1,2,128,1280]{3,2,1,0:T(8,128)(2,1)} %refs_2_.3, ...), custom_call_target="tpu_custom_call" | custom-call | tf_op jit(solution)/shard_map/pallas_call | solution.py:327
  6.9 1.3 %collective-permute-start.1 = (bf16[128,1280]{1,0:T(8,128)(2,1)S(1)}, bf16[128,1280]{1,0:T(8,128)(2,1)S(1)}, u32[]{:S(2)}, u32[]{:S(2)}) collective-permute-start(bf16[128,1280]{1,0:T(8,128)(2,1)S(1)} %get-tuple-element.26.refs_5_), channel_id=1, source_target_pairs={{0,128},{1,129},{2,130},{3,131},{4,132},{5,133},{6,134},{7,135},{8... | collective-permute-start | bytes 983048 | tf_op jit(solution)/shard_map/ppermute | solution.py:346
  8.2 1.3 %collective-permute-start = (bf16[128,1280]{1,0:T(8,128)(2,1)S(1)}, bf16[128,1280]{1,0:T(8,128)(2,1)S(1)}, u32[]{:S(2)}, u32[]{:S(2)}) collective-permute-start(bf16[128,1280]{1,0:T(8,128)(2,1)S(1)} %get-tuple-element.23.refs_5_), channel_id=1, source_target_pairs={{0,128},{1,129},{2,130},{3,131},{4,132},{5,133},{6,134},{7,135},{8... | collective-permute-start | bytes 983048 | tf_op jit(solution)/shard_map/ppermute | solution.py:346
  9.5 11.4 %collective-permute-done.1.refs_1_ = bf16[128,1280]{1,0:T(8,128)(2,1)S(1)} collective-permute-done((bf16[128,1280]{1,0:T(8,128)(2,1)S(1)}, bf16[128,1280]{1,0:T(8,128)(2,1)S(1)}, u32[]{:S(2)}, u32[]{:S(2)}) %collective-permute-start.1) | collective-permute-done | bytes 327712 | tf_op jit(solution)/shard_map/ppermute | solution.py:346
  20.9 4.4 %shard_map.69 = (bf16[1,2,128,1280]{3,2,1,0:T(8,128)(2,1)}, bf16[256,1280]{1,0:T(8,128)(2,1)S(1)}, bf16[128,1280]{1,0:T(8,128)(2,1)S(1)}, bf16[128,1280]{1,0:T(8,128)(2,1)S(1)}) custom-call(f32[2,1,1280]{2,1,0:T(1,128)S(1)} %get-tuple-element.22.refs_0_, bf16[128,1280]{1,0:T(8,128)(2,1)S(1)} %collective-permute-done.1.refs_1_, ...), custom_call_target="tpu_custom_call" | custom-call | flops 2000000000 | bytes 4000000 | tf_op jit(solution)/shard_map/pallas_call | solution.py:352
  25.3 1.5 %collective-permute-start.5 = (bf16[128,1280]{1,0:T(8,128)(2,1)S(1)}, bf16[128,1280]{1,0:T(8,128)(2,1)S(1)}, u32[]{:S(2)}, u32[]{:S(2)}) collective-permute-start(bf16[128,1280]{1,0:T(8,128)(2,1)S(1)} %get-tuple-element.32), channel_id=1, source_target_pairs={{128,0},{129,1},{130,2},{131,3},{132,4},{133,5},{134,6},{135,7},{1... | collective-permute-start | bytes 983048 | tf_op jit(solution)/shard_map/ppermute | solution.py:374
  26.8 4.4 %shard_map.70 = (bf16[1,2,128,1280]{3,2,1,0:T(8,128)(2,1)}, bf16[256,1280]{1,0:T(8,128)(2,1)S(1)}, bf16[128,1280]{1,0:T(8,128)(2,1)S(1)}, bf16[128,1280]{1,0:T(8,128)(2,1)S(1)}) custom-call(f32[2,1,1280]{2,1,0:T(1,128)S(1)} %get-tuple-element.22.refs_0_, ...), custom_call_target="tpu_custom_call", output_to_operand_aliasing={{0}: (7, {}), {1}: (8, {})} | custom-call | flops 2000000000 | bytes 4000000 | tf_op jit(solution)/shard_map/pallas_call | solution.py:352
  31.2 3.0 %collective-permute-start.4 = (bf16[256,1280]{1,0:T(8,128)(2,1)S(1)}, bf16[256,1280]{1,0:T(8,128)(2,1)S(1)}, u32[]{:S(2)}, u32[]{:S(2)}) collective-permute-start(bf16[256,1280]{1,0:T(8,128)(2,1)S(1)} %get-tuple-element.31.refs_0_), channel_id=1, source_target_pairs={{0,36},{1,125},{4,32},{5,105},{8,44},{9,101},{12,40},{13,113},{16,... | collective-permute-start | bytes 1966088 | tf_op jit(solution)/shard_map/ppermute | solution.py:321
  34.3 0.5 collective-permute-start.3
  34.7 0.2 collective-permute-start.2
  34.9 0.0 collective-permute-done.5.returned_ref
  34.9 1.0 shard_map.71.pieces_hbm
  35.9 7.1 %all-to-all-start = ((bf16[8,320,128]{2,1,0:T(8,128)(2,1)}), bf16[8,320,128]{2,1,0:T(8,128)(2,1)S(1)}, u32[]{:S(2)}, u32[]{:S(2)}) async-start(bf16[8,320,128]{2,1,0:T(8,128)(2,1)} %shard_map.71.pieces_hbm), calls=%async_computation | async-start | bytes 1310720 | tf_op jit(solution)/shard_map/all_to_all | solution.py:398
  43.0 1.0 copy-done.2
  44.0 0.1 shard_map.73
  44.1 3.4 %collective-permute-start.6 = (bf16[320,128]{1,0:T(8,128)(2,1)S(1)}, bf16[320,128]{1,0:T(8,128)(2,1)S(1)}, u32[]{:S(2)}, u32[]{:S(2)}) collective-permute-start(bf16[320,128]{1,0:T(8,128)(2,1)S(1)} %get-tuple-element.36), channel_id=1, source_target_pairs={{128,132},{129,157},{132,128},{133,137},{136,140},{137,133},{140,1... | collective-permute-start | bytes 245768 | tf_op jit(solution)/shard_map/ppermute | solution.py:321
  47.4 3.4 %collective-permute-start.7 = (bf16[320,128]{1,0:T(8,128)(2,1)S(1)}, bf16[320,128]{1,0:T(8,128)(2,1)S(1)}, u32[]{:S(2)}, u32[]{:S(2)}) collective-permute-start(bf16[320,128]{1,0:T(8,128)(2,1)S(1)} %get-tuple-element.37), channel_id=1, source_target_pairs={{128,160},{129,225},{132,164},{133,229},{136,168},{137,233},{140,1... | collective-permute-start | bytes 245768 | tf_op jit(solution)/shard_map/ppermute | solution.py:321
  50.8 2.5 %collective-permute-start.8 = (bf16[320,128]{1,0:T(8,128)(2,1)S(1)}, bf16[320,128]{1,0:T(8,128)(2,1)S(1)}, u32[]{:S(2)}, u32[]{:S(2)}) collective-permute-start(bf16[320,128]{1,0:T(8,128)(2,1)S(1)} %get-tuple-element.38), channel_id=1, source_target_pairs={{128,164},{129,253},{132,160},{133,233},{136,172},{137,229},{140,1... | collective-permute-start | bytes 245768 | tf_op jit(solution)/shard_map/ppermute | solution.py:321
  53.3 0.1 shard_map.72.refs_5_
  53.4 0.6 copy-done.4
  54.1 0.4 collective-permute-done.6.refs_6_
  54.4 3.6 %collective-permute-done.8.refs_8_ = bf16[320,128]{1,0:T(8,128)(2,1)S(1)} collective-permute-done((bf16[320,128]{1,0:T(8,128)(2,1)S(1)}, bf16[320,128]{1,0:T(8,128)(2,1)S(1)}, u32[]{:S(2)}, u32[]{:S(2)}) %collective-permute-start.8) | collective-permute-done | bytes 81952 | tf_op jit(solution)/shard_map/ppermute | solution.py:321
  58.1 0.9 copy-done.5
  59.0 2.0 %shard_map.74 = (f32[1280,128]{1,0:T(8,128)S(1)}, f32[1280,128]{1,0:T(8,128)S(1)}, bf16[128,16,128]{2,1,0:T(8,128)(2,1)S(1)}) custom-call(bf16[256,1280]{1,0:T(8,128)(2,1)S(1)} %get-tuple-element.31.refs_0_, bf16[256,1280]{1,0:T(8,128)(2,1)S(1)} %collective-permute-done.2.refs_0_.refs_1_, bf16[256,1280]{1,0:T(8,128)(2,1)S(1)} %collective-permute-done.3.refs_1_.refs_2_, ...), custom_call_target="tpu_custom_call" | custom-call | tf_op jit(solution)/shard_map/pallas_call | solution.py:416
  61.0 8.5 %collective-permute-start.9 = (bf16[128,16,128]{2,1,0:T(8,128)(2,1)S(1)}, bf16[128,16,128]{2,1,0:T(8,128)(2,1)S(1)}, u32[]{:S(2)}, u32[]{:S(2)}) collective-permute-start(bf16[128,16,128]{2,1,0:T(8,128)(2,1)S(1)} %get-tuple-element.41), channel_id=1, source_target_pairs={{0,1},{1,0},{2,3},{3,2},{4,5},{5,4},{6,7},{7,6},{8,9},{9,8},{10,11... | collective-permute-start | bytes 1572872 | tf_op jit(solution)/shard_map/ppermute | solution.py:424
  69.6 1.5 %collective-permute-done.9.other_ref = bf16[128,16,128]{2,1,0:T(8,128)(2,1)S(1)} collective-permute-done((bf16[128,16,128]{2,1,0:T(8,128)(2,1)S(1)}, bf16[128,16,128]{2,1,0:T(8,128)(2,1)S(1)}, u32[]{:S(2)}, u32[]{:S(2)}) %collective-permute-start.9) | collective-permute-done | bytes 524320 | tf_op jit(solution)/shard_map/ppermute | solution.py:424
  71.1 0.5 shard_map.75
  71.6 25.0 %all_to_all.10.shares_ref = bf16[128,16,128]{2,1,0:T(8,128)(2,1)S(1)} all-to-all(bf16[128,16,128]{2,1,0:T(8,128)(2,1)S(1)} %shard_map.75), channel_id=1, replica_groups=mesh['section'=2,'y'=4,'z'=8,'x'=2,'core'=2] {'y','z','x','core'}, dimensions={0} | all-to-all | bytes 1048576 | tf_op jit(solution)/shard_map/all_to_all | solution.py:433
  96.7 0.8 shard_map.76
  (18 shorter events, 0.0 us)
Async XLA Ops:
  0.6 20.3 %copy-start = (bf16[1,2,128,1280]{3,2,1,0:T(8,128)(2,1)S(1)}, bf16[1,2,128,1280]{3,2,1,0:T(8,128)(2,1)}, u32[]{:S(2)}) copy-start(bf16[1,2,128,1280]{3,2,1,0:T(8,128)(2,1)} %refs_2_.3) | copy-start | bytes 1966084
  0.6 1.0 copy-start.3
  1.6 0.7 copy-start.6
  2.3 0.7 copy-start.8
  3.0 17.9 %copy-start.7 = (f32[1,1280]{1,0:T(1,128)S(1)}, f32[1,1280]{1,0:T(1,128)}, u32[]{:S(2)}) copy-start(f32[1,1280]{1,0:T(1,128)} %refs_4_.3) | copy-start | bytes 15364
  6.9 14.0 %collective-permute-start.1 = (bf16[128,1280]{1,0:T(8,128)(2,1)S(1)}, bf16[128,1280]{1,0:T(8,128)(2,1)S(1)}, u32[]{:S(2)}, u32[]{:S(2)}) collective-permute-start(bf16[128,1280]{1,0:T(8,128)(2,1)S(1)} %get-tuple-element.26.refs_5_), channel_id=1, source_target_pairs={{0,128},{1,129},{2,130},{3,131},{4,132},{5,133},{6,134},{7,135},{8... | collective-permute-start | bytes 983048 | tf_op jit(solution)/shard_map/ppermute | solution.py:346
  8.2 18.6 %collective-permute-start = (bf16[128,1280]{1,0:T(8,128)(2,1)S(1)}, bf16[128,1280]{1,0:T(8,128)(2,1)S(1)}, u32[]{:S(2)}, u32[]{:S(2)}) collective-permute-start(bf16[128,1280]{1,0:T(8,128)(2,1)S(1)} %get-tuple-element.23.refs_5_), channel_id=1, source_target_pairs={{0,128},{1,129},{2,130},{3,131},{4,132},{5,133},{6,134},{7,135},{8... | collective-permute-start | bytes 983048 | tf_op jit(solution)/shard_map/ppermute | solution.py:346
  25.3 5.9 %copy-start.1 = (bf16[128,1280]{1,0:T(8,128)(2,1)}, bf16[128,1280]{1,0:T(8,128)(2,1)S(1)}, u32[]{:S(2)}) copy-start(bf16[128,1280]{1,0:T(8,128)(2,1)S(1)} %get-tuple-element.35.cot_ref) | copy-start | bytes 983044
  25.3 9.6 %collective-permute-start.5 = (bf16[128,1280]{1,0:T(8,128)(2,1)S(1)}, bf16[128,1280]{1,0:T(8,128)(2,1)S(1)}, u32[]{:S(2)}, u32[]{:S(2)}) collective-permute-start(bf16[128,1280]{1,0:T(8,128)(2,1)S(1)} %get-tuple-element.32), channel_id=1, source_target_pairs={{128,0},{129,1},{130,2},{131,3},{132,4},{133,5},{134,6},{135,7},{1... | collective-permute-start | bytes 983048 | tf_op jit(solution)/shard_map/ppermute | solution.py:374
  31.2 19.6 %collective-permute-start.4 = (bf16[256,1280]{1,0:T(8,128)(2,1)S(1)}, bf16[256,1280]{1,0:T(8,128)(2,1)S(1)}, u32[]{:S(2)}, u32[]{:S(2)}) collective-permute-start(bf16[256,1280]{1,0:T(8,128)(2,1)S(1)} %get-tuple-element.31.refs_0_), channel_id=1, source_target_pairs={{0,36},{1,125},{4,32},{5,105},{8,44},{9,101},{12,40},{13,113},{16,... | collective-permute-start | bytes 1966088 | tf_op jit(solution)/shard_map/ppermute | solution.py:321
  34.3 19.1 %collective-permute-start.3 = (bf16[256,1280]{1,0:T(8,128)(2,1)S(1)}, bf16[256,1280]{1,0:T(8,128)(2,1)S(1)}, u32[]{:S(2)}, u32[]{:S(2)}) collective-permute-start(bf16[256,1280]{1,0:T(8,128)(2,1)S(1)} %get-tuple-element.31.refs_0_), channel_id=1, source_target_pairs={{0,32},{1,97},{4,36},{5,101},{8,40},{9,105},{12,44},{13,109},{16,4... | collective-permute-start | bytes 1966088 | tf_op jit(solution)/shard_map/ppermute | solution.py:321
  34.7 18.6 %collective-permute-start.2 = (bf16[256,1280]{1,0:T(8,128)(2,1)S(1)}, bf16[256,1280]{1,0:T(8,128)(2,1)S(1)}, u32[]{:S(2)}, u32[]{:S(2)}) collective-permute-start(bf16[256,1280]{1,0:T(8,128)(2,1)S(1)} %get-tuple-element.31.refs_0_), channel_id=1, source_target_pairs={{0,4},{1,29},{4,0},{5,9},{8,12},{9,5},{12,8},{13,17},{16,20},{17,1... | collective-permute-start | bytes 1966088 | tf_op jit(solution)/shard_map/ppermute | solution.py:321
  35.9 22.2 %all-to-all-start = ((bf16[8,320,128]{2,1,0:T(8,128)(2,1)}), bf16[8,320,128]{2,1,0:T(8,128)(2,1)S(1)}, u32[]{:S(2)}, u32[]{:S(2)}) async-start(bf16[8,320,128]{2,1,0:T(8,128)(2,1)} %shard_map.71.pieces_hbm), calls=%async_computation | async-start | bytes 1310720 | tf_op jit(solution)/shard_map/all_to_all | solution.py:398
  43.0 1.0 copy-start.2
  44.1 10.4 %collective-permute-start.6 = (bf16[320,128]{1,0:T(8,128)(2,1)S(1)}, bf16[320,128]{1,0:T(8,128)(2,1)S(1)}, u32[]{:S(2)}, u32[]{:S(2)}) collective-permute-start(bf16[320,128]{1,0:T(8,128)(2,1)S(1)} %get-tuple-element.36), channel_id=1, source_target_pairs={{128,132},{129,157},{132,128},{133,137},{136,140},{137,133},{140,1... | collective-permute-start | bytes 245768 | tf_op jit(solution)/shard_map/ppermute | solution.py:321
  47.4 7.0 %collective-permute-start.7 = (bf16[320,128]{1,0:T(8,128)(2,1)S(1)}, bf16[320,128]{1,0:T(8,128)(2,1)S(1)}, u32[]{:S(2)}, u32[]{:S(2)}) collective-permute-start(bf16[320,128]{1,0:T(8,128)(2,1)S(1)} %get-tuple-element.37), channel_id=1, source_target_pairs={{128,160},{129,225},{132,164},{133,229},{136,168},{137,233},{140,1... | collective-permute-start | bytes 245768 | tf_op jit(solution)/shard_map/ppermute | solution.py:321
  50.8 7.2 %collective-permute-start.8 = (bf16[320,128]{1,0:T(8,128)(2,1)S(1)}, bf16[320,128]{1,0:T(8,128)(2,1)S(1)}, u32[]{:S(2)}, u32[]{:S(2)}) collective-permute-start(bf16[320,128]{1,0:T(8,128)(2,1)S(1)} %get-tuple-element.38), channel_id=1, source_target_pairs={{128,164},{129,253},{132,160},{133,233},{136,172},{137,229},{140,1... | collective-permute-start | bytes 245768 | tf_op jit(solution)/shard_map/ppermute | solution.py:321
  53.4 0.6 copy-start.4
  58.1 0.9 copy-start.5
  61.0 10.1 %collective-permute-start.9 = (bf16[128,16,128]{2,1,0:T(8,128)(2,1)S(1)}, bf16[128,16,128]{2,1,0:T(8,128)(2,1)S(1)}, u32[]{:S(2)}, u32[]{:S(2)}) collective-permute-start(bf16[128,16,128]{2,1,0:T(8,128)(2,1)S(1)} %get-tuple-element.41), channel_id=1, source_target_pairs={{0,1},{1,0},{2,3},{3,2},{4,5},{5,4},{6,7},{7,6},{8,9},{9,8},{10,11... | collective-permute-start | bytes 1572872 | tf_op jit(solution)/shard_map/ppermute | solution.py:424

commit v8 on v7

--- a/solution.py
+++ b/solution.py
@@ -17,7 +17,7 @@
 COST = 50_000_000_000
 PIECE = 320
 SHARE = 16
-TAIL = C + 8
+TAIL = C + 48
 PARAMS = pltpu.CompilerParams(vmem_limit_bytes=40 * 1024 * 1024)
 WHOLE = pltpu.CompilerParams(vmem_limit_bytes=52 * 1024 * 1024)
 MOST = pltpu.CompilerParams(vmem_limit_bytes=51 * 1024 * 1024)
@@ -247,19 +247,19 @@
     zeroth = core == 0
     main_ref[...] = jnp.where(zeroth, first, second)
     tail_ref[...] = jnp.where(zeroth, lower, upper)
-    main[...] = jnp.where(zeroth, second, first)
+    main[:C] = jnp.where(zeroth, second, first)
     tail[:C] = jnp.where(zeroth, upper, lower)
     tail[C:] = jnp.zeros((TAIL - C, 128), jnp.float32)
     pack(main, tail, staged)
-    away_ref[...] = staged[...].astype(jnp.bfloat16).reshape(LANES, SHARE, 128)
+    away_ref[...] = staged[: LANES * SHARE].astype(jnp.bfloat16).reshape(LANES, SHARE, 128)
 
 
 def pair_kernel(main_ref, tail_ref, other_ref, shares_ref, main, tail, staged):
-    main[...] = main_ref[...]
+    main[:C] = main_ref[...]
     tail[:C] = tail_ref[...]
     tail[C:] = jnp.zeros((TAIL - C, 128), jnp.float32)
     pack(main, tail, staged)
-    total = staged[...].reshape(LANES, SHARE, 128) + other_ref[...].astype(jnp.float32)
+    total = staged[: LANES * SHARE].reshape(LANES, SHARE, 128) + other_ref[...].astype(jnp.float32)
     shares_ref[...] = total.astype(jnp.bfloat16)
 
 
@@ -399,9 +399,9 @@
         pieces, ("section",) + DP, 0, 0, axis_index_groups=squares(), tiled=True
     )
     packed = [
-        pltpu.VMEM((C, 128), jnp.float32),
         pltpu.VMEM((TAIL, 128), jnp.float32),
-        pltpu.VMEM((LANES * SHARE, 128), jnp.float32),
+        pltpu.VMEM((TAIL, 128), jnp.float32),
+        pltpu.VMEM((LANES * SHARE + SHARE, 128), jnp.float32),
     ]
     share = jax.ShapeDtypeStruct((LANES, SHARE, 128), jnp.bfloat16)
     own = pl.pallas_call(
@@ -436,7 +436,7 @@
         out_shape=jax.ShapeDtypeStruct((C // LANES, 1, C), jnp.float32),
         in_specs=[VMEM],
         out_specs=VMEM,
-        scratch_shapes=[pltpu.VMEM((12, 128), jnp.float32)],
+        scratch_shapes=[pltpu.VMEM((40, 128), jnp.float32)],
         compiler_params=PARAMS,
     )(shares)
     return (outs, jnp.transpose(gradient, (1, 0, 2)))

time: 98 us -> 98.1 us (level)
  no operation moved by 1% of the time
where the time goes in v8:
time: 98.1 us; the launch traced here: 97.5 us
  starting transfers between devices  32.6 us (33%)
  blocking collectives  25 us (25%)
  Pallas kernels  17.4 us (18%)
  waiting for transfers between devices  17 us (17%)
  local copies, waits for them, and re-layouts  4.81 us (5%)
    all_to_all x1, blocking collectives, local(): shares = lax.all_to_all(shares, DP, 0, 0, tiled=True)  25 us
    ppermute x6, starting transfers between devices, exchange(): return lax.ppermute(block, ('section', 'y', 'z', 'core'), route)  12.9 us
    ppermute x2, waiting for transfers between devices, local(): received = [lax.ppermute(rows, 'section', [(0, 1)]) for rows in sent]  11.4 us
    pallas_call x2, Pallas kernels, up(): pl.pallas_call(functools.partial(up_kernel, number), out_shape=(whole, bo...  8.81 us
    ppermute x1, starting transfers between devices, local(): other = lax.ppermute(away, 'core', [(0, 1), (1, 0)])  8.54 us
    all_to_all x1, starting transfers between devices, local(): lax.all_to_all(pieces, ('section',) + DP, 0, 0, axis_index_groups=squares...  7.08 us
    unnamed x18, local copies, waits for them, and re-layouts  4.81 us
    ppermute x6, waiting for transfers between devices, exchange(): return lax.ppermute(block, ('section', 'y', 'z', 'core'), route)  4.02 us
  transfers between devices with their start and end apart: 11, of which 4 were waited for; matrix products, arithmetic and copies ran while one was open for 0% of the time, Pallas kernels for 10%

profile of v8, /device:TPU:6, one launch (start us, length us, event | category | flops | bytes accessed | tf_op | source)
XLA Modules:
  0.0 97.5 jit_solution(5631054151958662030)
XLA Ops:
  0.7 0.9 copy-done.3
  1.6 0.7 copy-done.6
  2.3 0.7 copy-done.8
  3.0 3.9 %shard_map.68 = (bf16[128,1280]{1,0:T(8,128)(2,1)S(1)}, bf16[128,1280]{1,0:T(8,128)(2,1)S(1)}, bf16[128,1280]{1,0:T(8,128)(2,1)S(1)}, bf16[128,1280]{1,0:T(8,128...) custom-call(s32[2,16]{1,0:T(2,128)S(1)} %copy-done.8, bf16[1,2,128,1280]{3,2,1,0:T(8,128)(2,1)} %refs_2_.3, ...), custom_call_target="tpu_custom_call" | custom-call | tf_op jit(solution)/shard_map/pallas_call | solution.py:327
  6.9 1.3 %collective-permute-start.1 = (bf16[128,1280]{1,0:T(8,128)(2,1)S(1)}, bf16[128,1280]{1,0:T(8,128)(2,1)S(1)}, u32[]{:S(2)}, u32[]{:S(2)}) collective-permute-start(bf16[128,1280]{1,0:T(8,128)(2,1)S(1)} %get-tuple-element.26.refs_5_), channel_id=1, source_target_pairs={{0,128},{1,129},{2,130},{3,131},{4,132},{5,133},{6,134},{7,135},{8... | collective-permute-start | bytes 983048 | tf_op jit(solution)/shard_map/ppermute | solution.py:346
  8.2 1.3 %collective-permute-start = (bf16[128,1280]{1,0:T(8,128)(2,1)S(1)}, bf16[128,1280]{1,0:T(8,128)(2,1)S(1)}, u32[]{:S(2)}, u32[]{:S(2)}) collective-permute-start(bf16[128,1280]{1,0:T(8,128)(2,1)S(1)} %get-tuple-element.23.refs_5_), channel_id=1, source_target_pairs={{0,128},{1,129},{2,130},{3,131},{4,132},{5,133},{6,134},{7,135},{8... | collective-permute-start | bytes 983048 | tf_op jit(solution)/shard_map/ppermute | solution.py:346
  9.5 11.4 %collective-permute-done.1.refs_1_ = bf16[128,1280]{1,0:T(8,128)(2,1)S(1)} collective-permute-done((bf16[128,1280]{1,0:T(8,128)(2,1)S(1)}, bf16[128,1280]{1,0:T(8,128)(2,1)S(1)}, u32[]{:S(2)}, u32[]{:S(2)}) %collective-permute-start.1) | collective-permute-done | bytes 327712 | tf_op jit(solution)/shard_map/ppermute | solution.py:346
  20.9 4.4 %shard_map.69 = (bf16[1,2,128,1280]{3,2,1,0:T(8,128)(2,1)}, bf16[256,1280]{1,0:T(8,128)(2,1)S(1)}, bf16[128,1280]{1,0:T(8,128)(2,1)S(1)}, bf16[128,1280]{1,0:T(8,128)(2,1)S(1)}) custom-call(f32[2,1,1280]{2,1,0:T(1,128)S(1)} %get-tuple-element.22.refs_0_, bf16[128,1280]{1,0:T(8,128)(2,1)S(1)} %collective-permute-done.1.refs_1_, ...), custom_call_target="tpu_custom_call" | custom-call | flops 2000000000 | bytes 4000000 | tf_op jit(solution)/shard_map/pallas_call | solution.py:352
  25.3 1.5 %collective-permute-start.5 = (bf16[128,1280]{1,0:T(8,128)(2,1)S(1)}, bf16[128,1280]{1,0:T(8,128)(2,1)S(1)}, u32[]{:S(2)}, u32[]{:S(2)}) collective-permute-start(bf16[128,1280]{1,0:T(8,128)(2,1)S(1)} %get-tuple-element.32), channel_id=1, source_target_pairs={{128,0},{129,1},{130,2},{131,3},{132,4},{133,5},{134,6},{135,7},{1... | collective-permute-start | bytes 983048 | tf_op jit(solution)/shard_map/ppermute | solution.py:374
  26.8 4.4 %shard_map.70 = (bf16[1,2,128,1280]{3,2,1,0:T(8,128)(2,1)}, bf16[256,1280]{1,0:T(8,128)(2,1)S(1)}, bf16[128,1280]{1,0:T(8,128)(2,1)S(1)}, bf16[128,1280]{1,0:T(8,128)(2,1)S(1)}) custom-call(f32[2,1,1280]{2,1,0:T(1,128)S(1)} %get-tuple-element.22.refs_0_, ...), custom_call_target="tpu_custom_call", output_to_operand_aliasing={{0}: (7, {}), {1}: (8, {})} | custom-call | flops 2000000000 | bytes 4000000 | tf_op jit(solution)/shard_map/pallas_call | solution.py:352
  31.2 3.0 %collective-permute-start.4 = (bf16[256,1280]{1,0:T(8,128)(2,1)S(1)}, bf16[256,1280]{1,0:T(8,128)(2,1)S(1)}, u32[]{:S(2)}, u32[]{:S(2)}) collective-permute-start(bf16[256,1280]{1,0:T(8,128)(2,1)S(1)} %get-tuple-element.31.refs_0_), channel_id=1, source_target_pairs={{0,36},{1,125},{4,32},{5,105},{8,44},{9,101},{12,40},{13,113},{16,... | collective-permute-start | bytes 1966088 | tf_op jit(solution)/shard_map/ppermute | solution.py:321
  34.3 0.5 collective-permute-start.3
  34.7 0.2 collective-permute-start.2
  34.9 0.0 collective-permute-done.5.returned_ref
  34.9 1.0 shard_map.71.pieces_hbm
  35.9 7.1 %all-to-all-start = ((bf16[8,320,128]{2,1,0:T(8,128)(2,1)}), bf16[8,320,128]{2,1,0:T(8,128)(2,1)S(1)}, u32[]{:S(2)}, u32[]{:S(2)}) async-start(bf16[8,320,128]{2,1,0:T(8,128)(2,1)} %shard_map.71.pieces_hbm), calls=%async_computation | async-start | bytes 1310720 | tf_op jit(solution)/shard_map/all_to_all | solution.py:398
  43.0 1.0 copy-done.2
  44.0 0.1 shard_map.73
  44.1 3.4 %collective-permute-start.6 = (bf16[320,128]{1,0:T(8,128)(2,1)S(1)}, bf16[320,128]{1,0:T(8,128)(2,1)S(1)}, u32[]{:S(2)}, u32[]{:S(2)}) collective-permute-start(bf16[320,128]{1,0:T(8,128)(2,1)S(1)} %get-tuple-element.36), channel_id=1, source_target_pairs={{128,132},{129,157},{132,128},{133,137},{136,140},{137,133},{140,1... | collective-permute-start | bytes 245768 | tf_op jit(solution)/shard_map/ppermute | solution.py:321
  47.4 3.4 %collective-permute-start.7 = (bf16[320,128]{1,0:T(8,128)(2,1)S(1)}, bf16[320,128]{1,0:T(8,128)(2,1)S(1)}, u32[]{:S(2)}, u32[]{:S(2)}) collective-permute-start(bf16[320,128]{1,0:T(8,128)(2,1)S(1)} %get-tuple-element.37), channel_id=1, source_target_pairs={{128,160},{129,225},{132,164},{133,229},{136,168},{137,233},{140,1... | collective-permute-start | bytes 245768 | tf_op jit(solution)/shard_map/ppermute | solution.py:321
  50.8 2.5 %collective-permute-start.8 = (bf16[320,128]{1,0:T(8,128)(2,1)S(1)}, bf16[320,128]{1,0:T(8,128)(2,1)S(1)}, u32[]{:S(2)}, u32[]{:S(2)}) collective-permute-start(bf16[320,128]{1,0:T(8,128)(2,1)S(1)} %get-tuple-element.38), channel_id=1, source_target_pairs={{128,164},{129,253},{132,160},{133,233},{136,172},{137,229},{140,1... | collective-permute-start | bytes 245768 | tf_op jit(solution)/shard_map/ppermute | solution.py:321
  53.3 0.1 shard_map.72.refs_5_
  53.4 0.6 copy-done.4
  54.1 0.4 collective-permute-done.6.refs_6_
  54.4 3.6 %collective-permute-done.8.refs_8_ = bf16[320,128]{1,0:T(8,128)(2,1)S(1)} collective-permute-done((bf16[320,128]{1,0:T(8,128)(2,1)S(1)}, bf16[320,128]{1,0:T(8,128)(2,1)S(1)}, u32[]{:S(2)}, u32[]{:S(2)}) %collective-permute-start.8) | collective-permute-done | bytes 81952 | tf_op jit(solution)/shard_map/ppermute | solution.py:321
  58.1 0.9 copy-done.5
  59.0 2.1 %shard_map.74 = (f32[1280,128]{1,0:T(8,128)S(1)}, f32[1280,128]{1,0:T(8,128)S(1)}, bf16[128,16,128]{2,1,0:T(8,128)(2,1)S(1)}) custom-call(bf16[256,1280]{1,0:T(8,128)(2,1)S(1)} %get-tuple-element.31.refs_0_, bf16[256,1280]{1,0:T(8,128)(2,1)S(1)} %collective-permute-done.2.refs_0_.refs_1_, bf16[256,1280]{1,0:T(8,128)(2,1)S(1)} %collective-permute-done.3.refs_1_.refs_2_, ...), custom_call_target="tpu_custom_call" | custom-call | tf_op jit(solution)/shard_map/pallas_call | solution.py:416
  61.1 8.5 %collective-permute-start.9 = (bf16[128,16,128]{2,1,0:T(8,128)(2,1)S(1)}, bf16[128,16,128]{2,1,0:T(8,128)(2,1)S(1)}, u32[]{:S(2)}, u32[]{:S(2)}) collective-permute-start(bf16[128,16,128]{2,1,0:T(8,128)(2,1)S(1)} %get-tuple-element.41), channel_id=1, source_target_pairs={{0,1},{1,0},{2,3},{3,2},{4,5},{5,4},{6,7},{7,6},{8,9},{9,8},{10,11... | collective-permute-start | bytes 1572872 | tf_op jit(solution)/shard_map/ppermute | solution.py:424
  69.6 1.5 %collective-permute-done.9.other_ref = bf16[128,16,128]{2,1,0:T(8,128)(2,1)S(1)} collective-permute-done((bf16[128,16,128]{2,1,0:T(8,128)(2,1)S(1)}, bf16[128,16,128]{2,1,0:T(8,128)(2,1)S(1)}, u32[]{:S(2)}, u32[]{:S(2)}) %collective-permute-start.9) | collective-permute-done | bytes 524320 | tf_op jit(solution)/shard_map/ppermute | solution.py:424
  71.1 0.6 shard_map.75
  71.7 25.0 %all_to_all.10.shares_ref = bf16[128,16,128]{2,1,0:T(8,128)(2,1)S(1)} all-to-all(bf16[128,16,128]{2,1,0:T(8,128)(2,1)S(1)} %shard_map.75), channel_id=1, replica_groups=mesh['section'=2,'y'=4,'z'=8,'x'=2,'core'=2] {'y','z','x','core'}, dimensions={0} | all-to-all | bytes 1048576 | tf_op jit(solution)/shard_map/all_to_all | solution.py:433
  96.8 0.8 shard_map.76
  (18 shorter events, 0.0 us)
Async XLA Ops:
  0.6 20.3 %copy-start = (bf16[1,2,128,1280]{3,2,1,0:T(8,128)(2,1)S(1)}, bf16[1,2,128,1280]{3,2,1,0:T(8,128)(2,1)}, u32[]{:S(2)}) copy-start(bf16[1,2,128,1280]{3,2,1,0:T(8,128)(2,1)} %refs_2_.3) | copy-start | bytes 1966084
  0.6 1.0 copy-start.3
  1.6 0.7 copy-start.6
  2.3 0.7 copy-start.8
  3.0 17.9 %copy-start.7 = (f32[1,1280]{1,0:T(1,128)S(1)}, f32[1,1280]{1,0:T(1,128)}, u32[]{:S(2)}) copy-start(f32[1,1280]{1,0:T(1,128)} %refs_4_.3) | copy-start | bytes 15364
  6.9 14.0 %collective-permute-start.1 = (bf16[128,1280]{1,0:T(8,128)(2,1)S(1)}, bf16[128,1280]{1,0:T(8,128)(2,1)S(1)}, u32[]{:S(2)}, u32[]{:S(2)}) collective-permute-start(bf16[128,1280]{1,0:T(8,128)(2,1)S(1)} %get-tuple-element.26.refs_5_), channel_id=1, source_target_pairs={{0,128},{1,129},{2,130},{3,131},{4,132},{5,133},{6,134},{7,135},{8... | collective-permute-start | bytes 983048 | tf_op jit(solution)/shard_map/ppermute | solution.py:346
  8.2 18.6 %collective-permute-start = (bf16[128,1280]{1,0:T(8,128)(2,1)S(1)}, bf16[128,1280]{1,0:T(8,128)(2,1)S(1)}, u32[]{:S(2)}, u32[]{:S(2)}) collective-permute-start(bf16[128,1280]{1,0:T(8,128)(2,1)S(1)} %get-tuple-element.23.refs_5_), channel_id=1, source_target_pairs={{0,128},{1,129},{2,130},{3,131},{4,132},{5,133},{6,134},{7,135},{8... | collective-permute-start | bytes 983048 | tf_op jit(solution)/shard_map/ppermute | solution.py:346
  25.3 5.9 %copy-start.1 = (bf16[128,1280]{1,0:T(8,128)(2,1)}, bf16[128,1280]{1,0:T(8,128)(2,1)S(1)}, u32[]{:S(2)}) copy-start(bf16[128,1280]{1,0:T(8,128)(2,1)S(1)} %get-tuple-element.35.cot_ref) | copy-start | bytes 983044
  25.3 9.6 %collective-permute-start.5 = (bf16[128,1280]{1,0:T(8,128)(2,1)S(1)}, bf16[128,1280]{1,0:T(8,128)(2,1)S(1)}, u32[]{:S(2)}, u32[]{:S(2)}) collective-permute-start(bf16[128,1280]{1,0:T(8,128)(2,1)S(1)} %get-tuple-element.32), channel_id=1, source_target_pairs={{128,0},{129,1},{130,2},{131,3},{132,4},{133,5},{134,6},{135,7},{1... | collective-permute-start | bytes 983048 | tf_op jit(solution)/shard_map/ppermute | solution.py:374
  31.2 19.6 %collective-permute-start.4 = (bf16[256,1280]{1,0:T(8,128)(2,1)S(1)}, bf16[256,1280]{1,0:T(8,128)(2,1)S(1)}, u32[]{:S(2)}, u32[]{:S(2)}) collective-permute-start(bf16[256,1280]{1,0:T(8,128)(2,1)S(1)} %get-tuple-element.31.refs_0_), channel_id=1, source_target_pairs={{0,36},{1,125},{4,32},{5,105},{8,44},{9,101},{12,40},{13,113},{16,... | collective-permute-start | bytes 1966088 | tf_op jit(solution)/shard_map/ppermute | solution.py:321
  34.3 19.1 %collective-permute-start.3 = (bf16[256,1280]{1,0:T(8,128)(2,1)S(1)}, bf16[256,1280]{1,0:T(8,128)(2,1)S(1)}, u32[]{:S(2)}, u32[]{:S(2)}) collective-permute-start(bf16[256,1280]{1,0:T(8,128)(2,1)S(1)} %get-tuple-element.31.refs_0_), channel_id=1, source_target_pairs={{0,32},{1,97},{4,36},{5,101},{8,40},{9,105},{12,44},{13,109},{16,4... | collective-permute-start | bytes 1966088 | tf_op jit(solution)/shard_map/ppermute | solution.py:321
  34.7 18.6 %collective-permute-start.2 = (bf16[256,1280]{1,0:T(8,128)(2,1)S(1)}, bf16[256,1280]{1,0:T(8,128)(2,1)S(1)}, u32[]{:S(2)}, u32[]{:S(2)}) collective-permute-start(bf16[256,1280]{1,0:T(8,128)(2,1)S(1)} %get-tuple-element.31.refs_0_), channel_id=1, source_target_pairs={{0,4},{1,29},{4,0},{5,9},{8,12},{9,5},{12,8},{13,17},{16,20},{17,1... | collective-permute-start | bytes 1966088 | tf_op jit(solution)/shard_map/ppermute | solution.py:321
  35.9 22.2 %all-to-all-start = ((bf16[8,320,128]{2,1,0:T(8,128)(2,1)}), bf16[8,320,128]{2,1,0:T(8,128)(2,1)S(1)}, u32[]{:S(2)}, u32[]{:S(2)}) async-start(bf16[8,320,128]{2,1,0:T(8,128)(2,1)} %shard_map.71.pieces_hbm), calls=%async_computation | async-start | bytes 1310720 | tf_op jit(solution)/shard_map/all_to_all | solution.py:398
  43.0 1.0 copy-start.2
  44.1 10.4 %collective-permute-start.6 = (bf16[320,128]{1,0:T(8,128)(2,1)S(1)}, bf16[320,128]{1,0:T(8,128)(2,1)S(1)}, u32[]{:S(2)}, u32[]{:S(2)}) collective-permute-start(bf16[320,128]{1,0:T(8,128)(2,1)S(1)} %get-tuple-element.36), channel_id=1, source_target_pairs={{128,132},{129,157},{132,128},{133,137},{136,140},{137,133},{140,1... | collective-permute-start | bytes 245768 | tf_op jit(solution)/shard_map/ppermute | solution.py:321
  47.4 7.0 %collective-permute-start.7 = (bf16[320,128]{1,0:T(8,128)(2,1)S(1)}, bf16[320,128]{1,0:T(8,128)(2,1)S(1)}, u32[]{:S(2)}, u32[]{:S(2)}) collective-permute-start(bf16[320,128]{1,0:T(8,128)(2,1)S(1)} %get-tuple-element.37), channel_id=1, source_target_pairs={{128,160},{129,225},{132,164},{133,229},{136,168},{137,233},{140,1... | collective-permute-start | bytes 245768 | tf_op jit(solution)/shard_map/ppermute | solution.py:321
  50.8 7.2 %collective-permute-start.8 = (bf16[320,128]{1,0:T(8,128)(2,1)S(1)}, bf16[320,128]{1,0:T(8,128)(2,1)S(1)}, u32[]{:S(2)}, u32[]{:S(2)}) collective-permute-start(bf16[320,128]{1,0:T(8,128)(2,1)S(1)} %get-tuple-element.38), channel_id=1, source_target_pairs={{128,164},{129,253},{132,160},{133,233},{136,172},{137,229},{140,1... | collective-permute-start | bytes 245768 | tf_op jit(solution)/shard_map/ppermute | solution.py:321
  53.4 0.6 copy-start.4
  58.1 0.9 copy-start.5
  61.1 10.1 %collective-permute-start.9 = (bf16[128,16,128]{2,1,0:T(8,128)(2,1)S(1)}, bf16[128,16,128]{2,1,0:T(8,128)(2,1)S(1)}, u32[]{:S(2)}, u32[]{:S(2)}) collective-permute-start(bf16[128,16,128]{2,1,0:T(8,128)(2,1)S(1)} %get-tuple-element.41), channel_id=1, source_target_pairs={{0,1},{1,0},{2,3},{3,2},{4,5},{5,4},{6,7},{7,6},{8,9},{9,8},{10,11... | collective-permute-start | bytes 1572872 | tf_op jit(solution)/shard_map/ppermute | solution.py:424

commit v9 on v8

--- a/solution.py
+++ b/solution.py
@@ -62,8 +62,8 @@
             )
         )
     ]
-    for copy in copies:
-        copy.start()
+    for at in (0, 4, 1, 2, 3):
+        copies[at].start()
     copies[0].wait()
     copies[1].wait()
     for number in range(MICRO):
@@ -203,17 +203,16 @@
         refs[turn - 1][...] = refs[3][lax.bitwise_xor(own, turn)]
 
 
-def own_kernel(cot_ref, *refs):
-    own_ref, pieces_ref = refs[3:]
-    store_pieces(pieces_ref, 0, cot_ref[...].astype(jnp.float32))
-    own_ref[...] = pieces_ref[own_quarter()]
+def gathered_kernel(*refs):
+    refs[-1][...] = jnp.zeros_like(refs[-1])
 
 
 def weight_kernel(*refs):
-    active_refs, piece_ref, cot_refs = refs[:4], refs[4], refs[5:9]
-    main_ref, tail_ref, away_ref, main, tail, staged = refs[9:]
+    active_refs, piece_ref, cot_ref, cot_refs = refs[:4], refs[4], refs[5], refs[6:9]
+    main_ref, tail_ref, away_ref, main, tail, staged, own_ref = refs[10:]
     down, core = lax.axis_index("section") == 0, lax.axis_index("core")
     own = own_quarter()
+    store_pieces(own_ref, 0, cot_ref[...].astype(jnp.float32))
     low = lax.broadcasted_iota(jnp.int32, (ROWS // 2, 128), 1) < 64
     zero = jnp.zeros((ROWS // 2, 128), jnp.bfloat16)
     product = None
@@ -222,7 +221,8 @@
         for number in range(MICRO):
             piece = piece_ref[4 * number + lax.bitwise_xor(own, turn)]
             if number == 0:
-                piece = jnp.where(down, piece, cot_refs[turn][...])
+                cot = cot_refs[turn - 1][...] if turn else own_ref[own]
+                piece = jnp.where(down, piece, cot)
             end = piece[2 * ROWS :]
             right.append(
                 jnp.concatenate(
@@ -404,23 +404,22 @@
         pltpu.VMEM((LANES * SHARE + SHARE, 128), jnp.float32),
     ]
     share = jax.ShapeDtypeStruct((LANES, SHARE, 128), jnp.bfloat16)
-    own = pl.pallas_call(
-        own_kernel,
-        out_shape=piece,
-        in_specs=[VMEM] + [HBM] * 3,
+    gathered = pl.pallas_call(
+        gathered_kernel,
+        out_shape=jax.ShapeDtypeStruct((8, 128), jnp.float32),
+        in_specs=[HBM] * 3,
         out_specs=VMEM,
-        scratch_shapes=[pltpu.VMEM((4, PIECE, 128), jnp.bfloat16)],
         compiler_params=PARAMS,
         cost_estimate=pl.CostEstimate(flops=COST, bytes_accessed=2_000_000, transcendentals=0),
-    )(cot_0, *others)
+    )(*others)
     main, tail, away = pl.pallas_call(
         weight_kernel,
         out_shape=(jax.ShapeDtypeStruct((C, 128), jnp.float32),) * 2 + (share,),
-        in_specs=[VMEM] * 9,
+        in_specs=[VMEM] * 9 + [HBM],
         out_specs=(VMEM,) * 3,
-        scratch_shapes=packed,
+        scratch_shapes=packed + [pltpu.VMEM((4, PIECE, 128), jnp.bfloat16)],
         compiler_params=PARAMS,
-    )(actives, *others, arrived, own, *turned)
+    )(actives, *others, arrived, cot_0, *turned, gathered)
     other = lax.ppermute(away, "core", [(0, 1), (1, 0)])
     shares = pl.pallas_call(
         pair_kernel,

time: 98.1 us -> 97.5 us (level)
  local copies, waits for them, and re-layouts: 4.81 us -> 2.32 us
  Pallas kernels: 17.4 us -> 18.4 us
    unnamed x18 -> x10, local copies, waits for them, and re-layouts: 4.81 us -> 2.32 us
    pallas_call x1, Pallas kernels: 2.09 us -> 3.26 us  [local(): pl.pallas_call(weight_kernel, out_shape=(jax.ShapeDtypeStruct((C, 128), j...]
  transfers between devices with their start and end apart: 11 -> 11, of which waited for: 4 -> 5; matrix products, arithmetic and copies ran while one was open for 0% -> 0% of each run, Pallas kernels for 10% -> 10%
where the time goes in v9:
time: 97.5 us; the launch traced here: 97 us
  starting transfers between devices  32.6 us (33%)
  blocking collectives  25 us (26%)
  Pallas kernels  18.4 us (19%)
  waiting for transfers between devices  17.8 us (18%)
  local copies, waits for them, and re-layouts  2.32 us (2%)
    all_to_all x1, blocking collectives, local(): shares = lax.all_to_all(shares, DP, 0, 0, tiled=True)  25 us
    ppermute x6, starting transfers between devices, exchange(): return lax.ppermute(block, ('section', 'y', 'z', 'core'), route)  12.9 us
    ppermute x2, waiting for transfers between devices, local(): received = [lax.ppermute(rows, 'section', [(0, 1)]) for rows in sent]  11.5 us
    ppermute x1, starting transfers between devices, local(): other = lax.ppermute(away, 'core', [(0, 1), (1, 0)])  8.58 us
    pallas_call x2, Pallas kernels, up(): pl.pallas_call(functools.partial(up_kernel, number), out_shape=(whole, bo...  8.58 us
    all_to_all x1, starting transfers between devices, local(): lax.all_to_all(pieces, ('section',) + DP, 0, 0, axis_index_groups=squares...  7.08 us
    ppermute x6, waiting for transfers between devices, exchange(): return lax.ppermute(block, ('section', 'y', 'z', 'core'), route)  4.73 us
    pallas_call x1, Pallas kernels, local(): pl.pallas_call(down_kernel, out_shape=(half,) * 4 + (jax.ShapeDtypeStruct...  4.16 us
  transfers between devices with their start and end apart: 11, of which 5 were waited for; matrix products, arithmetic and copies ran while one was open for 0% of the time, Pallas kernels for 10%

profile of v9, /device:TPU:6, one launch (start us, length us, event | category | flops | bytes accessed | tf_op | source)
XLA Modules:
  0.0 97.0 jit_solution(16128670442558602998)
XLA Ops:
  0.7 0.9 copy-done.1
  1.6 0.7 copy-done.2
  2.3 0.7 copy-done.4
  3.0 4.2 %shard_map.68 = (bf16[128,1280]{1,0:T(8,128)(2,1)S(1)}, bf16[128,1280]{1,0:T(8,128)(2,1)S(1)}, bf16[128,1280]{1,0:T(8,128)(2,1)S(1)}, bf16[128,1280]{1,0:T(8,128...) custom-call(s32[2,16]{1,0:T(2,128)S(1)} %copy-done.4, bf16[1,2,128,1280]{3,2,1,0:T(8,128)(2,1)} %refs_2_.3, ...), custom_call_target="tpu_custom_call" | custom-call | tf_op jit(solution)/shard_map/pallas_call | solution.py:327
  7.1 1.3 %collective-permute-start.1 = (bf16[128,1280]{1,0:T(8,128)(2,1)S(1)}, bf16[128,1280]{1,0:T(8,128)(2,1)S(1)}, u32[]{:S(2)}, u32[]{:S(2)}) collective-permute-start(bf16[128,1280]{1,0:T(8,128)(2,1)S(1)} %get-tuple-element.26.refs_5_), channel_id=1, source_target_pairs={{0,128},{1,129},{2,130},{3,131},{4,132},{5,133},{6,134},{7,135},{8... | collective-permute-start | bytes 983048 | tf_op jit(solution)/shard_map/ppermute | solution.py:346
  8.4 1.3 %collective-permute-start = (bf16[128,1280]{1,0:T(8,128)(2,1)S(1)}, bf16[128,1280]{1,0:T(8,128)(2,1)S(1)}, u32[]{:S(2)}, u32[]{:S(2)}) collective-permute-start(bf16[128,1280]{1,0:T(8,128)(2,1)S(1)} %get-tuple-element.23.refs_5_), channel_id=1, source_target_pairs={{0,128},{1,129},{2,130},{3,131},{4,132},{5,133},{6,134},{7,135},{8... | collective-permute-start | bytes 983048 | tf_op jit(solution)/shard_map/ppermute | solution.py:346
  9.7 11.4 %collective-permute-done.1.refs_1_ = bf16[128,1280]{1,0:T(8,128)(2,1)S(1)} collective-permute-done((bf16[128,1280]{1,0:T(8,128)(2,1)S(1)}, bf16[128,1280]{1,0:T(8,128)(2,1)S(1)}, u32[]{:S(2)}, u32[]{:S(2)}) %collective-permute-start.1) | collective-permute-done | bytes 327712 | tf_op jit(solution)/shard_map/ppermute | solution.py:346
  21.1 4.3 %shard_map.69 = (bf16[1,2,128,1280]{3,2,1,0:T(8,128)(2,1)}, bf16[256,1280]{1,0:T(8,128)(2,1)}, bf16[128,1280]{1,0:T(8,128)(2,1)S(1)}, bf16[128,1280]{1,0:T(8,128)(2,1)S(1)}) custom-call(f32[2,1,1280]{2,1,0:T(1,128)S(1)} %get-tuple-element.22.refs_0_, bf16[128,1280]{1,0:T(8,128)(2,1)S(1)} %collective-permute-done.1.refs_1_, ...), custom_call_target="tpu_custom_call" | custom-call | flops 2000000000 | bytes 4000000 | tf_op jit(solution)/shard_map/pallas_call | solution.py:352
  25.4 1.5 %collective-permute-start.5 = (bf16[128,1280]{1,0:T(8,128)(2,1)S(1)}, bf16[128,1280]{1,0:T(8,128)(2,1)S(1)}, u32[]{:S(2)}, u32[]{:S(2)}) collective-permute-start(bf16[128,1280]{1,0:T(8,128)(2,1)S(1)} %get-tuple-element.32), channel_id=1, source_target_pairs={{128,0},{129,1},{130,2},{131,3},{132,4},{133,5},{134,6},{135,7},{1... | collective-permute-start | bytes 983048 | tf_op jit(solution)/shard_map/ppermute | solution.py:374
  26.9 0.1 collective-permute-done.refs_1_
  27.0 4.3 %shard_map.70 = (bf16[1,2,128,1280]{3,2,1,0:T(8,128)(2,1)}, bf16[256,1280]{1,0:T(8,128)(2,1)}, bf16[128,1280]{1,0:T(8,128)(2,1)S(1)}, bf16[128,1280]{1,0:T(8,128)(2,1)S(1)}) custom-call(f32[2,1,1280]{2,1,0:T(1,128)S(1)} %get-tuple-element.22.refs_0_, ...), custom_call_target="tpu_custom_call", output_to_operand_aliasing={{0}: (7, {}), {1}: (8, {})} | custom-call | flops 2000000000 | bytes 4000000 | tf_op jit(solution)/shard_map/pallas_call | solution.py:352
  31.3 3.0 %collective-permute-start.4 = (bf16[256,1280]{1,0:T(8,128)(2,1)}, bf16[256,1280]{1,0:T(8,128)(2,1)S(1)}, u32[]{:S(2)}, u32[]{:S(2)}) collective-permute-start(bf16[256,1280]{1,0:T(8,128)(2,1)} %get-tuple-element.31.refs_0_), channel_id=1, source_target_pairs={{0,36},{1,125},{4,32},{5,105},{8,44},{9,101},{12,40},{13,113},{16,... | collective-permute-start | bytes 1966088 | tf_op jit(solution)/shard_map/ppermute | solution.py:321
  34.3 0.4 collective-permute-start.3
  34.8 0.2 collective-permute-start.2
  35.0 0.0 collective-permute-done.5.returned_ref
  35.0 1.0 %shard_map.71.pieces_hbm = bf16[8,320,128]{2,1,0:T(8,128)(2,1)} custom-call(bf16[128,1280]{1,0:T(8,128)(2,1)S(1)} %collective-permute-done.5.returned_ref, bf16[128,1280]{1,0:T(8,128)(2,1)S(1)} %get-tuple-element.33.cot_ref, bf16[128,1280]{1,0:T(8,128)(2,1)S(1)} %get-tuple-element.34.back_ref), custom_call_target="tpu_custom_call" | custom-call | flops 49999998976 | bytes 2000000 | tf_op jit(solution)/shard_map/pallas_call | solution.py:376
  36.0 7.1 %all-to-all-start = ((bf16[8,320,128]{2,1,0:T(8,128)(2,1)}), bf16[8,320,128]{2,1,0:T(8,128)(2,1)S(1)}, u32[]{:S(2)}, u32[]{:S(2)}) async-start(bf16[8,320,128]{2,1,0:T(8,128)(2,1)} %shard_map.71.pieces_hbm), calls=%async_computation | async-start | bytes 1310720 | tf_op jit(solution)/shard_map/all_to_all | solution.py:398
  43.1 0.1 shard_map.72
  43.2 3.4 %collective-permute-start.6 = (bf16[320,128]{1,0:T(8,128)(2,1)S(1)}, bf16[320,128]{1,0:T(8,128)(2,1)S(1)}, u32[]{:S(2)}, u32[]{:S(2)}) collective-permute-start(bf16[320,128]{1,0:T(8,128)(2,1)S(1)} %get-tuple-element.36), channel_id=1, source_target_pairs={{128,132},{129,157},{132,128},{133,137},{136,140},{137,133},{140,1... | collective-permute-start | bytes 245768 | tf_op jit(solution)/shard_map/ppermute | solution.py:321
  46.5 3.4 %collective-permute-start.7 = (bf16[320,128]{1,0:T(8,128)(2,1)S(1)}, bf16[320,128]{1,0:T(8,128)(2,1)S(1)}, u32[]{:S(2)}, u32[]{:S(2)}) collective-permute-start(bf16[320,128]{1,0:T(8,128)(2,1)S(1)} %get-tuple-element.37), channel_id=1, source_target_pairs={{128,160},{129,225},{132,164},{133,229},{136,168},{137,233},{140,1... | collective-permute-start | bytes 245768 | tf_op jit(solution)/shard_map/ppermute | solution.py:321
  49.9 0.0 collective-permute-done.4.refs_2_.refs_3_
  49.9 2.5 %collective-permute-start.8 = (bf16[320,128]{1,0:T(8,128)(2,1)S(1)}, bf16[320,128]{1,0:T(8,128)(2,1)S(1)}, u32[]{:S(2)}, u32[]{:S(2)}) collective-permute-start(bf16[320,128]{1,0:T(8,128)(2,1)S(1)} %get-tuple-element.38), channel_id=1, source_target_pairs={{128,164},{129,253},{132,160},{133,233},{136,172},{137,229},{140,1... | collective-permute-start | bytes 245768 | tf_op jit(solution)/shard_map/ppermute | solution.py:321
  52.4 0.0 collective-permute-done.3.refs_1_.refs_2_
  52.4 0.0 collective-permute-done.2.refs_0_.refs_1_
  52.4 2.3 %collective-permute-done.6.refs_6_ = bf16[320,128]{1,0:T(8,128)(2,1)S(1)} collective-permute-done((bf16[320,128]{1,0:T(8,128)(2,1)S(1)}, bf16[320,128]{1,0:T(8,128)(2,1)S(1)}, u32[]{:S(2)}, u32[]{:S(2)}) %collective-permute-start.6) | collective-permute-done | bytes 81952 | tf_op jit(solution)/shard_map/ppermute | solution.py:321
  54.7 2.5 %collective-permute-done.8.refs_8_ = bf16[320,128]{1,0:T(8,128)(2,1)S(1)} collective-permute-done((bf16[320,128]{1,0:T(8,128)(2,1)S(1)}, bf16[320,128]{1,0:T(8,128)(2,1)S(1)}, u32[]{:S(2)}, u32[]{:S(2)}) %collective-permute-start.8) | collective-permute-done | bytes 81952 | tf_op jit(solution)/shard_map/ppermute | solution.py:321
  57.2 3.3 %shard_map.74 = (f32[1280,128]{1,0:T(8,128)S(1)}, f32[1280,128]{1,0:T(8,128)S(1)}, bf16[128,16,128]{2,1,0:T(8,128)(2,1)S(1)}) custom-call(bf16[256,1280]{1,0:T(8,128)(2,1)} %get-tuple-element.31.refs_0_, bf16[256,1280]{1,0:T(8,128)(2,1)S(1)} %collective-permute-done.2.refs_0_.refs_1_, bf16[256,1280]{1,0:T(8,128)(2,1)S(1)} %collective-permute-done.3.refs_1_.refs_2_, ...), custom_call_target="tpu_custom_call" | custom-call | tf_op jit(solution)/shard_map/pallas_call | solution.py:415
  60.4 8.6 %collective-permute-start.9 = (bf16[128,16,128]{2,1,0:T(8,128)(2,1)S(1)}, bf16[128,16,128]{2,1,0:T(8,128)(2,1)S(1)}, u32[]{:S(2)}, u32[]{:S(2)}) collective-permute-start(bf16[128,16,128]{2,1,0:T(8,128)(2,1)S(1)} %get-tuple-element.41), channel_id=1, source_target_pairs={{0,1},{1,0},{2,3},{3,2},{4,5},{5,4},{6,7},{7,6},{8,9},{9,8},{10,11... | collective-permute-start | bytes 1572872 | tf_op jit(solution)/shard_map/ppermute | solution.py:423
  69.0 1.5 %collective-permute-done.9.other_ref = bf16[128,16,128]{2,1,0:T(8,128)(2,1)S(1)} collective-permute-done((bf16[128,16,128]{2,1,0:T(8,128)(2,1)S(1)}, bf16[128,16,128]{2,1,0:T(8,128)(2,1)S(1)}, u32[]{:S(2)}, u32[]{:S(2)}) %collective-permute-start.9) | collective-permute-done | bytes 524320 | tf_op jit(solution)/shard_map/ppermute | solution.py:423
  70.6 0.6 shard_map.75
  71.1 25.0 %all_to_all.10.shares_ref = bf16[128,16,128]{2,1,0:T(8,128)(2,1)S(1)} all-to-all(bf16[128,16,128]{2,1,0:T(8,128)(2,1)S(1)} %shard_map.75), channel_id=1, replica_groups=mesh['section'=2,'y'=4,'z'=8,'x'=2,'core'=2] {'y','z','x','core'}, dimensions={0} | all-to-all | bytes 1048576 | tf_op jit(solution)/shard_map/all_to_all | solution.py:432
  96.2 0.8 shard_map.76
  (10 shorter events, 0.0 us)
Async XLA Ops:
  0.6 20.5 %copy-start = (bf16[1,2,128,1280]{3,2,1,0:T(8,128)(2,1)S(1)}, bf16[1,2,128,1280]{3,2,1,0:T(8,128)(2,1)}, u32[]{:S(2)}) copy-start(bf16[1,2,128,1280]{3,2,1,0:T(8,128)(2,1)} %refs_2_.3) | copy-start | bytes 1966084
  0.6 1.0 copy-start.1
  1.6 0.7 copy-start.2
  2.3 0.7 copy-start.4
  3.0 18.2 %copy-start.3 = (f32[1,1280]{1,0:T(1,128)S(1)}, f32[1,1280]{1,0:T(1,128)}, u32[]{:S(2)}) copy-start(f32[1,1280]{1,0:T(1,128)} %refs_4_.3) | copy-start | bytes 15364
  7.1 14.0 %collective-permute-start.1 = (bf16[128,1280]{1,0:T(8,128)(2,1)S(1)}, bf16[128,1280]{1,0:T(8,128)(2,1)S(1)}, u32[]{:S(2)}, u32[]{:S(2)}) collective-permute-start(bf16[128,1280]{1,0:T(8,128)(2,1)S(1)} %get-tuple-element.26.refs_5_), channel_id=1, source_target_pairs={{0,128},{1,129},{2,130},{3,131},{4,132},{5,133},{6,134},{7,135},{8... | collective-permute-start | bytes 983048 | tf_op jit(solution)/shard_map/ppermute | solution.py:346
  8.4 18.6 %collective-permute-start = (bf16[128,1280]{1,0:T(8,128)(2,1)S(1)}, bf16[128,1280]{1,0:T(8,128)(2,1)S(1)}, u32[]{:S(2)}, u32[]{:S(2)}) collective-permute-start(bf16[128,1280]{1,0:T(8,128)(2,1)S(1)} %get-tuple-element.23.refs_5_), channel_id=1, source_target_pairs={{0,128},{1,129},{2,130},{3,131},{4,132},{5,133},{6,134},{7,135},{8... | collective-permute-start | bytes 983048 | tf_op jit(solution)/shard_map/ppermute | solution.py:346
  25.4 9.6 %collective-permute-start.5 = (bf16[128,1280]{1,0:T(8,128)(2,1)S(1)}, bf16[128,1280]{1,0:T(8,128)(2,1)S(1)}, u32[]{:S(2)}, u32[]{:S(2)}) collective-permute-start(bf16[128,1280]{1,0:T(8,128)(2,1)S(1)} %get-tuple-element.32), channel_id=1, source_target_pairs={{128,0},{129,1},{130,2},{131,3},{132,4},{133,5},{134,6},{135,7},{1... | collective-permute-start | bytes 983048 | tf_op jit(solution)/shard_map/ppermute | solution.py:374
  31.3 18.6 %collective-permute-start.4 = (bf16[256,1280]{1,0:T(8,128)(2,1)}, bf16[256,1280]{1,0:T(8,128)(2,1)S(1)}, u32[]{:S(2)}, u32[]{:S(2)}) collective-permute-start(bf16[256,1280]{1,0:T(8,128)(2,1)} %get-tuple-element.31.refs_0_), channel_id=1, source_target_pairs={{0,36},{1,125},{4,32},{5,105},{8,44},{9,101},{12,40},{13,113},{16,... | collective-permute-start | bytes 1966088 | tf_op jit(solution)/shard_map/ppermute | solution.py:321
  34.3 18.1 %collective-permute-start.3 = (bf16[256,1280]{1,0:T(8,128)(2,1)}, bf16[256,1280]{1,0:T(8,128)(2,1)S(1)}, u32[]{:S(2)}, u32[]{:S(2)}) collective-permute-start(bf16[256,1280]{1,0:T(8,128)(2,1)} %get-tuple-element.31.refs_0_), channel_id=1, source_target_pairs={{0,32},{1,97},{4,36},{5,101},{8,40},{9,105},{12,44},{13,109},{16,4... | collective-permute-start | bytes 1966088 | tf_op jit(solution)/shard_map/ppermute | solution.py:321
  34.8 17.7 %collective-permute-start.2 = (bf16[256,1280]{1,0:T(8,128)(2,1)}, bf16[256,1280]{1,0:T(8,128)(2,1)S(1)}, u32[]{:S(2)}, u32[]{:S(2)}) collective-permute-start(bf16[256,1280]{1,0:T(8,128)(2,1)} %get-tuple-element.31.refs_0_), channel_id=1, source_target_pairs={{0,4},{1,29},{4,0},{5,9},{8,12},{9,5},{12,8},{13,17},{16,20},{17,1... | collective-permute-start | bytes 1966088 | tf_op jit(solution)/shard_map/ppermute | solution.py:321
  36.0 21.2 %all-to-all-start = ((bf16[8,320,128]{2,1,0:T(8,128)(2,1)}), bf16[8,320,128]{2,1,0:T(8,128)(2,1)S(1)}, u32[]{:S(2)}, u32[]{:S(2)}) async-start(bf16[8,320,128]{2,1,0:T(8,128)(2,1)} %shard_map.71.pieces_hbm), calls=%async_computation | async-start | bytes 1310720 | tf_op jit(solution)/shard_map/all_to_all | solution.py:398
  43.2 11.5 %collective-permute-start.6 = (bf16[320,128]{1,0:T(8,128)(2,1)S(1)}, bf16[320,128]{1,0:T(8,128)(2,1)S(1)}, u32[]{:S(2)}, u32[]{:S(2)}) collective-permute-start(bf16[320,128]{1,0:T(8,128)(2,1)S(1)} %get-tuple-element.36), channel_id=1, source_target_pairs={{128,132},{129,157},{132,128},{133,137},{136,140},{137,133},{140,1... | collective-permute-start | bytes 245768 | tf_op jit(solution)/shard_map/ppermute | solution.py:321
  46.5 8.2 %collective-permute-start.7 = (bf16[320,128]{1,0:T(8,128)(2,1)S(1)}, bf16[320,128]{1,0:T(8,128)(2,1)S(1)}, u32[]{:S(2)}, u32[]{:S(2)}) collective-permute-start(bf16[320,128]{1,0:T(8,128)(2,1)S(1)} %get-tuple-element.37), channel_id=1, source_target_pairs={{128,160},{129,225},{132,164},{133,229},{136,168},{137,233},{140,1... | collective-permute-start | bytes 245768 | tf_op jit(solution)/shard_map/ppermute | solution.py:321
  49.9 7.2 %collective-permute-start.8 = (bf16[320,128]{1,0:T(8,128)(2,1)S(1)}, bf16[320,128]{1,0:T(8,128)(2,1)S(1)}, u32[]{:S(2)}, u32[]{:S(2)}) collective-permute-start(bf16[320,128]{1,0:T(8,128)(2,1)S(1)} %get-tuple-element.38), channel_id=1, source_target_pairs={{128,164},{129,253},{132,160},{133,233},{136,172},{137,229},{140,1... | collective-permute-start | bytes 245768 | tf_op jit(solution)/shard_map/ppermute | solution.py:321
  60.4 10.1 %collective-permute-start.9 = (bf16[128,16,128]{2,1,0:T(8,128)(2,1)S(1)}, bf16[128,16,128]{2,1,0:T(8,128)(2,1)S(1)}, u32[]{:S(2)}, u32[]{:S(2)}) collective-permute-start(bf16[128,16,128]{2,1,0:T(8,128)(2,1)S(1)} %get-tuple-element.41), channel_id=1, source_target_pairs={{0,1},{1,0},{2,3},{3,2},{4,5},{5,4},{6,7},{7,6},{8,9},{9,8},{10,11... | collective-permute-start | bytes 1572872 | tf_op jit(solution)/shard_map/ppermute | solution.py:423
